TPU v7x, 128 devices: a whole 4x4x4 slice. The times are simulated.
128 devices in a mesh: gx: 8 (over x_lo, z), gy: 16 (over y, x_hi, core).
Axes of the slice: x: 4 (x_hi: 2, x_lo: 2; x = x_hi * 2 + x_lo), y: 4, z: 4, core: 2. Of those that a mesh axis runs over, the one named last changes fastest.
Arguments:
- fine: bfloat16 [8192, 32, 512], P(('gx', 'gy')), may hold values from -6 to 6
- coarse: bfloat16 [1024, 32, 512], P(('gx', 'gy')), may hold values from -6 to 6
- weight: bfloat16 [27, 32, 32], replicated, may hold values from -0.21875 to 0.21875
- cotangent: bfloat16 [8192, 32, 512], P(('gx', 'gy')), may hold values from -6 to 6
- adjacency: int32 [8192, 27], P(('gx', 'gy')), may hold values from -1 to 575, as said below
- send_list: int32 [16384, 1], P(('gx', 'gy')), may hold values from -1 to 63, as said below
- child_src: int32 [8192], P(('gx', 'gy')), may hold values from -1 to 127, as said below
Outputs:
- block_out: bfloat16 [8192, 32, 512], P(('gx', 'gy'))
- fine_grad: bfloat16 [8192, 32, 512], P(('gx', 'gy'))
- coarse_grad: bfloat16 [1024, 32, 512], P(('gx', 'gy'))
- weight_grad: float32 [27, 32, 32], replicated
Inputs may be any that keep to these rules, and one draw needn't show every extreme that they name: `adjacency`: entries follow the geometry of a grid of bricks: device (ix, iy) owns the brick columns x in [4 ix, 4 (ix + 1)), y in [4 iy, 4 (iy + 1)) and z layers 0 to 3, one slot a cell; an entry names a live brick at that displacement and never lies outside the mesh; neighbourhood is symmetric; entry 13 of a live slot is the slot itself; all entries of an empty slot are -1. Device 0 has every slot live. `send_list`: every octant id appears at most once on a device; it names the parent of exactly the fine slot whose child_src points at it. In every draw some device sends 1 octants to some device. child_src is -1 exactly for empty fine slots; no two fine slots of one device share a value.
All inputs are finite; a program needn't handle non-finite values.
Results may differ from a plain program's by a relative error of at most 0.0057.
Values may be sent and summed in bfloat16 or wider, within the bound.
No kernel may reach another device: no remote copies, remote signals or barrier semaphores. Data moves between devices by JAX's collectives and lax.ppermute only.
A program may use at most 320 MiB of HBM per device.

v0:
```python
from functools import partial

import jax
import jax.numpy as jnp
from jax import lax
from jax.sharding import PartitionSpec as P

offset_list = [
    (off_x, off_y, off_z) for off_x in (-1, 0, 1) for off_y in (-1, 0, 1) for off_z in (-1, 0, 1)
]
shift_list = [off_x * 100 + off_y * 10 + off_z for off_x, off_y, off_z in offset_list]
window_start = 111
window_len = 778
row_block = 4


def padded_2(block, sides, width):
    for axis, dim in sides:
        count = lax.axis_size(axis)
        forward = [(i, i + 1) for i in range(count - 1)]
        backward = [(target, source) for source, target in forward]
        low = lax.ppermute(
            lax.slice_in_dim(block, block.shape[dim] - width, None, axis=dim), axis, forward
        )
        high = lax.ppermute(lax.slice_in_dim(block, 0, width, axis=dim), axis, backward)
        block = jnp.concatenate([low, block, high], axis=dim)
    return block


def span(offset):
    if offset < 0:
        return (7, 8)
    if offset == 0:
        return (0, 8)
    return (0, 1)


def interior(values):
    leading = values.shape[:-1]
    padded = jnp.pad(values, [(0, 0)] * len(leading) + [(0, 22)])
    padded = padded.reshape(leading + (8, 100))[..., :80]
    return padded.reshape(leading + (8, 8, 10))[..., :8].reshape(leading + (512,))


def spread(values):
    leading = values.shape[:-1]
    volume = values.reshape(leading + (8, 8, 8))
    volume = jnp.pad(volume, [(0, 0)] * len(leading) + [(0, 0), (0, 0), (0, 2)]).reshape(
        leading + (8, 80)
    )
    volume = jnp.pad(volume, [(0, 0)] * len(leading) + [(0, 0), (0, 20)]).reshape(leading + (800,))
    return volume[..., :window_len]


def silu_slope(preact):
    sigma = jax.nn.sigmoid(preact)
    return sigma * (1.0 + preact * (1.0 - sigma))


def whole_piece(received, dev_x, dev_y, span_x, span_y, span_z):
    capacity, channels = (received.shape[2], received.shape[3])
    bricks = received[dev_x + 1, dev_y + 1].reshape(capacity, channels, 8, 8, 8)
    return bricks[:, :, span_x[0] : span_x[1], span_y[0] : span_y[1], span_z[0] : span_z[1]]


def assemble(bricks, adjacency, fetch):
    capacity, channels = (bricks.shape[0], bricks.shape[1])
    portions = {}
    for position, (off_x, off_y, off_z) in enumerate(offset_list):
        span_x, span_y, span_z = (span(off_x), span(off_y), span(off_z))
        own_part = bricks[:, :, span_x[0] : span_x[1], span_y[0] : span_y[1], span_z[0] : span_z[1]]
        if position == 13:
            portions[off_x, off_y, off_z] = own_part
            continue
        pieces = []
        for dev_x in (-1, 0, 1):
            for dev_y in (-1, 0, 1):
                if dev_x == 0 and dev_y == 0:
                    pieces.append(own_part)
                elif dev_x in (0, off_x) and dev_y in (0, off_y):
                    pieces.append(fetch(dev_x, dev_y, span_x, span_y, span_z))
                else:
                    pieces.append(jnp.zeros_like(own_part))
        pieces.append(jnp.zeros_like(own_part[:1]))
        lookup = jnp.concatenate(pieces, axis=0)
        column = adjacency[:, position]
        row_ids = jnp.where(column < 0, 9 * capacity, column)
        portions[off_x, off_y, off_z] = jnp.take(lookup, row_ids, axis=0)
    planes = []
    for off_x in (-1, 0, 1):
        strips = []
        for off_y in (-1, 0, 1):
            strips.append(
                jnp.concatenate([portions[off_x, off_y, off_z] for off_z in (-1, 0, 1)], axis=4)
            )
        planes.append(jnp.concatenate(strips, axis=3))
    return jnp.concatenate(planes, axis=2).reshape(capacity, channels, 1000)


def columns(padded, direction):
    return jnp.stack(
        [
            lax.slice_in_dim(
                padded,
                window_start + direction * offset_flat,
                window_start + direction * offset_flat + window_len,
                axis=2,
            )
            for offset_flat in shift_list
        ],
        axis=1,
    )


def on_device(fine, coarse, weight, cotangent, adjacency, send_list, child_src):
    capacity, channels = (fine.shape[0], fine.shape[1])
    parcels = coarse.shape[0]
    pair_slots = send_list.shape[1]
    devices = lax.axis_size("gx") * lax.axis_size("gy")
    alive_mask = (adjacency[:, 13] >= 0).astype(jnp.float32)
    octants = (
        coarse.reshape(parcels, channels, 2, 4, 2, 4, 2, 4)
        .transpose(0, 2, 4, 6, 1, 3, 5, 7)
        .reshape(parcels * 8, channels, 64)
    )
    octant_table = jnp.concatenate([octants, jnp.zeros_like(octants[:1])], axis=0)
    outgoing = jnp.take(octant_table, jnp.where(send_list < 0, parcels * 8, send_list), axis=0)
    incoming = lax.all_to_all(outgoing, ("gx", "gy"), split_axis=0, concat_axis=0, tiled=True)
    incoming = incoming.reshape(devices * pair_slots, channels, 64)
    parent_table = jnp.concatenate([incoming, jnp.zeros_like(incoming[:1])], axis=0)
    parents = jnp.take(
        parent_table, jnp.where(child_src < 0, devices * pair_slots, child_src), axis=0
    ).reshape(capacity, channels, 4, 4, 4)
    upsampled = jnp.repeat(jnp.repeat(jnp.repeat(parents, 2, axis=2), 2, axis=3), 2, axis=4)
    alive5 = alive_mask[:, None, None, None, None]
    hidden = (
        (
            fine.astype(jnp.float32).reshape(capacity, channels, 8, 8, 8)
            + upsampled.astype(jnp.float32)
        )
        * alive5
    ).astype(jnp.bfloat16)
    near_hidden = padded_2(
        hidden.reshape(capacity, channels, 512)[None, None], (("gx", 0), ("gy", 1)), 1
    )
    padded_h = assemble(hidden, adjacency, partial(whole_piece, near_hidden))
    blocks = capacity // row_block

    def forward_rows(inputs):
        padded_block, hidden_block, cot_block, alive_block = inputs
        stacked = columns(padded_block, 1)
        preact = interior(
            jnp.einsum("koc,bkcp->bop", weight, stacked, preferred_element_type=jnp.float32)
        )
        mixed_out = ((hidden_block.astype(jnp.float32) + jax.nn.silu(preact)) * alive_block).astype(
            jnp.bfloat16
        )
        grad_pre = (cot_block.astype(jnp.float32) * silu_slope(preact) * alive_block).astype(
            jnp.bfloat16
        )
        return (mixed_out, grad_pre)

    block_out, grad_pre = lax.map(
        forward_rows,
        (
            padded_h.reshape(blocks, row_block, channels, 1000),
            hidden.reshape(blocks, row_block, channels, 512),
            cotangent.reshape(blocks, row_block, channels, 512),
            alive_mask.reshape(blocks, row_block, 1, 1),
        ),
    )
    block_out = block_out.reshape(capacity, channels, 512)
    grad_pre = grad_pre.reshape(capacity, channels, 512)
    grad_bricks = grad_pre.reshape(capacity, channels, 8, 8, 8)
    near_grad = padded_2(grad_pre[None, None], (("gx", 0), ("gy", 1)), 1)
    padded_d = assemble(grad_bricks, adjacency, partial(whole_piece, near_grad))

    def backward_rows(running, inputs):
        padded_hb, padded_db, grad_block = inputs
        stacked_h = columns(padded_hb, 1)
        stacked_d = columns(padded_db, -1)
        running = running + jnp.einsum(
            "bop,bkcp->koc", spread(grad_block), stacked_h, preferred_element_type=jnp.float32
        )
        back_conv = interior(
            jnp.einsum("koc,bkop->bcp", weight, stacked_d, preferred_element_type=jnp.float32)
        )
        return (running, back_conv)

    local_grad, back_conv = lax.scan(
        backward_rows,
        jnp.zeros((27, channels, channels), jnp.float32),
        (
            padded_h.reshape(blocks, row_block, channels, 1000),
            padded_d.reshape(blocks, row_block, channels, 1000),
            grad_pre.reshape(blocks, row_block, channels, 512),
        ),
    )
    weight_grad = lax.psum(local_grad, ("gx", "gy"))
    back_conv = back_conv.reshape(capacity, channels, 512)
    grad_hidden = (cotangent.astype(jnp.float32) + back_conv) * alive_mask[:, None, None]
    fine_grad = grad_hidden.astype(jnp.bfloat16)
    pooled = (
        grad_hidden.reshape(capacity, channels, 4, 2, 4, 2, 4, 2)
        .sum(axis=(3, 5, 7))
        .astype(jnp.bfloat16)
        .reshape(capacity, channels * 64)
    )
    selector = (
        child_src[None, :] == jnp.arange(devices * pair_slots, dtype=jnp.int32)[:, None]
    ).astype(jnp.bfloat16)
    returning = (
        jnp.dot(selector, pooled, preferred_element_type=jnp.float32)
        .astype(jnp.bfloat16)
        .reshape(devices, pair_slots, channels, 64)
    )
    returned = lax.all_to_all(returning, ("gx", "gy"), split_axis=0, concat_axis=0, tiled=True)
    returned = returned.reshape(devices * pair_slots, channels * 64)
    picker = (
        send_list.reshape(devices * pair_slots)[None, :]
        == jnp.arange(parcels * 8, dtype=jnp.int32)[:, None]
    ).astype(jnp.bfloat16)
    octant_grad = jnp.dot(picker, returned, preferred_element_type=jnp.float32).astype(jnp.bfloat16)
    coarse_grad = (
        octant_grad.reshape(parcels, 2, 2, 2, channels, 4, 4, 4)
        .transpose(0, 4, 1, 5, 2, 6, 3, 7)
        .reshape(parcels, channels, 512)
    )
    return (block_out, fine_grad, coarse_grad, weight_grad)


def solution(mesh):
    return jax.shard_map(
        on_device,
        mesh=mesh,
        in_specs=(
            P(("gx", "gy"), None, None),
            P(("gx", "gy"), None, None),
            P(),
            P(("gx", "gy"), None, None),
            P(("gx", "gy"), None),
            P(("gx", "gy"), None),
            P(("gx", "gy")),
        ),
        out_specs=(
            P(("gx", "gy"), None, None),
            P(("gx", "gy"), None, None),
            P(("gx", "gy"), None, None),
            P(),
        ),
        check_vma=False,
    )
```

profile of v0, /device:TPU:1, one launch (start us, length us, event | category | flops | bytes accessed | tf_op | source)
XLA Modules:
  0.0 1870.1 jit_solution(11602218976269093458)
XLA Ops:
  18.7 12.3 all-to-all-start
  34.9 11.5 copy.3134
  115.1 12.1 broadcast_in_dim.189.clone.1
  127.2 12.1 multiply_convert_fusion.2
  178.1 15.0 multiply_convert_fusion.3
  265.4 12.6 copy.2903
  281.1 12.1 copy.2973
  351.4 12.7 copy.2902
  371.5 12.5 copy.2929
  387.3 12.5 copy.2904
  408.4 12.5 copy.2928
  431.0 12.0 copy.2972
  443.0 12.9 copy.2994
  574.9 50.5 %maximum_maximum_fusion = bf16[64,32,10,10,10]{1,0,4,3,2:T(8,128)(2,1)} fusion(bf16[64,32,1,1,1]{1,0,4,3,2:T(8,128)(2,1)} %bitcast_select_fusion.31, bf16[64,32,1,1,8]{1,0,4,3,2:T(8,128)(2,1)S(1)} %bitcast_select_fusion.21, bf16[64,32,1,1,1]{1,0,4,3,2:T(8,128)(2,1)S(1)} %bitcast_select_fusion.32, bf16[64,32,1,8,1]{1,0,4,3,2:T(8,128)(2,1)} %copy_select_fusion, ...), kind=kLoop, calls=%fused_computation.238 | loop fusion | flops 53248000 | bytes 8192000 | tf_op jit(solution)/shard_map/concatenate | solution.py:97
  625.4 23.3 %copy.3006 = bf16[16,4,32,1000]{3,2,1,0:T(8,128)(2,1)} copy(bf16[16,4,32,1000]{2,1,0,3:T(4,128)(2,1)} %bitcast.1007) | data formatting | bytes 8192000 | tf_op jit(solution)/shard_map/while | solution.py:163
  648.6 156.6 %while.29 = (s32[]{:T(128)}, bf16[16,4,32,512]{3,2,1,0:T(8,128)(2,1)}, bf16[16,4,32,512]{3,2,1,0:T(8,128)(2,1)}, bf16[16,4,32,512]{3,2,1,0:T(8,128)(2,1)}, bf16[...) while((s32[]{:T(128)}, ...), condition=%wide.region_1.9_spmd, body=%wide.region_0.8_spmd.sunk | while | flops 173129728 | bytes 23341728 | solution.py:163
  935.4 12.6 copy.3009
  977.2 12.7 copy.3081
  1024.3 12.5 copy.3008
  1036.8 12.0 copy.3010
  1061.9 12.8 copy.3035
  1092.3 11.9 copy.3033
  1200.6 12.7 copy.3080
  1229.7 12.1 copy.3103
  1265.0 23.2 %pad_maximum_fusion = bf16[64,32,10,10,10]{1,4,3,2,0:T(8,128)(2,1)} fusion(bf16[64,32,1,10,10]{1,4,3,2,0:T(8,128)(2,1)} %maximum_bitcast_fusion.1, bf16[64,32,8,1,10]{1,4,3,2,0:T(8,128)(2,1)} %maximum_bitcast_fusion.3, bf16[64,32,8,8,1]{1,4,3,2,0:T(2,128)(2,1)} %copy.3064, bf16[64,32,8,8,8]{1,4,3,2,0:T(8,128)(2,1)} %bitcast.995, ...), kind=kLoop, calls=%fused_computation.235 | loop fusion | flops 28672000 | bytes 8192000 | tf_op jit(solution)/shard_map/concatenate | solution.py:97
  1288.2 18.1 copy.3117
  1306.3 23.3 %copy.3120 = bf16[16,4,32,1000]{3,2,1,0:T(8,128)(2,1)} copy(bf16[16,4,32,1000]{2,1,0,3:T(4,128)(2,1)} %bitcast.1008) | data formatting | bytes 8192000
  1329.6 347.2 %while.30 = (s32[]{:T(128)}, f32[27,32,32]{1,2,0:T(8,128)S(1)}, f32[16,4,32,512]{3,2,1,0:T(8,128)}, bf16[16,4,32,1000]{3,2,1,0:T(8,128)(2,1)}, bf16[16,4,32,512]...) while((s32[]{:T(128)}, f32[27,32,32]{1,2,0:T(8,128)S(1)}, ...), condition=%wide.region_3.0_spmd.clone, body=%wide.region_2.10_spmd.clone.sunk | while | flops 344217600 | bytes 65186460 | solution.py:190
  1711.6 12.8 all-to-all-done.1
  1726.5 19.1 %reshape.370 = bf16[8,2,2,2,32,4,4,4]{7,6,5,4,3,2,1,0:T(4,128)(2,1)} reshape(bf16[64,2048]{1,0:T(8,128)(2,1)S(1)} %convolution_convert_fusion.1) | data formatting | bytes 524288 | tf_op jit(solution)/shard_map/reshape | solution.py:225
  1745.6 13.1 copy.3128
  1760.1 101.1 %all-reduce.8.cloned.1.call-done = f32[27,32,32]{2,1,0:T(8,128)} async-done(((f32[27,32,32]{2,1,0:T(8,128)}), f32[27,32,32]{2,1,0:T(8,128)}) %all-reduce.8.cloned.1.call-update) | async-done | bytes 110608 | tf_op jit(solution)/shard_map/psum | solution.py:199
  (2595 shorter events, 1298.6 us)
Async XLA Ops:
  18.7 59.7 %all-to-all-start = ((bf16[128,2,1024]{2,1,0:T(2,128)(2,1)}), bf16[128,2,1024]{2,1,0:T(2,128)(2,1)}, u32[]{:S(2)}, u32[]{:S(2)}) async-start(bf16[128,2,1024]{2,1,0:T(2,128)(2,1)} %reshape.1419), calls=%async_computation | async-start | bytes 1048576 | tf_op jit(solution)/shard_map/all_to_all | solution.py:128
  32.3 94.9 %copy-start.113 = (f32[64]{0:T(128)}, f32[64]{0:T(128)S(1)}, u32[]{:S(2)}) copy-start(f32[64]{0:T(128)S(1)} %fusion.102) | copy-start | bytes 772
  64.9 245.9 %copy-start.115 = (s32[1024]{0:T(1024)}, s32[1024]{0:T(1024)S(1)}, u32[]{:S(2)}) copy-start(s32[1024]{0:T(1024)S(1)} %get-tuple-element.726) | copy-start | bytes 12292
  71.6 141.3 %copy-start.110 = (bf16[577]{0:T(1024)(128)(2,1)}, bf16[577]{0:T(1024)(128)(2,1)S(1)}, u32[]{:S(2)}) copy-start(bf16[577]{0:T(1024)(128)(2,1)S(1)} %pad.110.clone) | copy-start | bytes 3466
  102.0 91.2 %collective-permute-start = (bf16[1,1,64,32,512]{4,3,2,1,0:T(8,128)(2,1)}, bf16[1,1,64,32,512]{4,3,2,1,0:T(8,128)(2,1)}, u32[]{:S(2)}, u32[]{:S(2)}) collective-permute-start(bf16[1,1,64,32,512]{4,3,2,1,0:T(8,128)(2,1)} %fusion.96), channel_id=1, source_target_pairs={{0,16},{16,32},{32,48},{48,64},{64,80},{80,96},{96,112},{1,17},{17... | collective-permute-start | bytes 6291464 | tf_op jit(solution)/shard_map/ppermute | solution.py:22
  106.7 86.5 %collective-permute-start.1 = (bf16[1,1,64,32,512]{4,3,2,1,0:T(8,128)(2,1)}, bf16[1,1,64,32,512]{4,3,2,1,0:T(8,128)(2,1)S(1)}, u32[]{:S(2)}, u32[]{:S(2)}) collective-permute-start(bf16[1,1,64,32,512]{4,3,2,1,0:T(8,128)(2,1)} %fusion.96), channel_id=1, source_target_pairs={{16,0},{32,16},{48,32},{64,48},{80,64},{96,80},{112,96},{17,1},{33... | collective-permute-start | bytes 6291464 | tf_op jit(solution)/shard_map/ppermute | solution.py:25
  199.5 146.1 %collective-permute-start.2 = (bf16[3,1,64,32,512]{4,3,2,1,0:T(8,128)(2,1)}, bf16[3,1,64,32,512]{4,3,2,1,0:T(8,128)(2,1)}, u32[]{:S(2)}, u32[]{:S(2)}) collective-permute-start(bf16[3,1,64,32,512]{4,3,2,1,0:T(8,128)(2,1)} %pad_maximum_fusion.1), channel_id=1, source_target_pairs={{0,1},{1,2},{2,3},{3,4},{4,5},{5,6},{6,7},{7,8},{8,9},{9,10},{10,1... | collective-permute-start | bytes 18874376 | tf_op jit(solution)/shard_map/ppermute | solution.py:22
  210.5 155.3 %collective-permute-start.3 = (bf16[3,1,64,32,512]{4,3,2,1,0:T(8,128)(2,1)}, bf16[3,1,64,32,512]{4,3,2,1,0:T(8,128)(2,1)}, u32[]{:S(2)}, u32[]{:S(2)}) collective-permute-start(bf16[3,1,64,32,512]{4,3,2,1,0:T(8,128)(2,1)} %pad_maximum_fusion.1), channel_id=1, source_target_pairs={{1,0},{2,1},{3,2},{4,3},{5,4},{6,5},{7,6},{8,7},{9,8},{10,9},{11,1... | collective-permute-start | bytes 18874376 | tf_op jit(solution)/shard_map/ppermute | solution.py:25
  443.0 28.8 %copy-start.62 = (bf16[64,32,1,1,8]{0,4,3,2,1:T(8,128)(2,1)S(1)}, bf16[64,32,1,1,8]{0,4,3,2,1:T(8,128)(2,1)}, u32[]{:S(2)}) copy-start(bf16[64,32,1,1,8]{0,4,3,2,1:T(8,128)(2,1)} %copy.2975) | copy-start | bytes 98308
  443.0 28.8 %copy-start.65 = (bf16[64,32,1,1,8]{0,4,3,2,1:T(8,128)(2,1)S(1)}, bf16[64,32,1,1,8]{0,4,3,2,1:T(8,128)(2,1)}, u32[]{:S(2)}) copy-start(bf16[64,32,1,1,8]{0,4,3,2,1:T(8,128)(2,1)} %copy.2977) | copy-start | bytes 98308
  474.2 610.7 %copy-start.40 = (bf16[256,32,1,1,8]{0,4,3,2,1:T(8,128)(2,1)}, bf16[256,32,1,1,8]{0,4,3,2,1:T(8,128)(2,1)S(1)}, u32[]{:S(2)}) copy-start(bf16[256,32,1,1,8]{0,4,3,2,1:T(8,128)(2,1)S(1)} %broadcast.380) | copy-start | bytes 393220
  526.0 29.2 %copy-start.124 = (pred[64]{0:T(512)(128)(4,1)S(1)}, pred[64]{0:T(512)(128)(4,1)}, u32[]{:S(2)}) copy-start(pred[64]{0:T(512)(128)(4,1)} %get-tuple-element.689) | copy-start | bytes 196
  526.3 31.6 %copy-start.129 = (pred[64]{0:T(512)(128)(4,1)S(1)}, pred[64]{0:T(512)(128)(4,1)}, u32[]{:S(2)}) copy-start(pred[64]{0:T(512)(128)(4,1)} %get-tuple-element.699) | copy-start | bytes 196
  805.2 54.2 %collective-permute-start.4 = (bf16[1,1,64,32,512]{4,3,2,1,0:T(8,128)(2,1)}, bf16[1,1,64,32,512]{4,3,2,1,0:T(8,128)(2,1)}, u32[]{:S(2)}, u32[]{:S(2)}) collective-permute-start(bf16[1,1,64,32,512]{4,3,2,1,0:T(8,128)(2,1)} %bitcast.1069), channel_id=1, source_target_pairs={{0,16},{16,32},{32,48},{48,64},{64,80},{80,96},{96,112},{1,17},{17... | collective-permute-start | bytes 6291464 | tf_op jit(solution)/shard_map/ppermute | solution.py:22
  810.9 49.5 %collective-permute-start.5 = (bf16[1,1,64,32,512]{4,3,2,1,0:T(8,128)(2,1)}, bf16[1,1,64,32,512]{4,3,2,1,0:T(8,128)(2,1)}, u32[]{:S(2)}, u32[]{:S(2)}) collective-permute-start(bf16[1,1,64,32,512]{4,3,2,1,0:T(8,128)(2,1)} %bitcast.1070), channel_id=1, source_target_pairs={{16,0},{32,16},{48,32},{64,48},{80,64},{96,80},{112,96},{17,1},{33... | collective-permute-start | bytes 6291464 | tf_op jit(solution)/shard_map/ppermute | solution.py:25
  866.7 151.7 %collective-permute-start.6 = (bf16[3,1,64,32,512]{4,3,2,1,0:T(8,128)(2,1)}, bf16[3,1,64,32,512]{4,3,2,1,0:T(8,128)(2,1)}, u32[]{:S(2)}, u32[]{:S(2)}) collective-permute-start(bf16[3,1,64,32,512]{4,3,2,1,0:T(8,128)(2,1)} %pad_maximum_fusion.2), channel_id=1, source_target_pairs={{0,1},{1,2},{2,3},{3,4},{4,5},{5,6},{6,7},{7,8},{8,9},{9,10},{10,1... | collective-permute-start | bytes 18874376 | tf_op jit(solution)/shard_map/ppermute | solution.py:22
  883.9 172.2 %collective-permute-start.7 = (bf16[3,1,64,32,512]{4,3,2,1,0:T(8,128)(2,1)}, bf16[3,1,64,32,512]{4,3,2,1,0:T(8,128)(2,1)}, u32[]{:S(2)}, u32[]{:S(2)}) collective-permute-start(bf16[3,1,64,32,512]{4,3,2,1,0:T(8,128)(2,1)} %pad_maximum_fusion.2), channel_id=1, source_target_pairs={{1,0},{2,1},{3,2},{4,3},{5,4},{6,5},{7,6},{8,7},{9,8},{10,9},{11,1... | collective-permute-start | bytes 18874376 | tf_op jit(solution)/shard_map/ppermute | solution.py:25
  1092.3 29.1 %copy-start.138 = (pred[64]{0:T(512)(128)(4,1)S(1)}, pred[64]{0:T(512)(128)(4,1)}, u32[]{:S(2)}) copy-start(pred[64]{0:T(512)(128)(4,1)} %get-tuple-element.705) | copy-start | bytes 196
  1092.3 33.2 %copy-start.136 = (pred[64]{0:T(512)(128)(4,1)S(1)}, pred[64]{0:T(512)(128)(4,1)}, u32[]{:S(2)}) copy-start(pred[64]{0:T(512)(128)(4,1)} %get-tuple-element.709) | copy-start | bytes 196
  1092.3 35.0 %copy-start.17 = (bf16[256,32,8,1,1]{0,2,4,3,1:T(8,128)(2,1)S(1)}, bf16[256,32,8,1,1]{0,2,4,3,1:T(8,128)(2,1)}, u32[]{:S(2)}) copy-start(bf16[256,32,8,1,1]{0,2,4,3,1:T(8,128)(2,1)} %copy-done.16) | copy-start | bytes 393220
  1092.3 35.0 %copy-start.30 = (bf16[64,32,8,1,1]{0,2,4,3,1:T(8,128)(2,1)S(1)}, bf16[64,32,8,1,1]{0,2,4,3,1:T(8,128)(2,1)}, u32[]{:S(2)}) copy-start(bf16[64,32,8,1,1]{0,2,4,3,1:T(8,128)(2,1)} %copy-done.29) | copy-start | bytes 98308
  1092.3 35.0 %copy-start.32 = (bf16[128,32,8,1,1]{0,2,4,3,1:T(8,128)(2,1)S(1)}, bf16[128,32,8,1,1]{0,2,4,3,1:T(8,128)(2,1)}, u32[]{:S(2)}) copy-start(bf16[128,32,8,1,1]{0,2,4,3,1:T(8,128)(2,1)} %copy-done.31) | copy-start | bytes 196612
  1104.3 31.3 %copy-start.4 = (bf16[256,32,8,1,8]{0,4,3,2,1:T(8,128)(2,1)S(1)}, bf16[256,32,8,1,8]{0,4,3,2,1:T(8,128)(2,1)}, u32[]{:S(2)}) copy-start(bf16[256,32,8,1,8]{0,4,3,2,1:T(8,128)(2,1)} %copy-done.3) | copy-start | bytes 3145732
  1104.3 31.3 %copy-start.8 = (bf16[64,32,8,1,8]{0,4,3,2,1:T(8,128)(2,1)S(1)}, bf16[64,32,8,1,8]{0,4,3,2,1:T(8,128)(2,1)}, u32[]{:S(2)}) copy-start(bf16[64,32,8,1,8]{0,4,3,2,1:T(8,128)(2,1)} %copy-done.7) | copy-start | bytes 786436
  1104.3 31.4 %copy-start.10 = (bf16[128,32,8,1,8]{0,4,3,2,1:T(8,128)(2,1)S(1)}, bf16[128,32,8,1,8]{0,4,3,2,1:T(8,128)(2,1)}, u32[]{:S(2)}) copy-start(bf16[128,32,8,1,8]{0,4,3,2,1:T(8,128)(2,1)} %copy-done.9) | copy-start | bytes 1572868
  1104.3 31.4 %copy-start.12 = (bf16[1,32,8,1,8]{0,4,3,2,1:T(8,128)(2,1)S(1)}, bf16[1,32,8,1,8]{0,4,3,2,1:T(8,128)(2,1)}, u32[]{:S(2)}) copy-start(bf16[1,32,8,1,8]{0,4,3,2,1:T(8,128)(2,1)} %copy-done.11) | copy-start | bytes 12292
  1200.6 28.9 %copy-start.54 = (bf16[64,32,1,1,8]{1,0,4,3,2:T(8,128)(2,1)S(1)}, bf16[64,32,1,1,8]{1,0,4,3,2:T(8,128)(2,1)}, u32[]{:S(2)}) copy-start(bf16[64,32,1,1,8]{1,0,4,3,2:T(8,128)(2,1)} %get-tuple-element.568) | copy-start | bytes 98308
  1200.6 29.0 %copy-start.20 = (bf16[1,1,64,32,512]{4,3,2,1,0:T(8,128)(2,1)S(1)}, bf16[1,1,64,32,512]{4,3,2,1,0:T(8,128)(2,1)}, u32[]{:S(2)}) copy-start(bf16[1,1,64,32,512]{4,3,2,1,0:T(8,128)(2,1)} %get-tuple-element.663) | copy-start | bytes 6291460
  1329.6 347.2 %copy-start.114 = (f32[64]{0:T(128)S(1)}, f32[64]{0:T(128)}, u32[]{:S(2)}) copy-start(f32[64]{0:T(128)} %copy-done.113) | copy-start | bytes 772
  1696.5 29.6 %copy-start.167 = (s32[128,1]{0,1:T(1,128)S(1)}, s32[128,1]{0,1:T(1,128)}, u32[]{:S(2)}) copy-start(s32[128,1]{0,1:T(1,128)} %param.30) | copy-start | bytes 1540
  1700.4 24.0 %all-to-all-start.1 = ((bf16[128,2,1024]{2,1,0:T(2,128)(2,1)}), bf16[128,2,1024]{2,1,0:T(2,128)(2,1)S(1)}, u32[]{:S(2)}, u32[]{:S(2)}) async-start(bf16[128,2,1024]{2,1,0:T(2,128)(2,1)} %reshape.1421), calls=%async_computation.1 | async-start | bytes 1048576 | tf_op jit(solution)/shard_map/all_to_all | solution.py:217
  1710.6 150.6 %all-reduce.8.cloned.1.call-start = ((), (), s32[]{:S(2)}) async-start(), calls=%async_computation.2 | async-start | bytes 884736 | tf_op jit(solution)/shard_map/psum | solution.py:199
  (162 other events, 2240.1 us)
Sparse Core Ops, SparseCore 0:
  1716.8 144.4 all-reduce.7
where the time goes:
time: 1890 us; the launch traced here: 1870 us
  local copies, waits for them, and re-layouts  1330 us (70%)
  other arithmetic  236 us (12%)
  waiting for transfers between devices  115 us (6%)
  matrix products  111 us (6%)
  starting transfers between devices  50.3 us (3%)
    while x1344, local copies, waits for them, and re-layouts  244 us
    unnamed x449, local copies, waits for them, and re-layouts  177 us
    slice x16, local copies, waits for them, and re-layouts, whole_piece(): bricks = received[dev_x + 1, dev_y + 1].reshape(capacity, channels, 8, 8, 8)  172 us
    another operation x32, local copies, waits for them, and re-layouts, assemble(): portions[off_x, off_y, off_z] = jnp.take(lookup, row_ids, axis=0)  126 us
    gather x52, local copies, waits for them, and re-layouts, assemble(): portions[off_x, off_y, off_z] = jnp.take(lookup, row_ids, axis=0)  117 us
    psum x1, waiting for transfers between devices, on_device(): weight_grad = lax.psum(local_grad, ('gx', 'gy'))  101 us
    concatenate x2, other arithmetic, assemble(): return jnp.concatenate(planes, axis=2).reshape(capacity, channels, 1000)  73.7 us
    dot_general x16, matrix products, backward_rows(): jnp.einsum('bop,bkcp->koc', spread(grad_block), stacked_h, preferred_elem...  73.7 us
  transfers between devices with their start and end apart: 11, of which 3 were waited for; matrix products, arithmetic and copies ran while one was open for 30% of the time, Pallas kernels for 0%

commit v1 on v0

v1 whole, which is shorter than its diff:
```python
import jax
import jax.numpy as jnp
import numpy as np
from jax import lax
from jax.experimental import pallas as pl
from jax.experimental.pallas import tpu as pltpu
from jax.sharding import PartitionSpec as P

axes = ("gx", "gy")
channels = 32
capacity = 64
quad = 4
steps = capacity // quad
band = 9 * channels
depth = 10 * band
face_n = 16
corner_n = 4
side_n = face_n + 2 * corner_n
base_xm = capacity
base_xp = base_xm + face_n
base_ym = base_xp + face_n
base_yp = base_ym + side_n
zero_row = base_yp + side_n
table_rows = zero_row + 1
place_base = (
    base_ym + face_n,
    base_xm,
    base_yp + face_n,
    base_ym,
    0,
    base_yp,
    base_ym + face_n + corner_n,
    base_xp,
    base_yp + face_n + corner_n,
)
vmem = pl.BlockSpec(memory_space=pltpu.VMEM)
smem = pl.BlockSpec(memory_space=pltpu.SMEM)
bf16 = jnp.bfloat16
f32 = jnp.float32


def params():
    return pltpu.CompilerParams(vmem_limit_bytes=60 * 1024 * 1024)


def octant_matrix():
    out = np.zeros((512, 512), np.float32)
    for o in range(8):
        a, b, c = o // 4, o // 2 % 2, o % 2
        for v in range(64):
            x, y, z = v // 16, v // 4 % 4, v % 4
            out[(4 * a + x) * 64 + (4 * b + y) * 8 + 4 * c + z, o * 64 + v] = 1
    return out


def upsample_matrix():
    out = np.zeros((64, 512), np.float32)
    for p in range(512):
        x, y, z = p // 64, p // 8 % 8, p % 8
        out[(x // 2) * 16 + (y // 2) * 4 + z // 2, p] = 1
    wide = np.zeros((128, 1024), np.float32)
    wide[:64, :512] = out
    wide[64:, 512:] = out
    return wide


def y_face_matrix(y):
    out = np.zeros((512, 64), np.float32)
    for x in range(8):
        for z in range(8):
            out[x * 64 + y * 8 + z, x * 8 + z] = 1
    wide = np.zeros((1024, 128), np.float32)
    wide[:512, :64] = out
    wide[512:, 64:] = out
    return wide


def pool_matrix():
    out = np.zeros((4, 2, 128, 256), np.float32)
    for t in range(4):
        for b in range(4):
            for y in range(0, 8, 2):
                for z in range(0, 8, 2):
                    out[t, b // 2, (b % 2) * 64 + y * 8 + z, b * 64 + t * 16 + (y // 2) * 4 + z // 2] = 1
    return out.reshape(1024, 256)


def const(values):
    return jnp.asarray(values, dtype=bf16)


def lane_id(rows):
    return lax.broadcasted_iota(jnp.int32, (rows, 128), 1)


def roll(v, shift):
    return pltpu.roll(v, shift % 128, 1)


def octant_kernel(send, coarse, perm, out, tab):
    low = lane_id(16) < 64
    y = jnp.dot(coarse[...].reshape(256, 512), perm[...], preferred_element_type=f32).astype(bf16)
    for i in range(8):
        for g in range(4):
            part = y[i * 32 : i * 32 + 32, g * 128 : g * 128 + 128]
            tab[i * 8 + 2 * g] = jnp.where(low, part[:16], roll(part[16:], 64))
            tab[i * 8 + 2 * g + 1] = jnp.where(low, roll(part[:16], 64), part[16:])

    def body(i, carry):
        for j in range(8):
            d = i * 8 + j
            out[d] = tab[jnp.maximum(send[d], 0)]
        return carry

    lax.fori_loop(0, 16, body, 0)


def emit_faces(lists, bricks, ylow, yhigh, out_xm, out_xp, out_ym, out_yp, wide):
    low = lane_id(16) < 64
    for r in range(side_n):
        s = lists[r]
        out_xm[r] = jnp.where(low, bricks[s, 0:16, 0:128], roll(bricks[s, 16:32, 0:128], 64))
        s = lists[side_n + r]
        out_xp[r] = jnp.where(low, roll(bricks[s, 0:16, 384:512], 64), bricks[s, 16:32, 384:512])
    for side, (matrix, out) in enumerate(((ylow, out_ym), (yhigh, out_yp))):
        for r in range(face_n):
            s = lists[2 * side_n + side * face_n + r]
            wide[r * 16 : r * 16 + 16, 0:512] = bricks[s, 0:16, :]
            wide[r * 16 : r * 16 + 16, 512:1024] = bricks[s, 16:32, :]
        out[...] = (
            jnp.dot(wide[...], matrix[...], preferred_element_type=f32)
            .astype(bf16)
            .reshape(face_n, 16, 128)
        )


def hidden_kernel(
    child, alive, lists, incoming, fine, up, ylow, yhigh, hidden, xm, xp, ym, yp, wide
):
    def body(i, carry):
        rows = []
        for j in range(8):
            rows.append(incoming[jnp.maximum(child[i * 8 + j], 0)])
        big = jnp.dot(jnp.concatenate(rows, axis=0), up[...], preferred_element_type=f32)
        for j in range(8):
            s = i * 8 + j
            live = alive[s] > 0
            for h in range(2):
                total = fine[s, h * 16 : h * 16 + 16, :].astype(f32) + big[
                    j * 16 : j * 16 + 16, h * 512 : h * 512 + 512
                ]
                hidden[s, h * 16 : h * 16 + 16, :] = jnp.where(live, total, 0.0).astype(bf16)
        return carry

    lax.fori_loop(0, 8, body, 0)
    emit_faces(lists, hidden, ylow, yhigh, xm, xp, ym, yp, wide)


def fill_table(table, own, rxm, rxp, rym, ryp, elow, ehigh):
    def copy(i, carry):
        for j in range(8):
            table[i * 8 + j] = own[i * 8 + j]
        return carry

    lax.fori_loop(0, capacity // 8, copy, 0)
    for row, source, at in (
        [(base_xm + r, rxm, r) for r in range(face_n)]
        + [(base_ym + face_n + r, rym, face_n + r) for r in range(corner_n)]
        + [(base_yp + face_n + r, ryp, face_n + r) for r in range(corner_n)]
    ):
        table[row, 0:16, 384:512] = roll(source[at], 64)
        table[row, 16:32, 384:512] = source[at]
    for row, source, at in (
        [(base_xp + r, rxp, r) for r in range(face_n)]
        + [(base_ym + face_n + corner_n + r, rym, face_n + corner_n + r) for r in range(corner_n)]
        + [(base_yp + face_n + corner_n + r, ryp, face_n + corner_n + r) for r in range(corner_n)]
    ):
        table[row, 0:16, 0:128] = source[at]
        table[row, 16:32, 0:128] = roll(source[at], 64)
    for base, source, matrix in ((base_ym, rym, ehigh), (base_yp, ryp, elow)):
        big = jnp.dot(
            source[0:face_n].reshape(face_n * 16, 128), matrix[...], preferred_element_type=f32
        ).astype(bf16)
        for r in range(face_n):
            table[base + r, 0:16, :] = big[r * 16 : r * 16 + 16, 0:512]
            table[base + r, 16:32, :] = big[r * 16 : r * 16 + 16, 512:1024]
    table[zero_row] = jnp.zeros((channels, 512), bf16)


def to_pair(even_odd, low):
    first, second = even_odd
    return (
        jnp.where(low, first, roll(second, 64)),
        jnp.where(low, roll(first, 64), second),
    )


def build_stack(step, near, table, stack):
    lane = lane_id(channels)
    inner = lane & 63
    low = lane < 64
    y_first, y_last = inner < 8, inner >= 56
    z_first, z_last = (lane & 7) == 0, (lane & 7) == 7

    def sources(brick, off_x, tile):
        def at(off_y, off_z):
            row = near[brick * 27 + (off_x + 1) * 9 + (off_y + 1) * 3 + off_z + 1]
            return table[row, :, tile * 128 : tile * 128 + 128]

        return (
            at(0, 0),
            jnp.where(y_last, at(-1, 0), at(1, 0)),
            jnp.where(z_last, at(0, -1), at(0, 1)),
            jnp.where(
                y_last,
                jnp.where(z_last, at(-1, -1), at(-1, 1)),
                jnp.where(z_last, at(1, -1), at(1, 1)),
            ),
        )

    def shifts(plane, pair, kinds):
        own, near_y, near_z, near_yz = kinds
        own_z = (
            jnp.where(z_first, roll(near_z, -7), roll(own, 1)),
            own,
            jnp.where(z_last, roll(near_z, 7), roll(own, -1)),
        )
        next_z = (
            jnp.where(z_first, roll(near_yz, -7), roll(near_y, 1)),
            near_y,
            jnp.where(z_last, roll(near_yz, 7), roll(near_y, -1)),
        )
        for k in range(3):
            trio = (
                jnp.where(y_first, roll(next_z[k], -56), roll(own_z[k], 8)),
                own_z[k],
                jnp.where(y_last, roll(next_z[k], 56), roll(own_z[k], -8)),
            )
            for j in range(3):
                row = plane * band + (j * 3 + k) * channels
                stack[row : row + channels, pair * 128 : pair * 128 + 128] = trio[j]

    for pair in range(2):
        b0 = step * quad + 2 * pair
        for off_x, tile in ((-1, 3), (0, 0), (0, 1), (0, 2), (0, 3), (1, 0)):
            first = sources(b0, off_x, tile)
            second = sources(b0 + 1, off_x, tile)
            both = [to_pair(ab, low) for ab in zip(first, second)]
            if off_x <= 0:
                plane = 0 if off_x < 0 else 2 + 2 * tile
                shifts(plane, pair, [b[1] for b in both])
            if off_x >= 0:
                plane = 9 if off_x > 0 else 1 + 2 * tile
                shifts(plane, pair, [b[0] for b in both])


def alive_lanes(step, near):
    lane = lax.broadcasted_iota(jnp.int32, (1, 256), 1)
    out = jnp.zeros((1, 256), f32)
    for i in range(quad):
        live = (near[(step * quad + i) * 27 + 13] != zero_row).astype(f32)
        out = jnp.where(lane // 64 == i, live, out)
    return out


def quad_cotangent(cot, t, low):
    even, odd = [], []
    for pair in range(2):
        e, o = to_pair(
            (
                cot[2 * pair, :, t * 128 : t * 128 + 128],
                cot[2 * pair + 1, :, t * 128 : t * 128 + 128],
            ),
            low,
        )
        even.append(e)
        odd.append(o)
    return (
        jnp.concatenate(even, axis=1).astype(f32),
        jnp.concatenate(odd, axis=1).astype(f32),
    )


def from_pair(ref, at, even, odd, t, low):
    for pair in range(2):
        e = even[:, pair * 128 : pair * 128 + 128]
        o = odd[:, pair * 128 : pair * 128 + 128]
        ref[at + 2 * pair, :, t * 128 : t * 128 + 128] = jnp.where(low, e, roll(o, 64))
        ref[at + 2 * pair + 1, :, t * 128 : t * 128 + 128] = jnp.where(low, roll(e, 64), o)


def forward_kernel(
    near, lists, hidden, rxm, rxp, rym, ryp, cot, weight, elow, ehigh, ylow, yhigh,
    block_out, grad, stack_out, grad_pair, xm, xp, ym, yp, table, wide,
):
    step = pl.program_id(0)

    @pl.when(step == 0)
    def _():
        fill_table(table, hidden, rxm, rxp, rym, ryp, elow, ehigh)

    stack = stack_out.at[0]
    build_stack(step, near, table, stack)
    pre_all = jnp.dot(weight[...], stack[...], preferred_element_type=f32)
    low = lane_id(channels) < 64
    live = alive_lanes(step, near)
    for t in range(4):
        cots = quad_cotangent(cot, t, low)
        mixed, grads = [], []
        for p in range(2):
            x = 2 * t + p
            pre = pre_all[x * 32 : x * 32 + 32]
            row = (x + 1) * band + 4 * channels
            here = stack[row : row + channels, :].astype(f32)
            sigma = 0.5 * jnp.tanh(0.5 * pre) + 0.5
            mixed.append(((here + pre * sigma) * live).astype(bf16))
            grads.append((cots[p] * (sigma * (1.0 + pre * (1.0 - sigma))) * live).astype(bf16))
            grad_pair[0, x * 32 : x * 32 + 32, :] = grads[p]
        from_pair(block_out, 0, mixed[0], mixed[1], t, low)
        from_pair(grad, step * quad, grads[0], grads[1], t, low)

    @pl.when(step == steps - 1)
    def _():
        emit_faces(lists, grad, ylow, yhigh, xm, xp, ym, yp, wide)


def weight_kernel(stack, grad_pair, out, total, turned):
    step = pl.program_id(0)
    part = lax.dot_general(
        stack[0], grad_pair[0], (((1,), (1,)), ((), ())), preferred_element_type=f32
    )

    @pl.when(step == 0)
    def _():
        total[...] = part

    @pl.when(step > 0)
    def _():
        total[...] += part

    @pl.when(step == steps - 1)
    def _():
        acc = total[0 : 3 * band, 0:32]
        for x in range(1, 8):
            acc = acc + total[x * band : x * band + 3 * band, x * 32 : x * 32 + 32]
        turned[...] = jnp.zeros((1024, 128), f32)
        turned[0 : 3 * band, 0:32] = acc
        across = turned[...].T
        for j in range(4):
            out[j] = across[0:32, j * 256 : j * 256 + 256]


def backward_kernel(
    near, child, grad, rxm, rxp, rym, ryp, cot, weight, elow, ehigh, pool,
    fine_grad, back, table,
):
    step = pl.program_id(0)

    @pl.when(step == 0)
    def _():
        fill_table(table[0], grad, rxm, rxp, rym, ryp, elow, ehigh)
        back[...] = jnp.zeros_like(back)

    stack = table[1]
    build_stack(step, near, table[0], stack)
    conv = jnp.dot(weight[...], stack[...], preferred_element_type=f32)
    low = lane_id(channels) < 64
    low16 = lane_id(16) < 64
    live = alive_lanes(step, near)
    sums = []
    for t in range(4):
        cots = quad_cotangent(cot, t, low)
        full = [
            (cots[p] + conv[(2 * t + p) * 32 : (2 * t + p) * 32 + 32]) * live for p in range(2)
        ]
        from_pair(fine_grad, 0, full[0].astype(bf16), full[1].astype(bf16), t, low)
        both = full[0] + full[1]
        for pair in range(2):
            v = both[:, pair * 128 : pair * 128 + 128]
            v = v + roll(v, -1)
            v = v + roll(v, -8)
            sums.append(v.astype(bf16))
    pooled = jnp.dot(
        jnp.concatenate(sums, axis=1), pool[...], preferred_element_type=f32
    ).astype(bf16)
    for i in range(quad):
        tile = pooled[:, (i // 2) * 128 : (i // 2) * 128 + 128]
        if i % 2 == 0:
            packed = jnp.where(low16, tile[:16], roll(tile[16:], 64))
        else:
            packed = jnp.where(low16, roll(tile[:16], 64), tile[16:])
        target = child[step * quad + i]

        @pl.when(target >= 0)
        def _():
            back[target] = packed


def last_kernel(send, returned, totals, perm, coarse_grad, weight_grad, tab):
    low = lane_id(16) < 64
    tab[...] = jnp.zeros_like(tab)

    def body(i, carry):
        for j in range(8):
            d = i * 8 + j
            target = send[d]

            @pl.when(target >= 0)
            def _():
                tab[target] = returned[d]

        return carry

    lax.fori_loop(0, 16, body, 0)
    rows = []
    for i in range(8):
        tops, bottoms = [], []
        for g in range(4):
            a, b = tab[i * 8 + 2 * g], tab[i * 8 + 2 * g + 1]
            tops.append(jnp.where(low, a, roll(b, 64)))
            bottoms.append(jnp.where(low, roll(a, 64), b))
        rows.append(jnp.concatenate(tops, axis=1))
        rows.append(jnp.concatenate(bottoms, axis=1))
    spread = jnp.dot(jnp.concatenate(rows, axis=0), perm[...], preferred_element_type=f32)
    coarse_grad[...] = spread.astype(bf16).reshape(8, 32, 512)
    for k in range(27):
        weight_grad[k] = totals[k // 8, :, (k % 8) * 32 : (k % 8) * 32 + 32]


def shape(dims, kind=bf16):
    return jax.ShapeDtypeStruct(dims, kind)


def ranks(flags):
    before = (jnp.arange(capacity)[:, None] < jnp.arange(capacity)[None, :]).astype(bf16)
    return jnp.dot(flags.astype(bf16), before, preferred_element_type=f32).astype(jnp.int32)


def indices(adjacency):
    table_id = jnp.arange(9 * capacity, dtype=jnp.int32)
    hits = adjacency[:, :, None] == table_id
    rank = ranks(hits.any(axis=(0, 1)).reshape(9, capacity)).reshape(-1)
    row_base = jnp.asarray(np.repeat(np.array(place_base), capacity), jnp.int32)
    own = (table_id // capacity) == 4
    row_of = jnp.where(own, table_id % capacity, row_base + rank)
    near = jnp.sum(jnp.where(hits, row_of, 0), axis=2)
    near = jnp.where(adjacency < 0, zero_row, near)
    place = jnp.where(adjacency < 0, -1, adjacency // capacity)
    need = (place[None, :, :] == jnp.arange(9)[:, None, None]).any(axis=2)
    order = ranks(need)
    slot = jnp.arange(capacity, dtype=jnp.int32)
    pick = need[:, None, :] & (order[:, None, :] == jnp.arange(face_n)[None, :, None])
    chosen = jnp.sum(jnp.where(pick, slot, 0), axis=2)
    lists = jnp.concatenate(
        [
            chosen[1], chosen[0, :corner_n], chosen[2, :corner_n],
            chosen[7], chosen[6, :corner_n], chosen[8, :corner_n],
            chosen[3], chosen[5],
        ]
    )
    return near.reshape(-1).astype(jnp.int32), lists.astype(jnp.int32)


def banded(taps):
    return jnp.concatenate(
        [jnp.pad(taps, ((0, 0), (x * band, (7 - x) * band))) for x in range(8)], axis=0
    )


def moved(value, shift_x, shift_y):
    count_x, count_y = lax.axis_size("gx"), lax.axis_size("gy")
    pairs = [
        (i * count_y + j, (i + shift_x) * count_y + j + shift_y)
        for i in range(count_x)
        for j in range(count_y)
        if 0 <= i + shift_x < count_x and 0 <= j + shift_y < count_y
    ]
    return lax.ppermute(value, axes, pairs)


def halo(xm, xp, ym, yp):
    from_xm = moved(xp, 1, 0)
    from_xp = moved(xm, -1, 0)
    mid = face_n + corner_n
    up = jnp.concatenate([yp, from_xm[mid:], from_xp[mid:]], axis=0)
    down = jnp.concatenate([ym, from_xm[face_n:mid], from_xp[face_n:mid]], axis=0)
    from_ym = moved(up, 0, 1)
    from_yp = moved(down, 0, -1)
    return from_xm, from_xp, from_ym, from_yp


def exchange(value):
    return lax.all_to_all(value, axes, split_axis=0, concat_axis=0, tiled=True)


def whole(dims):
    return pl.BlockSpec(dims, lambda i: (0,) * len(dims))


def on_device(fine, coarse, weight, cotangent, adjacency, send_list, child_src):
    devices = lax.axis_size("gx") * lax.axis_size("gy")
    send = send_list.reshape(-1)
    perm = const(octant_matrix())
    perm_t = const(octant_matrix().T)
    y_low, y_high = y_face_matrix(0), y_face_matrix(7)
    ylow, yhigh = const(y_low), const(y_high)
    elow, ehigh = const(y_low.T), const(y_high.T)
    up = const(upsample_matrix())
    pool = const(pool_matrix())
    packed = (16, 128)
    side = shape((side_n,) + packed)
    face = shape((face_n,) + packed)

    outgoing = pl.pallas_call(
        octant_kernel,
        out_shape=shape((devices,) + packed),
        in_specs=[smem, vmem, vmem],
        out_specs=vmem,
        scratch_shapes=[pltpu.VMEM((64,) + packed, bf16)],
        compiler_params=params(),
        name="octants",
    )(send, coarse, perm)
    incoming = exchange(outgoing)

    near, lists = indices(adjacency)
    alive = (adjacency[:, 13] >= 0).astype(jnp.int32)
    taps = banded(weight.transpose(1, 0, 2).reshape(channels, 27 * channels))
    back_taps = banded(weight[::-1].transpose(2, 0, 1).reshape(channels, 27 * channels))

    hidden, xm, xp, ym, yp = pl.pallas_call(
        hidden_kernel,
        out_shape=(shape((capacity, channels, 512)), side, side, face, face),
        in_specs=[smem, smem, smem] + [vmem] * 5,
        out_specs=(vmem,) * 5,
        scratch_shapes=[pltpu.VMEM((face_n * 16, 1024), bf16)],
        compiler_params=params(),
        name="hidden",
    )(child_src, alive, lists, incoming, fine, up, ylow, yhigh)
    near_h = halo(xm, xp, ym, yp)

    bricks = whole((capacity, channels, 512))
    sides = [whole((n,) + packed) for n in (side_n, side_n, side_n, side_n)]
    per_quad = pl.BlockSpec((quad, channels, 512), lambda i: (i, 0, 0))
    stack_spec = pl.BlockSpec((1, depth, 256), lambda i: (i, 0, 0))
    pair_spec = pl.BlockSpec((1, 256, 256), lambda i: (i, 0, 0))
    table = pltpu.VMEM((table_rows, channels, 512), bf16)
    block_out, grad, stacks, grad_pair, gxm, gxp, gym, gyp = pl.pallas_call(
        forward_kernel,
        grid=(steps,),
        out_shape=(
            shape((capacity, channels, 512)),
            shape((capacity, channels, 512)),
            shape((steps, depth, 256)),
            shape((steps, 256, 256)),
            side, side, face, face,
        ),
        in_specs=[smem, smem, bricks]
        + sides
        + [per_quad, whole((256, depth))]
        + [whole((128, 1024))] * 2
        + [whole((1024, 128))] * 2,
        out_specs=(per_quad, bricks, stack_spec, pair_spec)
        + tuple(whole((n,) + packed) for n in (side_n, side_n, face_n, face_n)),
        scratch_shapes=[table, pltpu.VMEM((face_n * 16, 1024), bf16)],
        compiler_params=params(),
        name="forward",
    )(near, lists, hidden, *near_h, cotangent, taps, elow, ehigh, ylow, yhigh)
    near_g = halo(gxm, gxp, gym, gyp)

    term = pl.pallas_call(
        weight_kernel,
        grid=(steps,),
        out_shape=shape((4, 32, 256), f32),
        in_specs=[stack_spec, pair_spec],
        out_specs=whole((4, 32, 256)),
        scratch_shapes=[pltpu.VMEM((depth, 256), f32), pltpu.VMEM((1024, 128), f32)],
        compiler_params=params(),
        name="weight_term",
    )(stacks, grad_pair)
    terms = exchange(term.reshape(128, 256))
    mine = jnp.sum(terms, axis=0)
    totals = exchange(jnp.broadcast_to(mine[None, :], (devices, 256))).reshape(4, 32, 256)

    fine_grad, back = pl.pallas_call(
        backward_kernel,
        grid=(steps,),
        out_shape=(shape((capacity, channels, 512)), shape((devices,) + packed)),
        in_specs=[smem, smem, bricks]
        + sides
        + [per_quad, whole((256, depth)), whole((128, 1024)), whole((128, 1024))]
        + [whole((1024, 256))],
        out_specs=(per_quad, whole((devices,) + packed)),
        scratch_shapes=[[table, pltpu.VMEM((depth, 256), bf16)]],
        compiler_params=params(),
        name="backward",
    )(near, child_src, grad, *near_g, cotangent, back_taps, elow, ehigh, pool)
    returned = exchange(back)

    coarse_grad, weight_grad = pl.pallas_call(
        last_kernel,
        out_shape=(shape((8, channels, 512)), shape((27, channels, channels), f32)),
        in_specs=[smem, vmem, vmem, vmem],
        out_specs=(vmem, vmem),
        scratch_shapes=[pltpu.VMEM((64,) + packed, bf16)],
        compiler_params=params(),
        name="coarse",
    )(send, returned, totals, perm_t)
    return block_out, fine_grad, coarse_grad, weight_grad


def solution(mesh):
    return jax.shard_map(
        on_device,
        mesh=mesh,
        in_specs=(
            P(axes, None, None),
            P(axes, None, None),
            P(),
            P(axes, None, None),
            P(axes, None),
            P(axes, None),
            P(axes),
        ),
        out_specs=(
            P(axes, None, None),
            P(axes, None, None),
            P(axes, None, None),
            P(),
        ),
        check_vma=False,
    )
```

time: 1890 us -> 237 us (0.13); the launches traced: 1870 us -> 236 us
  local copies, waits for them, and re-layouts: 1330 us -> 14.8 us
  other arithmetic: 236 us -> 4.37 us
  Pallas kernels: 0 us -> 120 us
  matrix products: 111 us -> 0.26 us
  waiting for transfers between devices: 115 us -> 29 us
    slice x184 -> x4, local copies, waits for them, and re-layouts: 300 us -> 0.01 us  [the longest x2 0.01 us: halo(): from_xm[face_n:mid]]
    while x1347 -> x0, local copies, waits for them, and re-layouts: 276 us -> none
    unnamed x449 -> x49, local copies, waits for them, and re-layouts: 177 us -> 9.47 us
    another operation x97 -> x0, local copies, waits for them, and re-layouts: 132 us -> none  [the longest x32 126 us: assemble(): portions[off_x, off_y, off_z] = jnp.take(lookup, row_ids, axis=0)]
    gather x55 -> x0, local copies, waits for them, and re-layouts: 122 us -> none  [the longest x52 117 us: assemble(): portions[off_x, off_y, off_z] = jnp.take(lookup, row_ids, axis=0)]
    pallas_call x0 -> x6, Pallas kernels: none -> 120 us  [the longest x1 45.5 us: on_device(): pl.pallas_call(forward_kernel, grid=(steps,), out_shape=(shape((capacity,...]
    dot_general x50 -> x2, matrix products: 111 us -> 0.26 us  [ranks(): jnp.dot(flags.astype(bf16), before, preferred_element_type=f32)]
    psum x1 -> x0, waiting for transfers between devices: 101 us -> none  [on_device(): weight_grad = lax.psum(local_grad, ('gx', 'gy'))]
  transfers between devices with their start and end apart: 11 -> 12, of which waited for: 3 -> 5; matrix products, arithmetic and copies ran while one was open for 30% -> 7% of each run, Pallas kernels for 0% -> 27%
where the time goes in v1:
time: 237 us; the launch traced here: 236 us
  Pallas kernels  120 us (51%)
  starting transfers between devices  66.5 us (28%)
  waiting for transfers between devices  29 us (12%)
  local copies, waits for them, and re-layouts  14.8 us (6%)
  other arithmetic  4.37 us (2%)
    pallas_call x1, Pallas kernels, on_device(): pl.pallas_call(forward_kernel, grid=(steps,), out_shape=(shape((capacity,...  45.5 us
    all_to_all x4, starting transfers between devices, exchange(): return lax.all_to_all(value, axes, split_axis=0, concat_axis=0, tiled=True)  45 us
    pallas_call x1, Pallas kernels, on_device(): pl.pallas_call(backward_kernel, grid=(steps,), out_shape=(shape((capacity...  42.1 us
    ppermute x8, starting transfers between devices, moved(): return lax.ppermute(value, axes, pairs)  21.5 us
    pallas_call x1, Pallas kernels, on_device(): pl.pallas_call(weight_kernel, grid=(steps,), out_shape=shape((4, 32, 256)...  21.1 us
    all_to_all x4, waiting for transfers between devices, exchange(): return lax.all_to_all(value, axes, split_axis=0, concat_axis=0, tiled=True)  19.2 us
    ppermute x8, waiting for transfers between devices, moved(): return lax.ppermute(value, axes, pairs)  9.75 us
    unnamed x49, local copies, waits for them, and re-layouts  9.47 us
  transfers between devices with their start and end apart: 12, of which 5 were waited for; matrix products, arithmetic and copies ran while one was open for 7% of the time, Pallas kernels for 27%

profile of v1, /device:TPU:1, one launch (start us, length us, event | category | flops | bytes accessed | tf_op | source)
XLA Modules:
  0.0 236.3 jit_solution(3042704084415145034)
XLA Ops:
  0.7 2.6 %octants.1 = bf16[128,16,128]{2,1,0:T(8,128)(2,1)} custom-call(s32[128]{0:T(128)} %bitcast.31, bf16[8,32,512]{2,1,0:T(8,128)(2,1)} %coarse.2, bf16[512,512]{1,0:T(8,128)(2,1)} %constant.72.clone.perm), custom_call_target="tpu_custom_call" | custom-call | tf_op jit(solution)/shard_map/octants/pallas_call | solution.py:514
  3.3 11.5 %all-to-all-start = ((bf16[128,16,128]{2,1,0:T(8,128)(2,1)}), bf16[128,16,128]{2,1,0:T(8,128)(2,1)S(1)}, u32[]{:S(2)}, u32[]{:S(2)}) async-start(bf16[128,16,128]{2,1,0:T(8,128)(2,1)} %octants.1), calls=%async_computation | async-start | bytes 1048576 | tf_op jit(solution)/shard_map/all_to_all | solution.py:493
  15.6 1.0 select_reduce_fusion
  18.2 0.8 pad_dynamic-update-slice_fusion.7
  19.1 0.8 pad_dynamic-update-slice_fusion.6
  19.9 0.8 pad_dynamic-update-slice_fusion.5
  22.6 6.0 %all-to-all-done.incoming = bf16[128,16,128]{2,1,0:T(8,128)(2,1)S(1)} async-done(((bf16[128,16,128]{2,1,0:T(8,128)(2,1)}), bf16[128,16,128]{2,1,0:T(8,128)(2,1)S(1)}, u32[]{:S(2)}, u32[]{:S(2)}) %all-to-all-start) | async-done | bytes 524320 | tf_op jit(solution)/shard_map/all_to_all | solution.py:493
  28.6 0.8 copy-done.1
  29.4 5.4 %hidden.1 = (bf16[64,32,512]{2,1,0:T(8,128)(2,1)}, bf16[24,16,128]{2,1,0:T(8,128)(2,1)}, bf16[24,16,128]{2,1,0:T(8,128)(2,1)}, bf16[16,16,128]{2,1,0:T(8,128)(2,1)}, bf16[16,16,128]{2,1,0:T(8,128)(2,1)}) custom-call(s32[64]{0:T(128)} %child.3, s32[64]{0:T(128)} %fusion.16.alive, s32[80]{0:T(128)} %concatenate.21.lists, bf16[128,16,128]{2,1,0:T(8,128)(2,1)} %copy-done.1, ...), custom_call_target="tpu_custom_call" | custom-call | tf_op jit(solution)/shard_map/hidden/pallas_call | solution.py:530
  34.8 1.3 collective-permute-start
  36.9 1.3 collective-permute-start.1
  38.6 4.4 %collective-permute-done.1.rxp = bf16[24,16,128]{2,1,0:T(8,128)(2,1)S(1)} collective-permute-done((bf16[24,16,128]{2,1,0:T(8,128)(2,1)}, bf16[24,16,128]{2,1,0:T(8,128)(2,1)S(1)}, u32[]{:S(2)}, u32[]{:S(2)}) %collective-permute-start.1) | collective-permute-done | bytes 98336 | tf_op jit(solution)/shard_map/ppermute | solution.py:478
  43.0 0.9 pad_maximum_fusion.1
  43.9 3.1 %collective-permute-start.3 = (bf16[24,16,128]{2,1,0:T(8,128)(2,1)S(1)}, bf16[24,16,128]{2,1,0:T(8,128)(2,1)S(1)}, u32[]{:S(2)}, u32[]{:S(2)}) collective-permute-start(bf16[24,16,128]{2,1,0:T(8,128)(2,1)S(1)} %pad_maximum_fusion.1), channel_id=1, source_target_pairs={{1,0},{2,1},{3,2},{4,3},{5,4},{6,5},{7,6},{8,7},{9,8},{10,9},{11,1... | collective-permute-start | bytes 294920 | tf_op jit(solution)/shard_map/ppermute | solution.py:478
  47.0 0.9 pad_maximum_fusion
  47.8 4.0 %collective-permute-start.2 = (bf16[24,16,128]{2,1,0:T(8,128)(2,1)S(1)}, bf16[24,16,128]{2,1,0:T(8,128)(2,1)S(1)}, u32[]{:S(2)}, u32[]{:S(2)}) collective-permute-start(bf16[24,16,128]{2,1,0:T(8,128)(2,1)S(1)} %pad_maximum_fusion), channel_id=1, source_target_pairs={{0,1},{1,2},{2,3},{3,4},{4,5},{5,6},{6,7},{7,8},{8,9},{9,10},{10,1... | collective-permute-start | bytes 294920 | tf_op jit(solution)/shard_map/ppermute | solution.py:478
  54.1 45.5 %forward.1 = (bf16[64,32,512]{2,1,0:T(8,128)(2,1)}, bf16[64,32,512]{2,1,0:T(8,128)(2,1)}, bf16[16,2880,256]{2,1,0:T(8,128)(2,1)}, bf16[16,256,256]{2,1,0:T(8,128...) custom-call(s32[1728]{0:T(1024)} %reshape.50.near, ...), custom_call_target="tpu_custom_call" | custom-call | tf_op jit(solution)/shard_map/forward/pallas_call | solution.py:547
  99.7 2.4 %collective-permute-start.4 = (bf16[24,16,128]{2,1,0:T(8,128)(2,1)}, bf16[24,16,128]{2,1,0:T(8,128)(2,1)S(1)}, u32[]{:S(2)}, u32[]{:S(2)}) collective-permute-start(bf16[24,16,128]{2,1,0:T(8,128)(2,1)} %get-tuple-element.28), channel_id=1, source_target_pairs={{0,16},{1,17},{2,18},{3,19},{4,20},{5,21},{6,22},{7,23},{8,24},{9,... | collective-permute-start | bytes 294920 | tf_op jit(solution)/shard_map/ppermute | solution.py:478
  102.0 0.8 pad_dynamic-update-slice_fusion.1
  102.8 21.1 %weight_term.1 = f32[4,32,256]{2,1,0:T(8,128)} custom-call(bf16[16,2880,256]{2,1,0:T(8,128)(2,1)} %get-tuple-element.34.stack, bf16[16,256,256]{2,1,0:T(8,128)(2,1)} %get-tuple-element.35.grad_pair), custom_call_target="tpu_custom_call" | custom-call | tf_op jit(solution)/shard_map/weight_term/pallas_call | solution.py:570
  123.9 1.7 copy.38
  125.6 12.6 %all-to-all-start.2 = ((f32[128,1,256]{2,1,0:T(1,128)}), f32[128,1,256]{2,1,0:T(1,128)S(1)}, u32[]{:S(2)}, u32[]{:S(2)}) async-start(f32[128,1,256]{2,1,0:T(1,128)} %copy.38), calls=%async_computation.2 | async-start | bytes 262144 | tf_op jit(solution)/shard_map/all_to_all | solution.py:493
  138.2 1.3 collective-permute-start.5
  139.5 4.9 %collective-permute-done.5.rxp = bf16[24,16,128]{2,1,0:T(8,128)(2,1)S(1)} collective-permute-done((bf16[24,16,128]{2,1,0:T(8,128)(2,1)S(1)}, bf16[24,16,128]{2,1,0:T(8,128)(2,1)S(1)}, u32[]{:S(2)}, u32[]{:S(2)}) %collective-permute-start.5) | collective-permute-done | bytes 98336 | tf_op jit(solution)/shard_map/ppermute | solution.py:478
  144.4 3.8 %collective-permute-start.7 = (bf16[24,16,128]{2,1,0:T(8,128)(2,1)S(1)}, bf16[24,16,128]{2,1,0:T(8,128)(2,1)S(1)}, u32[]{:S(2)}, u32[]{:S(2)}) collective-permute-start(bf16[24,16,128]{2,1,0:T(8,128)(2,1)S(1)} %pad_maximum_fusion.3), channel_id=1, source_target_pairs={{1,0},{2,1},{3,2},{4,3},{5,4},{6,5},{7,6},{8,7},{9,8},{10,9},{11,1... | collective-permute-start | bytes 294920 | tf_op jit(solution)/shard_map/ppermute | solution.py:478
  148.2 4.4 %collective-permute-start.6 = (bf16[24,16,128]{2,1,0:T(8,128)(2,1)S(1)}, bf16[24,16,128]{2,1,0:T(8,128)(2,1)S(1)}, u32[]{:S(2)}, u32[]{:S(2)}) collective-permute-start(bf16[24,16,128]{2,1,0:T(8,128)(2,1)S(1)} %pad_maximum_fusion.2), channel_id=1, source_target_pairs={{0,1},{1,2},{2,3},{3,4},{4,5},{5,6},{6,7},{7,8},{8,9},{9,10},{10,1... | collective-permute-start | bytes 294920 | tf_op jit(solution)/shard_map/ppermute | solution.py:478
  153.5 11.2 %all-to-all-start.3 = ((f32[128,1,256]{2,1,0:T(1,128)}), f32[128,1,256]{2,1,0:T(1,128)S(1)}, u32[]{:S(2)}, u32[]{:S(2)}) async-start(f32[128,1,256]{2,1,0:T(1,128)} %broadcast_in_dim.46), calls=%async_computation.3 | async-start | bytes 262144 | tf_op jit(solution)/shard_map/all_to_all | solution.py:493
  166.1 42.1 %backward.1 = (bf16[64,32,512]{2,1,0:T(8,128)(2,1)}, bf16[128,16,128]{2,1,0:T(8,128)(2,1)}) custom-call(s32[1728]{0:T(1024)} %reshape.50.near, s32[64]{0:T(128)} %child.3, bf16[64,32,512]{2,1,0:T(8,128)(2,1)} %get-tuple-element.27.grad, bf16[24,16,128]{2,1,0:T(8,128)(2,1)} %copy-done.4, bf16[24,16,128]{2,1,0:T(8,128)(2,1)} %copy-done.6, ...), custom_call_target="tpu_custom_call" | custom-call | tf_op jit(solution)/shard_map/backward/pallas_call | solution.py:584
  208.2 9.8 %all-to-all-start.1 = ((bf16[128,16,128]{2,1,0:T(8,128)(2,1)}), bf16[128,16,128]{2,1,0:T(8,128)(2,1)S(1)}, u32[]{:S(2)}, u32[]{:S(2)}) async-start(bf16[128,16,128]{2,1,0:T(8,128)(2,1)} %get-tuple-element.33), calls=%async_computation.1 | async-start | bytes 1048576 | tf_op jit(solution)/shard_map/all_to_all | solution.py:493
  218.7 13.2 %all-to-all-done.1.returned = bf16[128,16,128]{2,1,0:T(8,128)(2,1)S(1)} async-done(((bf16[128,16,128]{2,1,0:T(8,128)(2,1)}), bf16[128,16,128]{2,1,0:T(8,128)(2,1)S(1)}, u32[]{:S(2)}, u32[]{:S(2)}) %all-to-all-start.1) | async-done | bytes 524320 | tf_op jit(solution)/shard_map/all_to_all | solution.py:493
  231.9 0.8 copy-done
  232.7 3.6 %coarse.3 = (bf16[8,32,512]{2,1,0:T(8,128)(2,1)}, f32[27,32,32]{2,1,0:T(8,128)}) custom-call(s32[128]{0:T(128)} %bitcast.32, bf16[128,16,128]{2,1,0:T(8,128)(2,1)} %copy-done, f32[4,32,256]{2,1,0:T(8,128)} %bitcast.30, bf16[512,512]{1,0:T(8,128)(2,1)} %constant.73.clone.perm), custom_call_target="tpu_custom_call" | custom-call | tf_op jit(solution)/shard_map/coarse/pallas_call | solution.py:599
  (80 shorter events, 10.8 us)
Async XLA Ops:
  0.6 14.8 %copy-start.15 = (s32[9,64]{1,0:T(8,128)S(1)}, s32[9,64]{1,0:T(8,128)}, u32[]{:S(2)}) copy-start(s32[9,64]{1,0:T(8,128)} %constant.118) | copy-start | bytes 6916
  0.6 14.1 %copy-start.8 = (s32[64,27]{0,1:T(8,128)S(1)}, s32[64,27]{0,1:T(8,128)}, u32[]{:S(2)}) copy-start(s32[64,27]{0,1:T(8,128)} %param.20) | copy-start | bytes 20740
  0.7 16.5 %copy-start.3 = (bf16[27,32,32]{2,1,0:T(8,128)(2,1)S(1)}, bf16[27,32,32]{2,1,0:T(8,128)(2,1)}, u32[]{:S(2)}) copy-start(bf16[27,32,32]{2,1,0:T(8,128)(2,1)} %param.18) | copy-start | bytes 165892
  3.3 25.4 %all-to-all-start = ((bf16[128,16,128]{2,1,0:T(8,128)(2,1)}), bf16[128,16,128]{2,1,0:T(8,128)(2,1)S(1)}, u32[]{:S(2)}, u32[]{:S(2)}) async-start(bf16[128,16,128]{2,1,0:T(8,128)(2,1)} %octants.1), calls=%async_computation | async-start | bytes 1048576 | tf_op jit(solution)/shard_map/all_to_all | solution.py:493
  18.1 35.4 %copy-start.2 = (bf16[256,2880]{1,0:T(8,128)(2,1)}, bf16[256,2880]{1,0:T(8,128)(2,1)S(1)}, u32[]{:S(2)}) copy-start(bf16[256,2880]{1,0:T(8,128)(2,1)S(1)} %pad_dynamic-update-slice_fusion.8.weight) | copy-start | bytes 4423684
  28.6 0.8 copy-start.1
  34.8 3.8 %collective-permute-start = (bf16[24,16,128]{2,1,0:T(8,128)(2,1)}, bf16[24,16,128]{2,1,0:T(8,128)(2,1)S(1)}, u32[]{:S(2)}, u32[]{:S(2)}) collective-permute-start(bf16[24,16,128]{2,1,0:T(8,128)(2,1)} %get-tuple-element.22), channel_id=1, source_target_pairs={{0,16},{1,17},{2,18},{3,19},{4,20},{5,21},{6,22},{7,23},{8,24},{9,... | collective-permute-start | bytes 294920 | tf_op jit(solution)/shard_map/ppermute | solution.py:478
  36.9 6.1 %collective-permute-start.1 = (bf16[24,16,128]{2,1,0:T(8,128)(2,1)}, bf16[24,16,128]{2,1,0:T(8,128)(2,1)S(1)}, u32[]{:S(2)}, u32[]{:S(2)}) collective-permute-start(bf16[24,16,128]{2,1,0:T(8,128)(2,1)} %get-tuple-element.23), channel_id=1, source_target_pairs={{16,0},{17,1},{18,2},{19,3},{20,4},{21,5},{22,6},{23,7},{24,8},{25... | collective-permute-start | bytes 294920 | tf_op jit(solution)/shard_map/ppermute | solution.py:478
  38.6 14.8 %copy-start.5 = (bf16[24,16,128]{2,1,0:T(8,128)(2,1)}, bf16[24,16,128]{2,1,0:T(8,128)(2,1)S(1)}, u32[]{:S(2)}) copy-start(bf16[24,16,128]{2,1,0:T(8,128)(2,1)S(1)} %collective-permute-done.rxm) | copy-start | bytes 294916
  43.0 10.5 %copy-start.7 = (bf16[24,16,128]{2,1,0:T(8,128)(2,1)}, bf16[24,16,128]{2,1,0:T(8,128)(2,1)S(1)}, u32[]{:S(2)}) copy-start(bf16[24,16,128]{2,1,0:T(8,128)(2,1)S(1)} %collective-permute-done.1.rxp) | copy-start | bytes 294916
  43.9 9.5 %collective-permute-start.3 = (bf16[24,16,128]{2,1,0:T(8,128)(2,1)S(1)}, bf16[24,16,128]{2,1,0:T(8,128)(2,1)S(1)}, u32[]{:S(2)}, u32[]{:S(2)}) collective-permute-start(bf16[24,16,128]{2,1,0:T(8,128)(2,1)S(1)} %pad_maximum_fusion.1), channel_id=1, source_target_pairs={{1,0},{2,1},{3,2},{4,3},{5,4},{6,5},{7,6},{8,7},{9,8},{10,9},{11,1... | collective-permute-start | bytes 294920 | tf_op jit(solution)/shard_map/ppermute | solution.py:478
  47.8 5.6 %collective-permute-start.2 = (bf16[24,16,128]{2,1,0:T(8,128)(2,1)S(1)}, bf16[24,16,128]{2,1,0:T(8,128)(2,1)S(1)}, u32[]{:S(2)}, u32[]{:S(2)}) collective-permute-start(bf16[24,16,128]{2,1,0:T(8,128)(2,1)S(1)} %pad_maximum_fusion), channel_id=1, source_target_pairs={{0,1},{1,2},{2,3},{3,4},{4,5},{5,6},{6,7},{7,8},{8,9},{9,10},{10,1... | collective-permute-start | bytes 294920 | tf_op jit(solution)/shard_map/ppermute | solution.py:478
  53.4 0.6 copy-start.10
  53.5 0.6 copy-start.12
  99.7 39.8 %collective-permute-start.4 = (bf16[24,16,128]{2,1,0:T(8,128)(2,1)}, bf16[24,16,128]{2,1,0:T(8,128)(2,1)S(1)}, u32[]{:S(2)}, u32[]{:S(2)}) collective-permute-start(bf16[24,16,128]{2,1,0:T(8,128)(2,1)} %get-tuple-element.28), channel_id=1, source_target_pairs={{0,16},{1,17},{2,18},{3,19},{4,20},{5,21},{6,22},{7,23},{8,24},{9,... | collective-permute-start | bytes 294920 | tf_op jit(solution)/shard_map/ppermute | solution.py:478
  102.8 35.4 %copy-start.16 = (bf16[24,16,128]{2,1,0:T(8,128)(2,1)S(1)}, bf16[24,16,128]{2,1,0:T(8,128)(2,1)}, u32[]{:S(2)}) copy-start(bf16[24,16,128]{2,1,0:T(8,128)(2,1)} %get-tuple-element.29) | copy-start | bytes 294916
  102.8 41.6 %copy-start.14 = (bf16[16,16,128]{2,1,0:T(8,128)(2,1)S(1)}, bf16[16,16,128]{2,1,0:T(8,128)(2,1)}, u32[]{:S(2)}) copy-start(bf16[16,16,128]{2,1,0:T(8,128)(2,1)} %get-tuple-element.31) | copy-start | bytes 196612
  102.8 45.4 %copy-start.13 = (bf16[16,16,128]{2,1,0:T(8,128)(2,1)S(1)}, bf16[16,16,128]{2,1,0:T(8,128)(2,1)}, u32[]{:S(2)}) copy-start(bf16[16,16,128]{2,1,0:T(8,128)(2,1)} %get-tuple-element.30) | copy-start | bytes 196612
  125.6 27.0 %all-to-all-start.2 = ((f32[128,1,256]{2,1,0:T(1,128)}), f32[128,1,256]{2,1,0:T(1,128)S(1)}, u32[]{:S(2)}, u32[]{:S(2)}) async-start(f32[128,1,256]{2,1,0:T(1,128)} %copy.38), calls=%async_computation.2 | async-start | bytes 262144 | tf_op jit(solution)/shard_map/all_to_all | solution.py:493
  138.2 6.2 %collective-permute-start.5 = (bf16[24,16,128]{2,1,0:T(8,128)(2,1)S(1)}, bf16[24,16,128]{2,1,0:T(8,128)(2,1)S(1)}, u32[]{:S(2)}, u32[]{:S(2)}) collective-permute-start(bf16[24,16,128]{2,1,0:T(8,128)(2,1)S(1)} %copy-done.16), channel_id=1, source_target_pairs={{16,0},{17,1},{18,2},{19,3},{20,4},{21,5},{22,6},{23,7},{24,8},{25... | collective-permute-start | bytes 294920 | tf_op jit(solution)/shard_map/ppermute | solution.py:478
  139.5 25.9 %copy-start.4 = (bf16[24,16,128]{2,1,0:T(8,128)(2,1)}, bf16[24,16,128]{2,1,0:T(8,128)(2,1)S(1)}, u32[]{:S(2)}) copy-start(bf16[24,16,128]{2,1,0:T(8,128)(2,1)S(1)} %collective-permute-done.4.rxm) | copy-start | bytes 294916
  144.4 21.1 %copy-start.6 = (bf16[24,16,128]{2,1,0:T(8,128)(2,1)}, bf16[24,16,128]{2,1,0:T(8,128)(2,1)S(1)}, u32[]{:S(2)}) copy-start(bf16[24,16,128]{2,1,0:T(8,128)(2,1)S(1)} %collective-permute-done.5.rxp) | copy-start | bytes 294916
  144.4 21.0 %collective-permute-start.7 = (bf16[24,16,128]{2,1,0:T(8,128)(2,1)S(1)}, bf16[24,16,128]{2,1,0:T(8,128)(2,1)S(1)}, u32[]{:S(2)}, u32[]{:S(2)}) collective-permute-start(bf16[24,16,128]{2,1,0:T(8,128)(2,1)S(1)} %pad_maximum_fusion.3), channel_id=1, source_target_pairs={{1,0},{2,1},{3,2},{4,3},{5,4},{6,5},{7,6},{8,7},{9,8},{10,9},{11,1... | collective-permute-start | bytes 294920 | tf_op jit(solution)/shard_map/ppermute | solution.py:478
  148.2 17.2 %collective-permute-start.6 = (bf16[24,16,128]{2,1,0:T(8,128)(2,1)S(1)}, bf16[24,16,128]{2,1,0:T(8,128)(2,1)S(1)}, u32[]{:S(2)}, u32[]{:S(2)}) collective-permute-start(bf16[24,16,128]{2,1,0:T(8,128)(2,1)S(1)} %pad_maximum_fusion.2), channel_id=1, source_target_pairs={{0,1},{1,2},{2,3},{3,4},{4,5},{5,6},{6,7},{7,8},{8,9},{9,10},{10,1... | collective-permute-start | bytes 294920 | tf_op jit(solution)/shard_map/ppermute | solution.py:478
  153.5 54.7 %all-to-all-start.3 = ((f32[128,1,256]{2,1,0:T(1,128)}), f32[128,1,256]{2,1,0:T(1,128)S(1)}, u32[]{:S(2)}, u32[]{:S(2)}) async-start(f32[128,1,256]{2,1,0:T(1,128)} %broadcast_in_dim.46), calls=%async_computation.3 | async-start | bytes 262144 | tf_op jit(solution)/shard_map/all_to_all | solution.py:493
  165.4 0.6 copy-start.9
  165.4 0.7 copy-start.11
  208.2 23.6 %all-to-all-start.1 = ((bf16[128,16,128]{2,1,0:T(8,128)(2,1)}), bf16[128,16,128]{2,1,0:T(8,128)(2,1)S(1)}, u32[]{:S(2)}, u32[]{:S(2)}) async-start(bf16[128,16,128]{2,1,0:T(8,128)(2,1)} %get-tuple-element.33), calls=%async_computation.1 | async-start | bytes 1048576 | tf_op jit(solution)/shard_map/all_to_all | solution.py:493
  231.9 0.8 copy-start

commit v2 on v1

--- a/solution.py
+++ b/solution.py
@@ -195,12 +195,21 @@
     )
 
 
-def build_stack(step, near, table, stack):
+def shift_matrix():
+    out = np.zeros((256, 256), np.float32)
+    for lane in range(128):
+        z = lane % 8
+        out[lane - 1 if z > 0 else 128 + lane + 7, lane] = 1
+        out[lane + 1 if z < 7 else 128 + lane - 7, 128 + lane] = 1
+    return out
+
+
+def build_stack(index, near, table, shift, kinds, turned, stack):
     lane = lane_id(channels)
     inner = lane & 63
     low = lane < 64
     y_first, y_last = inner < 8, inner >= 56
-    z_first, z_last = (lane & 7) == 0, (lane & 7) == 7
+    z_last = (lane & 7) == 7
 
     def sources(brick, off_x, tile):
         def at(off_y, off_z):
@@ -209,8 +218,8 @@
 
         return (
             at(0, 0),
+            jnp.where(z_last, at(0, -1), at(0, 1)),
             jnp.where(y_last, at(-1, 0), at(1, 0)),
-            jnp.where(z_last, at(0, -1), at(0, 1)),
             jnp.where(
                 y_last,
                 jnp.where(z_last, at(-1, -1), at(-1, 1)),
@@ -218,40 +227,41 @@
             ),
         )
 
-    def shifts(plane, pair, kinds):
-        own, near_y, near_z, near_yz = kinds
-        own_z = (
-            jnp.where(z_first, roll(near_z, -7), roll(own, 1)),
-            own,
-            jnp.where(z_last, roll(near_z, 7), roll(own, -1)),
-        )
-        next_z = (
-            jnp.where(z_first, roll(near_yz, -7), roll(near_y, 1)),
-            near_y,
-            jnp.where(z_last, roll(near_yz, 7), roll(near_y, -1)),
-        )
-        for k in range(3):
-            trio = (
-                jnp.where(y_first, roll(next_z[k], -56), roll(own_z[k], 8)),
-                own_z[k],
-                jnp.where(y_last, roll(next_z[k], 56), roll(own_z[k], -8)),
-            )
-            for j in range(3):
-                row = plane * band + (j * 3 + k) * channels
-                stack[row : row + channels, pair * 128 : pair * 128 + 128] = trio[j]
-
     for pair in range(2):
-        b0 = step * quad + 2 * pair
+        b0 = index * quad + 2 * pair
         for off_x, tile in ((-1, 3), (0, 0), (0, 1), (0, 2), (0, 3), (1, 0)):
             first = sources(b0, off_x, tile)
             second = sources(b0 + 1, off_x, tile)
-            both = [to_pair(ab, low) for ab in zip(first, second)]
-            if off_x <= 0:
-                plane = 0 if off_x < 0 else 2 + 2 * tile
-                shifts(plane, pair, [b[1] for b in both])
-            if off_x >= 0:
-                plane = 9 if off_x > 0 else 1 + 2 * tile
-                shifts(plane, pair, [b[0] for b in both])
+            for kind in range(4):
+                swap = kind >= 2
+                even, odd = to_pair(
+                    (second[kind], first[kind]) if swap else (first[kind], second[kind]), low
+                )
+                base = (2 * pair + kind // 2) * 320
+                at_lane = (kind % 2) * 128
+                if off_x <= 0:
+                    row = base + (0 if off_x < 0 else 2 + 2 * tile) * channels
+                    kinds[row : row + channels, at_lane : at_lane + 128] = odd
+                if off_x >= 0:
+                    row = base + (9 if off_x > 0 else 1 + 2 * tile) * channels
+                    kinds[row : row + channels, at_lane : at_lane + 128] = even
+    turned[...] = jnp.dot(kinds[...], shift[...], preferred_element_type=f32).astype(bf16)
+    for pair in range(2):
+        for plane in range(10):
+            own_row = 2 * pair * 320 + plane * channels
+            far_row = own_row + 320
+            for k in range(3):
+                source, at_lane = ((turned, 0), (kinds, 0), (turned, 128))[k]
+                own = source[own_row : own_row + channels, at_lane : at_lane + 128]
+                far = source[far_row : far_row + channels, at_lane : at_lane + 128]
+                trio = (
+                    roll(jnp.where(y_last, far, own), 8),
+                    own,
+                    roll(jnp.where(y_first, far, own), -8),
+                )
+                for j in range(3):
+                    row = plane * band + (j * 3 + k) * channels
+                    stack[row : row + channels, pair * 128 : pair * 128 + 128] = trio[j]
 
 
 def alive_lanes(step, near):
@@ -263,13 +273,13 @@
     return out
 
 
-def quad_cotangent(cot, t, low):
+def quad_cotangent(cot, at, t, low):
     even, odd = [], []
     for pair in range(2):
         e, o = to_pair(
             (
-                cot[2 * pair, :, t * 128 : t * 128 + 128],
-                cot[2 * pair + 1, :, t * 128 : t * 128 + 128],
+                cot[at + 2 * pair, :, t * 128 : t * 128 + 128],
+                cot[at + 2 * pair + 1, :, t * 128 : t * 128 + 128],
             ),
             low,
         )
@@ -290,113 +300,153 @@
 
 
 def forward_kernel(
-    near, lists, hidden, rxm, rxp, rym, ryp, cot, weight, elow, ehigh, ylow, yhigh,
-    block_out, grad, stack_out, grad_pair, xm, xp, ym, yp, table, wide,
+    near, lists, hidden, rxm, rxp, rym, ryp, cot, weight, elow, ehigh, ylow, yhigh, shift,
+    block_out, grad, term, xm, xp, ym, yp,
+    table, wide, kinds, turned, stacks, total, term_wide,
 ):
     step = pl.program_id(0)
+
+    def build(index, slot):
+        build_stack(index, near, table, shift, kinds[slot], turned[slot], stacks[slot])
 
     @pl.when(step == 0)
     def _():
         fill_table(table, hidden, rxm, rxp, rym, ryp, elow, ehigh)
-
-    stack = stack_out.at[0]
-    build_stack(step, near, table, stack)
-    pre_all = jnp.dot(weight[...], stack[...], preferred_element_type=f32)
+        total[...] = jnp.zeros_like(total)
+        build(0, 0)
+
     low = lane_id(channels) < 64
-    live = alive_lanes(step, near)
-    for t in range(4):
-        cots = quad_cotangent(cot, t, low)
-        mixed, grads = [], []
-        for p in range(2):
-            x = 2 * t + p
-            pre = pre_all[x * 32 : x * 32 + 32]
-            row = (x + 1) * band + 4 * channels
-            here = stack[row : row + channels, :].astype(f32)
-            sigma = 0.5 * jnp.tanh(0.5 * pre) + 0.5
-            mixed.append(((here + pre * sigma) * live).astype(bf16))
-            grads.append((cots[p] * (sigma * (1.0 + pre * (1.0 - sigma))) * live).astype(bf16))
-            grad_pair[0, x * 32 : x * 32 + 32, :] = grads[p]
-        from_pair(block_out, 0, mixed[0], mixed[1], t, low)
-        from_pair(grad, step * quad, grads[0], grads[1], t, low)
-
-    @pl.when(step == steps - 1)
+
+    def process(index, slot):
+        stack = stacks[slot]
+        pre_all = jnp.dot(weight[...], stack[...], preferred_element_type=f32)
+        live = alive_lanes(index, near)
+        grad_pair = []
+        for t in range(4):
+            cots = quad_cotangent(cot, slot * quad, t, low)
+            mixed, grads = [], []
+            for p in range(2):
+                x = 2 * t + p
+                pre = pre_all[x * 32 : x * 32 + 32]
+                row = (x + 1) * band + 4 * channels
+                here = stack[row : row + channels, :].astype(f32)
+                sigma = 0.5 * jnp.tanh(0.5 * pre) + 0.5
+                mixed.append(((here + pre * sigma) * live).astype(bf16))
+                grads.append((cots[p] * (sigma * (1.0 + pre * (1.0 - sigma))) * live).astype(bf16))
+            from_pair(block_out, slot * quad, mixed[0], mixed[1], t, low)
+            from_pair(grad, index * quad, grads[0], grads[1], t, low)
+            grad_pair += grads
+        grad_all = jnp.concatenate(grad_pair, axis=0)
+        for x in range(10):
+            total[x * band : x * band + band] += lax.dot_general(
+                stack[x * band : x * band + band],
+                grad_all,
+                (((1,), (1,)), ((), ())),
+                preferred_element_type=f32,
+            )
+
+    build(2 * step + 1, 1)
+    process(2 * step, 0)
+    build(jnp.minimum(2 * step + 2, steps - 1), 0)
+    process(2 * step + 1, 1)
+
+    @pl.when(step == steps // 2 - 1)
     def _():
         emit_faces(lists, grad, ylow, yhigh, xm, xp, ym, yp, wide)
-
-
-def weight_kernel(stack, grad_pair, out, total, turned):
-    step = pl.program_id(0)
-    part = lax.dot_general(
-        stack[0], grad_pair[0], (((1,), (1,)), ((), ())), preferred_element_type=f32
-    )
-
-    @pl.when(step == 0)
-    def _():
-        total[...] = part
-
-    @pl.when(step > 0)
-    def _():
-        total[...] += part
-
-    @pl.when(step == steps - 1)
-    def _():
         acc = total[0 : 3 * band, 0:32]
         for x in range(1, 8):
             acc = acc + total[x * band : x * band + 3 * band, x * 32 : x * 32 + 32]
-        turned[...] = jnp.zeros((1024, 128), f32)
-        turned[0 : 3 * band, 0:32] = acc
-        across = turned[...].T
+        term_wide[...] = jnp.zeros((1024, 128), f32)
+        term_wide[0 : 3 * band, 0:32] = acc
+        across = term_wide[...].T
         for j in range(4):
-            out[j] = across[0:32, j * 256 : j * 256 + 256]
+            term[j] = across[0:32, j * 256 : j * 256 + 256]
 
 
 def backward_kernel(
-    near, child, grad, rxm, rxp, rym, ryp, cot, weight, elow, ehigh, pool,
-    fine_grad, back, table,
+    near, child, grad, rxm, rxp, rym, ryp, cot, weight, elow, ehigh, pool, shift, terms,
+    fine_grad, back,
+    table, kinds, turned, stacks, octants,
 ):
     step = pl.program_id(0)
 
+    def build(index, slot):
+        build_stack(index, near, table, shift, kinds[slot], turned[slot], stacks[slot])
+
     @pl.when(step == 0)
     def _():
-        fill_table(table[0], grad, rxm, rxp, rym, ryp, elow, ehigh)
-        back[...] = jnp.zeros_like(back)
-
-    stack = table[1]
-    build_stack(step, near, table[0], stack)
-    conv = jnp.dot(weight[...], stack[...], preferred_element_type=f32)
+        fill_table(table, grad, rxm, rxp, rym, ryp, elow, ehigh)
+        build(0, 0)
+        rest = jnp.sum(terms[...], axis=0, keepdims=True)
+        rows = []
+        for i in range(3):
+            part = rest.astype(bf16)
+            rest = rest - part.astype(f32)
+            rows += [part[:, 0:128].astype(f32), part[:, 128:256].astype(f32)]
+        rows += [jnp.zeros((2, 128), f32)]
+        tail = jnp.concatenate(rows, axis=0).astype(bf16)
+        clear = jnp.zeros((16, 128), bf16)
+
+        def body(i, carry):
+            for j in range(8):
+                back[i * 8 + j, 0:16, :] = clear
+                back[i * 8 + j, 16:24, :] = tail
+            return carry
+
+        lax.fori_loop(0, 16, body, 0)
+
     low = lane_id(channels) < 64
     low16 = lane_id(16) < 64
-    live = alive_lanes(step, near)
-    sums = []
-    for t in range(4):
-        cots = quad_cotangent(cot, t, low)
-        full = [
-            (cots[p] + conv[(2 * t + p) * 32 : (2 * t + p) * 32 + 32]) * live for p in range(2)
-        ]
-        from_pair(fine_grad, 0, full[0].astype(bf16), full[1].astype(bf16), t, low)
-        both = full[0] + full[1]
-        for pair in range(2):
-            v = both[:, pair * 128 : pair * 128 + 128]
-            v = v + roll(v, -1)
-            v = v + roll(v, -8)
-            sums.append(v.astype(bf16))
-    pooled = jnp.dot(
-        jnp.concatenate(sums, axis=1), pool[...], preferred_element_type=f32
-    ).astype(bf16)
-    for i in range(quad):
-        tile = pooled[:, (i // 2) * 128 : (i // 2) * 128 + 128]
-        if i % 2 == 0:
-            packed = jnp.where(low16, tile[:16], roll(tile[16:], 64))
-        else:
-            packed = jnp.where(low16, roll(tile[:16], 64), tile[16:])
-        target = child[step * quad + i]
-
-        @pl.when(target >= 0)
-        def _():
-            back[target] = packed
-
-
-def last_kernel(send, returned, totals, perm, coarse_grad, weight_grad, tab):
+
+    def process(index, slot):
+        conv = jnp.dot(weight[...], stacks[slot][...], preferred_element_type=f32)
+        live = alive_lanes(index, near)
+        sums = []
+        for t in range(4):
+            cots = quad_cotangent(cot, slot * quad, t, low)
+            full = [
+                (cots[p] + conv[(2 * t + p) * 32 : (2 * t + p) * 32 + 32]) * live
+                for p in range(2)
+            ]
+            from_pair(fine_grad, slot * quad, full[0].astype(bf16), full[1].astype(bf16), t, low)
+            both = full[0] + full[1]
+            for pair in range(2):
+                v = both[:, pair * 128 : pair * 128 + 128]
+                v = v + roll(v, -1)
+                v = v + roll(v, -8)
+                sums.append(v.astype(bf16))
+        pooled = jnp.dot(
+            jnp.concatenate(sums, axis=1), pool[...], preferred_element_type=f32
+        ).astype(bf16)
+        for i in range(quad):
+            tile = pooled[:, (i // 2) * 128 : (i // 2) * 128 + 128]
+            if i % 2 == 0:
+                packed = jnp.where(low16, tile[:16], roll(tile[16:], 64))
+            else:
+                packed = jnp.where(low16, roll(tile[:16], 64), tile[16:])
+            octants[index * quad + i] = packed
+
+    build(2 * step + 1, 1)
+    process(2 * step, 0)
+    build(jnp.minimum(2 * step + 2, steps - 1), 0)
+    process(2 * step + 1, 1)
+
+    @pl.when(step == steps // 2 - 1)
+    def _():
+        def body(i, carry):
+            for j in range(8):
+                target = child[i * 8 + j]
+
+                @pl.when(target >= 0)
+                def _():
+                    back[target, 0:16, :] = octants[i * 8 + j]
+
+            return carry
+
+        lax.fori_loop(0, capacity // 8, body, 0)
+
+
+def last_kernel(send, returned, perm, coarse_grad, weight_grad, tab, parts):
     low = lane_id(16) < 64
     tab[...] = jnp.zeros_like(tab)
 
@@ -407,7 +457,7 @@
 
             @pl.when(target >= 0)
             def _():
-                tab[target] = returned[d]
+                tab[target] = returned[d, 0:16, :]
 
         return carry
 
@@ -423,8 +473,14 @@
         rows.append(jnp.concatenate(bottoms, axis=1))
     spread = jnp.dot(jnp.concatenate(rows, axis=0), perm[...], preferred_element_type=f32)
     coarse_grad[...] = spread.astype(bf16).reshape(8, 32, 512)
-    for k in range(27):
-        weight_grad[k] = totals[k // 8, :, (k % 8) * 32 : (k % 8) * 32 + 32]
+    parts[...] = returned[:, 16:24, :].astype(f32)
+    for half in range(2):
+        total = parts[:, half, :] + parts[:, half + 2, :] + parts[:, half + 4, :]
+        for j in range(4):
+            for i in range(4):
+                k = j * 8 + half * 4 + i
+                if k < 27:
+                    weight_grad[k] = total[j * 32 : j * 32 + 32, i * 32 : i * 32 + 32]
 
 
 def shape(dims, kind=bf16):
@@ -507,6 +563,7 @@
     elow, ehigh = const(y_low.T), const(y_high.T)
     up = const(upsample_matrix())
     pool = const(pool_matrix())
+    shift = const(shift_matrix())
     packed = (16, 128)
     side = shape((side_n,) + packed)
     face = shape((face_n,) + packed)
@@ -539,72 +596,65 @@
     near_h = halo(xm, xp, ym, yp)
 
     bricks = whole((capacity, channels, 512))
-    sides = [whole((n,) + packed) for n in (side_n, side_n, side_n, side_n)]
-    per_quad = pl.BlockSpec((quad, channels, 512), lambda i: (i, 0, 0))
-    stack_spec = pl.BlockSpec((1, depth, 256), lambda i: (i, 0, 0))
-    pair_spec = pl.BlockSpec((1, 256, 256), lambda i: (i, 0, 0))
+    sides = [whole((side_n,) + packed)] * 4
+    per_step = pl.BlockSpec((2 * quad, channels, 512), lambda i: (i, 0, 0))
     table = pltpu.VMEM((table_rows, channels, 512), bf16)
-    block_out, grad, stacks, grad_pair, gxm, gxp, gym, gyp = pl.pallas_call(
+    wide = pltpu.VMEM((face_n * 16, 1024), bf16)
+    work = [
+        [pltpu.VMEM((1280, 256), bf16)] * 2,
+        [pltpu.VMEM((1280, 256), bf16)] * 2,
+        [pltpu.VMEM((depth, 256), bf16)] * 2,
+    ]
+    block_out, grad, term, gxm, gxp, gym, gyp = pl.pallas_call(
         forward_kernel,
-        grid=(steps,),
+        grid=(steps // 2,),
         out_shape=(
             shape((capacity, channels, 512)),
             shape((capacity, channels, 512)),
-            shape((steps, depth, 256)),
-            shape((steps, 256, 256)),
+            shape((4, 32, 256), f32),
             side, side, face, face,
         ),
         in_specs=[smem, smem, bricks]
         + sides
-        + [per_quad, whole((256, depth))]
+        + [per_step, whole((256, depth))]
         + [whole((128, 1024))] * 2
-        + [whole((1024, 128))] * 2,
-        out_specs=(per_quad, bricks, stack_spec, pair_spec)
+        + [whole((1024, 128))] * 2
+        + [whole((256, 256))],
+        out_specs=(per_step, bricks, whole((4, 32, 256)))
         + tuple(whole((n,) + packed) for n in (side_n, side_n, face_n, face_n)),
-        scratch_shapes=[table, pltpu.VMEM((face_n * 16, 1024), bf16)],
+        scratch_shapes=[table, wide]
+        + work
+        + [pltpu.VMEM((depth, 256), f32), pltpu.VMEM((1024, 128), f32)],
         compiler_params=params(),
         name="forward",
-    )(near, lists, hidden, *near_h, cotangent, taps, elow, ehigh, ylow, yhigh)
+    )(near, lists, hidden, *near_h, cotangent, taps, elow, ehigh, ylow, yhigh, shift)
     near_g = halo(gxm, gxp, gym, gyp)
-
-    term = pl.pallas_call(
-        weight_kernel,
-        grid=(steps,),
-        out_shape=shape((4, 32, 256), f32),
-        in_specs=[stack_spec, pair_spec],
-        out_specs=whole((4, 32, 256)),
-        scratch_shapes=[pltpu.VMEM((depth, 256), f32), pltpu.VMEM((1024, 128), f32)],
-        compiler_params=params(),
-        name="weight_term",
-    )(stacks, grad_pair)
-    terms = exchange(term.reshape(128, 256))
-    mine = jnp.sum(terms, axis=0)
-    totals = exchange(jnp.broadcast_to(mine[None, :], (devices, 256))).reshape(4, 32, 256)
+    terms = exchange(term.reshape(devices, 256))
 
     fine_grad, back = pl.pallas_call(
         backward_kernel,
-        grid=(steps,),
-        out_shape=(shape((capacity, channels, 512)), shape((devices,) + packed)),
+        grid=(steps // 2,),
+        out_shape=(shape((capacity, channels, 512)), shape((devices, 24, 128))),
         in_specs=[smem, smem, bricks]
         + sides
-        + [per_quad, whole((256, depth)), whole((128, 1024)), whole((128, 1024))]
-        + [whole((1024, 256))],
-        out_specs=(per_quad, whole((devices,) + packed)),
-        scratch_shapes=[[table, pltpu.VMEM((depth, 256), bf16)]],
+        + [per_step, whole((256, depth)), whole((128, 1024)), whole((128, 1024))]
+        + [whole((1024, 256)), whole((256, 256)), whole((devices, 256))],
+        out_specs=(per_step, whole((devices, 24, 128))),
+        scratch_shapes=[table] + work + [pltpu.VMEM((capacity,) + packed, bf16)],
         compiler_params=params(),
         name="backward",
-    )(near, child_src, grad, *near_g, cotangent, back_taps, elow, ehigh, pool)
+    )(near, child_src, grad, *near_g, cotangent, back_taps, elow, ehigh, pool, shift, terms)
     returned = exchange(back)
 
     coarse_grad, weight_grad = pl.pallas_call(
         last_kernel,
         out_shape=(shape((8, channels, 512)), shape((27, channels, channels), f32)),
-        in_specs=[smem, vmem, vmem, vmem],
+        in_specs=[smem, vmem, vmem],
         out_specs=(vmem, vmem),
-        scratch_shapes=[pltpu.VMEM((64,) + packed, bf16)],
+        scratch_shapes=[pltpu.VMEM((64,) + packed, bf16), pltpu.VMEM((devices, 8, 128), f32)],
         compiler_params=params(),
         name="coarse",
-    )(send, returned, totals, perm_t)
+    )(send, returned, perm_t)
     return block_out, fine_grad, coarse_grad, weight_grad
 
 

time: 237 us -> 191 us (0.81)
  Pallas kernels: 120 us -> 81.6 us
  blocking collectives: 0 us -> 25.7 us
  starting transfers between devices: 66.5 us -> 46.3 us
  waiting for transfers between devices: 29 us -> 15.9 us
    pallas_call x3 -> x2, Pallas kernels: 109 us -> 69.9 us  [the longest x1 35.1 us: on_device(): pl.pallas_call(forward_kernel, grid=(steps // 2,), out_shape=(shape((capa...]
    all_to_all x0 -> x1, blocking collectives: none -> 25.7 us  [exchange(): return lax.all_to_all(value, axes, split_axis=0, concat_axis=0, tiled=True)]
    all_to_all x4 -> x2, starting transfers between devices: 45 us -> 21.6 us  [exchange(): return lax.all_to_all(value, axes, split_axis=0, concat_axis=0, tiled=True)]
    all_to_all x4 -> x2, waiting for transfers between devices: 19.2 us -> 6.33 us  [exchange(): return lax.all_to_all(value, axes, split_axis=0, concat_axis=0, tiled=True)]
    ppermute x8, starting transfers between devices: 21.5 us -> 24.7 us  [moved(): return lax.ppermute(value, axes, pairs)]
    unnamed x49 -> x41, local copies, waits for them, and re-layouts: 9.47 us -> 8.59 us
  transfers between devices with their start and end apart: 12 -> 10, of which waited for: 5 -> 6; matrix products, arithmetic and copies ran while one was open for 7% -> 9% of each run, Pallas kernels for 27% -> 0%
where the time goes in v2:
time: 191 us; the launch traced here: 190 us
  Pallas kernels  81.6 us (43%)
  starting transfers between devices  46.3 us (24%)
  blocking collectives  25.7 us (13%)
  waiting for transfers between devices  15.9 us (8%)
  local copies, waits for them, and re-layouts  13.2 us (7%)
  other arithmetic  5.91 us (3%)
    pallas_call x1, Pallas kernels, on_device(): pl.pallas_call(forward_kernel, grid=(steps // 2,), out_shape=(shape((capa...  35.1 us
    pallas_call x1, Pallas kernels, on_device(): pl.pallas_call(backward_kernel, grid=(steps // 2,), out_shape=(shape((cap...  34.7 us
    all_to_all x1, blocking collectives, exchange(): return lax.all_to_all(value, axes, split_axis=0, concat_axis=0, tiled=True)  25.7 us
    ppermute x8, starting transfers between devices, moved(): return lax.ppermute(value, axes, pairs)  24.7 us
    all_to_all x2, starting transfers between devices, exchange(): return lax.all_to_all(value, axes, split_axis=0, concat_axis=0, tiled=True)  21.6 us
    ppermute x8, waiting for transfers between devices, moved(): return lax.ppermute(value, axes, pairs)  9.53 us
    unnamed x41, local copies, waits for them, and re-layouts  8.59 us
    all_to_all x2, waiting for transfers between devices, exchange(): return lax.all_to_all(value, axes, split_axis=0, concat_axis=0, tiled=True)  6.33 us
  transfers between devices with their start and end apart: 10, of which 6 were waited for; matrix products, arithmetic and copies ran while one was open for 9% of the time, Pallas kernels for 0%

profile of v2, /device:TPU:1, one launch (start us, length us, event | category | flops | bytes accessed | tf_op | source)
XLA Modules:
  0.0 189.9 jit_solution(10568495450626837891)
XLA Ops:
  0.7 2.6 %octants.1 = bf16[128,16,128]{2,1,0:T(8,128)(2,1)} custom-call(s32[128]{0:T(128)} %bitcast.33, bf16[8,32,512]{2,1,0:T(8,128)(2,1)} %coarse.2, bf16[512,512]{1,0:T(8,128)(2,1)} %constant.72.clone.perm), custom_call_target="tpu_custom_call" | custom-call | tf_op jit(solution)/shard_map/octants/pallas_call | solution.py:571
  3.3 11.5 %all-to-all-start = ((bf16[128,16,128]{2,1,0:T(8,128)(2,1)}), bf16[128,16,128]{2,1,0:T(8,128)(2,1)S(1)}, u32[]{:S(2)}, u32[]{:S(2)}) async-start(bf16[128,16,128]{2,1,0:T(8,128)(2,1)} %octants.1), calls=%async_computation | async-start | bytes 1048576 | tf_op jit(solution)/shard_map/all_to_all | solution.py:549
  15.6 1.0 select_reduce_fusion
  18.2 0.8 pad_dynamic-update-slice_fusion.7
  21.8 0.8 pad_dynamic-update-slice_fusion.4
  22.5 6.1 %all-to-all-done.incoming = bf16[128,16,128]{2,1,0:T(8,128)(2,1)S(1)} async-done(((bf16[128,16,128]{2,1,0:T(8,128)(2,1)}), bf16[128,16,128]{2,1,0:T(8,128)(2,1)S(1)}, u32[]{:S(2)}, u32[]{:S(2)}) %all-to-all-start) | async-done | bytes 524320 | tf_op jit(solution)/shard_map/all_to_all | solution.py:549
  28.6 0.8 copy-done
  29.4 5.4 %hidden.1 = (bf16[64,32,512]{2,1,0:T(8,128)(2,1)}, bf16[24,16,128]{2,1,0:T(8,128)(2,1)}, bf16[24,16,128]{2,1,0:T(8,128)(2,1)}, bf16[16,16,128]{2,1,0:T(8,128)(2,1)}, bf16[16,16,128]{2,1,0:T(8,128)(2,1)}) custom-call(s32[64]{0:T(128)} %child.3, s32[64]{0:T(128)} %fusion.16.alive, s32[80]{0:T(128)} %concatenate.21.lists, bf16[128,16,128]{2,1,0:T(8,128)(2,1)} %copy-done, ...), custom_call_target="tpu_custom_call" | custom-call | tf_op jit(solution)/shard_map/hidden/pallas_call | solution.py:587
  34.8 1.3 collective-permute-start.1
  36.8 4.0 %collective-permute-start = (bf16[24,16,128]{2,1,0:T(8,128)(2,1)}, bf16[24,16,128]{2,1,0:T(8,128)(2,1)S(1)}, u32[]{:S(2)}, u32[]{:S(2)}) collective-permute-start(bf16[24,16,128]{2,1,0:T(8,128)(2,1)} %get-tuple-element.21), channel_id=1, source_target_pairs={{0,16},{1,17},{2,18},{3,19},{4,20},{5,21},{6,22},{7,23},{8,24},{9,... | collective-permute-start | bytes 294920 | tf_op jit(solution)/shard_map/ppermute | solution.py:534
  40.9 1.8 collective-permute-done.rxm
  42.7 0.9 pad_maximum_fusion
  43.6 4.6 %collective-permute-start.2 = (bf16[24,16,128]{2,1,0:T(8,128)(2,1)S(1)}, bf16[24,16,128]{2,1,0:T(8,128)(2,1)S(1)}, u32[]{:S(2)}, u32[]{:S(2)}) collective-permute-start(bf16[24,16,128]{2,1,0:T(8,128)(2,1)S(1)} %pad_maximum_fusion), channel_id=1, source_target_pairs={{0,1},{1,2},{2,3},{3,4},{4,5},{5,6},{6,7},{7,8},{8,9},{9,10},{10,1... | collective-permute-start | bytes 294920 | tf_op jit(solution)/shard_map/ppermute | solution.py:534
  48.2 0.9 pad_maximum_fusion.1
  49.1 1.9 %collective-permute-start.3 = (bf16[24,16,128]{2,1,0:T(8,128)(2,1)S(1)}, bf16[24,16,128]{2,1,0:T(8,128)(2,1)S(1)}, u32[]{:S(2)}, u32[]{:S(2)}) collective-permute-start(bf16[24,16,128]{2,1,0:T(8,128)(2,1)S(1)} %pad_maximum_fusion.1), channel_id=1, source_target_pairs={{1,0},{2,1},{3,2},{4,3},{5,4},{6,5},{7,6},{8,7},{9,8},{10,9},{11,1... | collective-permute-start | bytes 294920 | tf_op jit(solution)/shard_map/ppermute | solution.py:534
  51.0 0.8 pad_dynamic-update-slice_fusion.2
  52.6 3.9 %collective-permute-done.3.ryp = bf16[24,16,128]{2,1,0:T(8,128)(2,1)S(1)} collective-permute-done((bf16[24,16,128]{2,1,0:T(8,128)(2,1)S(1)}, bf16[24,16,128]{2,1,0:T(8,128)(2,1)S(1)}, u32[]{:S(2)}, u32[]{:S(2)}) %collective-permute-start.3) | collective-permute-done | bytes 98336 | tf_op jit(solution)/shard_map/ppermute | solution.py:534
  57.2 35.1 %forward.1 = (bf16[64,32,512]{2,1,0:T(8,128)(2,1)}, bf16[64,32,512]{2,1,0:T(8,128)(2,1)}, f32[4,32,256]{2,1,0:T(8,128)}, bf16[24,16,128]{2,1,0:T(8,128)(2,1)}, b...) custom-call(s32[1728]{0:T(1024)} %reshape.40.near, s32[80]{0:T(128)} %concatenate.21.lists, ...), custom_call_target="tpu_custom_call" | custom-call | tf_op jit(solution)/shard_map/forward/pallas_call | solution.py:608
  92.3 1.3 collective-permute-start.5
  93.6 0.8 pad_dynamic-update-slice_fusion.1
  94.4 4.5 %collective-permute-start.4 = (bf16[24,16,128]{2,1,0:T(8,128)(2,1)}, bf16[24,16,128]{2,1,0:T(8,128)(2,1)S(1)}, u32[]{:S(2)}, u32[]{:S(2)}) collective-permute-start(bf16[24,16,128]{2,1,0:T(8,128)(2,1)} %get-tuple-element.27), channel_id=1, source_target_pairs={{0,16},{1,17},{2,18},{3,19},{4,20},{5,21},{6,22},{7,23},{8,24},{9,... | collective-permute-start | bytes 294920 | tf_op jit(solution)/shard_map/ppermute | solution.py:534
  98.9 1.7 copy.39
  100.6 10.1 %all-to-all-start.1 = ((f32[128,1,256]{2,1,0:T(1,128)}), f32[128,1,256]{2,1,0:T(1,128)S(1)}, u32[]{:S(2)}, u32[]{:S(2)}) async-start(f32[128,1,256]{2,1,0:T(1,128)} %copy.39), calls=%async_computation.1 | async-start | bytes 262144 | tf_op jit(solution)/shard_map/all_to_all | solution.py:549
  110.8 0.9 pad_maximum_fusion.2
  111.7 5.0 %collective-permute-start.6 = (bf16[24,16,128]{2,1,0:T(8,128)(2,1)S(1)}, bf16[24,16,128]{2,1,0:T(8,128)(2,1)S(1)}, u32[]{:S(2)}, u32[]{:S(2)}) collective-permute-start(bf16[24,16,128]{2,1,0:T(8,128)(2,1)S(1)} %pad_maximum_fusion.2), channel_id=1, source_target_pairs={{0,1},{1,2},{2,3},{3,4},{4,5},{5,6},{6,7},{7,8},{8,9},{9,10},{10,1... | collective-permute-start | bytes 294920 | tf_op jit(solution)/shard_map/ppermute | solution.py:534
  116.8 0.9 pad_maximum_fusion.3
  117.6 2.1 %collective-permute-start.7 = (bf16[24,16,128]{2,1,0:T(8,128)(2,1)S(1)}, bf16[24,16,128]{2,1,0:T(8,128)(2,1)S(1)}, u32[]{:S(2)}, u32[]{:S(2)}) collective-permute-start(bf16[24,16,128]{2,1,0:T(8,128)(2,1)S(1)} %pad_maximum_fusion.3), channel_id=1, source_target_pairs={{1,0},{2,1},{3,2},{4,3},{5,4},{6,5},{7,6},{8,7},{9,8},{10,9},{11,1... | collective-permute-start | bytes 294920 | tf_op jit(solution)/shard_map/ppermute | solution.py:534
  119.7 0.8 pad_dynamic-update-slice_fusion.weight
  121.4 3.7 %collective-permute-done.7.ryp = bf16[24,16,128]{2,1,0:T(8,128)(2,1)S(1)} collective-permute-done((bf16[24,16,128]{2,1,0:T(8,128)(2,1)S(1)}, bf16[24,16,128]{2,1,0:T(8,128)(2,1)S(1)}, u32[]{:S(2)}, u32[]{:S(2)}) %collective-permute-start.7) | collective-permute-done | bytes 98336 | tf_op jit(solution)/shard_map/ppermute | solution.py:534
  125.7 34.7 %backward.1 = (bf16[64,32,512]{2,1,0:T(8,128)(2,1)}, bf16[128,24,128]{2,1,0:T(8,128)(2,1)}) custom-call(s32[1728]{0:T(1024)} %reshape.40.near, s32[64]{0:T(128)} %child.3, bf16[64,32,512]{2,1,0:T(8,128)(2,1)} %get-tuple-element.26.grad, bf16[24,16,128]{2,1,0:T(8,128)(2,1)} %copy-done.5, bf16[24,16,128]{2,1,0:T(8,128)(2,1)} %copy-done.3, ...), custom_call_target="tpu_custom_call" | custom-call | tf_op jit(solution)/shard_map/backward/pallas_call | solution.py:634
  160.4 25.7 %all_to_all.21.returned = bf16[128,24,128]{2,1,0:T(8,128)(2,1)} all-to-all(bf16[128,24,128]{2,1,0:T(8,128)(2,1)} %get-tuple-element.33), channel_id=1, replica_groups=mesh['gx'=8,'gy'=16] {'gx','gy'}, dimensions={0} | all-to-all | bytes 1572864 | tf_op jit(solution)/shard_map/all_to_all | solution.py:549
  186.2 3.7 %coarse.3 = (bf16[8,32,512]{2,1,0:T(8,128)(2,1)}, f32[27,32,32]{2,1,0:T(8,128)}) custom-call(s32[128]{0:T(128)} %bitcast.34, bf16[128,24,128]{2,1,0:T(8,128)(2,1)} %all_to_all.21.returned, bf16[512,512]{1,0:T(8,128)(2,1)} %constant.73.clone.perm), custom_call_target="tpu_custom_call" | custom-call | tf_op jit(solution)/shard_map/coarse/pallas_call | solution.py:649
  (66 shorter events, 8.9 us)
Async XLA Ops:
  0.6 14.8 %copy-start.12 = (s32[9,64]{1,0:T(8,128)S(1)}, s32[9,64]{1,0:T(8,128)}, u32[]{:S(2)}) copy-start(s32[9,64]{1,0:T(8,128)} %constant.119) | copy-start | bytes 6916
  0.6 14.1 %copy-start.7 = (s32[64,27]{0,1:T(8,128)S(1)}, s32[64,27]{0,1:T(8,128)}, u32[]{:S(2)}) copy-start(s32[64,27]{0,1:T(8,128)} %param.21) | copy-start | bytes 20740
  0.7 16.5 %copy-start.2 = (bf16[27,32,32]{2,1,0:T(8,128)(2,1)S(1)}, bf16[27,32,32]{2,1,0:T(8,128)(2,1)}, u32[]{:S(2)}) copy-start(bf16[27,32,32]{2,1,0:T(8,128)(2,1)} %param.19) | copy-start | bytes 165892
  3.3 25.4 %all-to-all-start = ((bf16[128,16,128]{2,1,0:T(8,128)(2,1)}), bf16[128,16,128]{2,1,0:T(8,128)(2,1)S(1)}, u32[]{:S(2)}, u32[]{:S(2)}) async-start(bf16[128,16,128]{2,1,0:T(8,128)(2,1)} %octants.1), calls=%async_computation | async-start | bytes 1048576 | tf_op jit(solution)/shard_map/all_to_all | solution.py:549
  18.1 38.4 %copy-start.1 = (bf16[256,2880]{1,0:T(8,128)(2,1)}, bf16[256,2880]{1,0:T(8,128)(2,1)S(1)}, u32[]{:S(2)}) copy-start(bf16[256,2880]{1,0:T(8,128)(2,1)S(1)} %pad_dynamic-update-slice_fusion.8.weight) | copy-start | bytes 4423684
  28.6 0.8 copy-start
  34.8 6.1 %collective-permute-start.1 = (bf16[24,16,128]{2,1,0:T(8,128)(2,1)}, bf16[24,16,128]{2,1,0:T(8,128)(2,1)S(1)}, u32[]{:S(2)}, u32[]{:S(2)}) collective-permute-start(bf16[24,16,128]{2,1,0:T(8,128)(2,1)} %get-tuple-element.22), channel_id=1, source_target_pairs={{16,0},{17,1},{18,2},{19,3},{20,4},{21,5},{22,6},{23,7},{24,8},{25... | collective-permute-start | bytes 294920 | tf_op jit(solution)/shard_map/ppermute | solution.py:534
  36.8 5.9 %collective-permute-start = (bf16[24,16,128]{2,1,0:T(8,128)(2,1)}, bf16[24,16,128]{2,1,0:T(8,128)(2,1)S(1)}, u32[]{:S(2)}, u32[]{:S(2)}) collective-permute-start(bf16[24,16,128]{2,1,0:T(8,128)(2,1)} %get-tuple-element.21), channel_id=1, source_target_pairs={{0,16},{1,17},{2,18},{3,19},{4,20},{5,21},{6,22},{7,23},{8,24},{9,... | collective-permute-start | bytes 294920 | tf_op jit(solution)/shard_map/ppermute | solution.py:534
  40.9 15.6 %copy-start.4 = (bf16[24,16,128]{2,1,0:T(8,128)(2,1)}, bf16[24,16,128]{2,1,0:T(8,128)(2,1)S(1)}, u32[]{:S(2)}) copy-start(bf16[24,16,128]{2,1,0:T(8,128)(2,1)S(1)} %collective-permute-done.1.rxp) | copy-start | bytes 294916
  42.7 13.8 %copy-start.6 = (bf16[24,16,128]{2,1,0:T(8,128)(2,1)}, bf16[24,16,128]{2,1,0:T(8,128)(2,1)S(1)}, u32[]{:S(2)}) copy-start(bf16[24,16,128]{2,1,0:T(8,128)(2,1)S(1)} %collective-permute-done.rxm) | copy-start | bytes 294916
  43.6 9.0 %collective-permute-start.2 = (bf16[24,16,128]{2,1,0:T(8,128)(2,1)S(1)}, bf16[24,16,128]{2,1,0:T(8,128)(2,1)S(1)}, u32[]{:S(2)}, u32[]{:S(2)}) collective-permute-start(bf16[24,16,128]{2,1,0:T(8,128)(2,1)S(1)} %pad_maximum_fusion), channel_id=1, source_target_pairs={{0,1},{1,2},{2,3},{3,4},{4,5},{5,6},{6,7},{7,8},{8,9},{9,10},{10,1... | collective-permute-start | bytes 294920 | tf_op jit(solution)/shard_map/ppermute | solution.py:534
  49.1 7.4 %collective-permute-start.3 = (bf16[24,16,128]{2,1,0:T(8,128)(2,1)S(1)}, bf16[24,16,128]{2,1,0:T(8,128)(2,1)S(1)}, u32[]{:S(2)}, u32[]{:S(2)}) collective-permute-start(bf16[24,16,128]{2,1,0:T(8,128)(2,1)S(1)} %pad_maximum_fusion.1), channel_id=1, source_target_pairs={{1,0},{2,1},{3,2},{4,3},{5,4},{6,5},{7,6},{8,7},{9,8},{10,9},{11,1... | collective-permute-start | bytes 294920 | tf_op jit(solution)/shard_map/ppermute | solution.py:534
  52.6 3.9 %copy-start.8 = (bf16[24,16,128]{2,1,0:T(8,128)(2,1)}, bf16[24,16,128]{2,1,0:T(8,128)(2,1)S(1)}, u32[]{:S(2)}) copy-start(bf16[24,16,128]{2,1,0:T(8,128)(2,1)S(1)} %collective-permute-done.2.rym) | copy-start | bytes 294916
  56.5 0.7 copy-start.10
  92.3 18.4 %collective-permute-start.5 = (bf16[24,16,128]{2,1,0:T(8,128)(2,1)}, bf16[24,16,128]{2,1,0:T(8,128)(2,1)S(1)}, u32[]{:S(2)}, u32[]{:S(2)}) collective-permute-start(bf16[24,16,128]{2,1,0:T(8,128)(2,1)} %get-tuple-element.28), channel_id=1, source_target_pairs={{16,0},{17,1},{18,2},{19,3},{20,4},{21,5},{22,6},{23,7},{24,8},{25... | collective-permute-start | bytes 294920 | tf_op jit(solution)/shard_map/ppermute | solution.py:534
  94.4 16.4 %collective-permute-start.4 = (bf16[24,16,128]{2,1,0:T(8,128)(2,1)}, bf16[24,16,128]{2,1,0:T(8,128)(2,1)S(1)}, u32[]{:S(2)}, u32[]{:S(2)}) collective-permute-start(bf16[24,16,128]{2,1,0:T(8,128)(2,1)} %get-tuple-element.27), channel_id=1, source_target_pairs={{0,16},{1,17},{2,18},{3,19},{4,20},{5,21},{6,22},{7,23},{8,24},{9,... | collective-permute-start | bytes 294920 | tf_op jit(solution)/shard_map/ppermute | solution.py:534
  100.6 20.1 %all-to-all-start.1 = ((f32[128,1,256]{2,1,0:T(1,128)}), f32[128,1,256]{2,1,0:T(1,128)S(1)}, u32[]{:S(2)}, u32[]{:S(2)}) async-start(f32[128,1,256]{2,1,0:T(1,128)} %copy.39), calls=%async_computation.1 | async-start | bytes 262144 | tf_op jit(solution)/shard_map/all_to_all | solution.py:549
  110.8 14.3 %copy-start.3 = (bf16[24,16,128]{2,1,0:T(8,128)(2,1)}, bf16[24,16,128]{2,1,0:T(8,128)(2,1)S(1)}, u32[]{:S(2)}) copy-start(bf16[24,16,128]{2,1,0:T(8,128)(2,1)S(1)} %collective-permute-done.5.rxp) | copy-start | bytes 294916
  110.8 14.3 %copy-start.5 = (bf16[24,16,128]{2,1,0:T(8,128)(2,1)}, bf16[24,16,128]{2,1,0:T(8,128)(2,1)S(1)}, u32[]{:S(2)}) copy-start(bf16[24,16,128]{2,1,0:T(8,128)(2,1)S(1)} %collective-permute-done.4.rxm) | copy-start | bytes 294916
  111.7 9.7 %collective-permute-start.6 = (bf16[24,16,128]{2,1,0:T(8,128)(2,1)S(1)}, bf16[24,16,128]{2,1,0:T(8,128)(2,1)S(1)}, u32[]{:S(2)}, u32[]{:S(2)}) collective-permute-start(bf16[24,16,128]{2,1,0:T(8,128)(2,1)S(1)} %pad_maximum_fusion.2), channel_id=1, source_target_pairs={{0,1},{1,2},{2,3},{3,4},{4,5},{5,6},{6,7},{7,8},{8,9},{9,10},{10,1... | collective-permute-start | bytes 294920 | tf_op jit(solution)/shard_map/ppermute | solution.py:534
  117.6 7.4 %collective-permute-start.7 = (bf16[24,16,128]{2,1,0:T(8,128)(2,1)S(1)}, bf16[24,16,128]{2,1,0:T(8,128)(2,1)S(1)}, u32[]{:S(2)}, u32[]{:S(2)}) collective-permute-start(bf16[24,16,128]{2,1,0:T(8,128)(2,1)S(1)} %pad_maximum_fusion.3), channel_id=1, source_target_pairs={{1,0},{2,1},{3,2},{4,3},{5,4},{6,5},{7,6},{8,7},{9,8},{10,9},{11,1... | collective-permute-start | bytes 294920 | tf_op jit(solution)/shard_map/ppermute | solution.py:534
  121.4 3.7 %copy-start.9 = (bf16[24,16,128]{2,1,0:T(8,128)(2,1)}, bf16[24,16,128]{2,1,0:T(8,128)(2,1)S(1)}, u32[]{:S(2)}) copy-start(bf16[24,16,128]{2,1,0:T(8,128)(2,1)S(1)} %collective-permute-done.6.rym) | copy-start | bytes 294916
  125.0 0.6 copy-start.11

commit v3 on v2

--- a/solution.py
+++ b/solution.py
@@ -135,25 +135,27 @@
 
 
 def hidden_kernel(
-    child, alive, lists, incoming, fine, up, ylow, yhigh, hidden, xm, xp, ym, yp, wide
+    child, alive, lists, incoming, fine, up, ylow, yhigh, hidden, xm, xp, ym, yp, wide, full
 ):
-    def body(i, carry):
-        rows = []
-        for j in range(8):
-            rows.append(incoming[jnp.maximum(child[i * 8 + j], 0)])
-        big = jnp.dot(jnp.concatenate(rows, axis=0), up[...], preferred_element_type=f32)
-        for j in range(8):
-            s = i * 8 + j
-            live = alive[s] > 0
-            for h in range(2):
-                total = fine[s, h * 16 : h * 16 + 16, :].astype(f32) + big[
-                    j * 16 : j * 16 + 16, h * 512 : h * 512 + 512
-                ]
-                hidden[s, h * 16 : h * 16 + 16, :] = jnp.where(live, total, 0.0).astype(bf16)
-        return carry
-
-    lax.fori_loop(0, 8, body, 0)
-    emit_faces(lists, hidden, ylow, yhigh, xm, xp, ym, yp, wide)
+    step = pl.program_id(0)
+    rows = []
+    for j in range(16):
+        rows.append(incoming[jnp.maximum(child[step * 16 + j], 0)])
+    big = jnp.dot(jnp.concatenate(rows, axis=0), up[...], preferred_element_type=f32)
+    for j in range(16):
+        s = step * 16 + j
+        live = (alive[s] > 0).astype(f32)
+        for h in range(2):
+            total = fine[j, h * 16 : h * 16 + 16, :].astype(f32) + big[
+                j * 16 : j * 16 + 16, h * 512 : h * 512 + 512
+            ]
+            value = (total * live).astype(bf16)
+            hidden[j, h * 16 : h * 16 + 16, :] = value
+            full[s, h * 16 : h * 16 + 16, :] = value
+
+    @pl.when(step == pl.num_programs(0) - 1)
+    def _():
+        emit_faces(lists, full, ylow, yhigh, xm, xp, ym, yp, wide)
 
 
 def fill_table(table, own, rxm, rxp, rym, ryp, elow, ehigh):
@@ -264,6 +266,12 @@
                     stack[row : row + channels, pair * 128 : pair * 128 + 128] = trio[j]
 
 
+def banded(taps, weight):
+    weight[...] = jnp.zeros_like(weight)
+    for x in range(8):
+        weight[x * 32 : x * 32 + 32, x * band : x * band + 3 * band] = taps[...]
+
+
 def alive_lanes(step, near):
     lane = lax.broadcasted_iota(jnp.int32, (1, 256), 1)
     out = jnp.zeros((1, 256), f32)
@@ -300,9 +308,9 @@
 
 
 def forward_kernel(
-    near, lists, hidden, rxm, rxp, rym, ryp, cot, weight, elow, ehigh, ylow, yhigh, shift,
+    near, lists, hidden, rxm, rxp, rym, ryp, cot, taps, elow, ehigh, ylow, yhigh, shift,
     block_out, grad, term, xm, xp, ym, yp,
-    table, wide, kinds, turned, stacks, total, term_wide,
+    table, weight, wide, kinds, turned, stacks, total, term_wide,
 ):
     step = pl.program_id(0)
 
@@ -311,6 +319,7 @@
 
     @pl.when(step == 0)
     def _():
+        banded(taps, weight)
         fill_table(table, hidden, rxm, rxp, rym, ryp, elow, ehigh)
         total[...] = jnp.zeros_like(total)
         build(0, 0)
@@ -364,9 +373,9 @@
 
 
 def backward_kernel(
-    near, child, grad, rxm, rxp, rym, ryp, cot, weight, elow, ehigh, pool, shift, terms,
+    near, child, grad, rxm, rxp, rym, ryp, cot, taps, elow, ehigh, pool, shift, terms,
     fine_grad, back,
-    table, kinds, turned, stacks, octants,
+    table, weight, kinds, turned, stacks, octants,
 ):
     step = pl.program_id(0)
 
@@ -375,6 +384,7 @@
 
     @pl.when(step == 0)
     def _():
+        banded(taps, weight)
         fill_table(table, grad, rxm, rxp, rym, ryp, elow, ehigh)
         build(0, 0)
         rest = jnp.sum(terms[...], axis=0, keepdims=True)
@@ -415,16 +425,9 @@
                 v = v + roll(v, -1)
                 v = v + roll(v, -8)
                 sums.append(v.astype(bf16))
-        pooled = jnp.dot(
-            jnp.concatenate(sums, axis=1), pool[...], preferred_element_type=f32
-        ).astype(bf16)
-        for i in range(quad):
-            tile = pooled[:, (i // 2) * 128 : (i // 2) * 128 + 128]
-            if i % 2 == 0:
-                packed = jnp.where(low16, tile[:16], roll(tile[16:], 64))
-            else:
-                packed = jnp.where(low16, roll(tile[:16], 64), tile[16:])
-            octants[index * quad + i] = packed
+        rows = pl.ds(pl.multiple_of(index * channels, channels), channels)
+        for i in range(8):
+            octants[rows, i * 128 : i * 128 + 128] = sums[i]
 
     build(2 * step + 1, 1)
     process(2 * step, 0)
@@ -433,17 +436,16 @@
 
     @pl.when(step == steps // 2 - 1)
     def _():
-        def body(i, carry):
-            for j in range(8):
-                target = child[i * 8 + j]
-
-                @pl.when(target >= 0)
-                def _():
-                    back[target, 0:16, :] = octants[i * 8 + j]
-
-            return carry
-
-        lax.fori_loop(0, capacity // 8, body, 0)
+        pooled = jnp.dot(octants[...], pool[...], preferred_element_type=f32).astype(bf16)
+        for s in range(capacity):
+            row = s // quad * channels
+            at_lane = (s % quad) // 2 * 128
+            tile = pooled[row : row + channels, at_lane : at_lane + 128]
+            if s % 2 == 0:
+                packed = jnp.where(low16, tile[:16], roll(tile[16:], 64))
+            else:
+                packed = jnp.where(low16, roll(tile[:16], 64), tile[16:])
+            back[child[s], 0:16, :] = packed
 
 
 def last_kernel(send, returned, perm, coarse_grad, weight_grad, tab, parts):
@@ -517,12 +519,6 @@
     return near.reshape(-1).astype(jnp.int32), lists.astype(jnp.int32)
 
 
-def banded(taps):
-    return jnp.concatenate(
-        [jnp.pad(taps, ((0, 0), (x * band, (7 - x) * band))) for x in range(8)], axis=0
-    )
-
-
 def moved(value, shift_x, shift_y):
     count_x, count_y = lax.axis_size("gx"), lax.axis_size("gy")
     pairs = [
@@ -581,15 +577,25 @@
 
     near, lists = indices(adjacency)
     alive = (adjacency[:, 13] >= 0).astype(jnp.int32)
-    taps = banded(weight.transpose(1, 0, 2).reshape(channels, 27 * channels))
-    back_taps = banded(weight[::-1].transpose(2, 0, 1).reshape(channels, 27 * channels))
-
+    sender = jnp.arange(devices, dtype=jnp.int32)
+    unused = jnp.where((child_src[:, None] == sender).any(axis=0), devices, sender).min()
+    back_to = jnp.where(child_src < 0, unused, child_src)
+    taps = weight.transpose(1, 0, 2).reshape(channels, 27 * channels)
+    back_taps = weight[::-1].transpose(2, 0, 1).reshape(channels, 27 * channels)
+
+    part = pl.BlockSpec((16, channels, 512), lambda i: (i, 0, 0))
     hidden, xm, xp, ym, yp = pl.pallas_call(
         hidden_kernel,
+        grid=(capacity // 16,),
         out_shape=(shape((capacity, channels, 512)), side, side, face, face),
-        in_specs=[smem, smem, smem] + [vmem] * 5,
-        out_specs=(vmem,) * 5,
-        scratch_shapes=[pltpu.VMEM((face_n * 16, 1024), bf16)],
+        in_specs=[smem, smem, smem, whole((devices,) + packed), part]
+        + [whole((128, 1024))]
+        + [whole((1024, 128))] * 2,
+        out_specs=(part,) + tuple(whole((n,) + packed) for n in (side_n, side_n, face_n, face_n)),
+        scratch_shapes=[
+            pltpu.VMEM((face_n * 16, 1024), bf16),
+            pltpu.VMEM((capacity, channels, 512), bf16),
+        ],
         compiler_params=params(),
         name="hidden",
     )(child_src, alive, lists, incoming, fine, up, ylow, yhigh)
@@ -600,6 +606,7 @@
     per_step = pl.BlockSpec((2 * quad, channels, 512), lambda i: (i, 0, 0))
     table = pltpu.VMEM((table_rows, channels, 512), bf16)
     wide = pltpu.VMEM((face_n * 16, 1024), bf16)
+    banded_weight = pltpu.VMEM((256, depth), bf16)
     work = [
         [pltpu.VMEM((1280, 256), bf16)] * 2,
         [pltpu.VMEM((1280, 256), bf16)] * 2,
@@ -616,13 +623,13 @@
         ),
         in_specs=[smem, smem, bricks]
         + sides
-        + [per_step, whole((256, depth))]
+        + [per_step, whole((channels, 27 * channels))]
         + [whole((128, 1024))] * 2
         + [whole((1024, 128))] * 2
         + [whole((256, 256))],
         out_specs=(per_step, bricks, whole((4, 32, 256)))
         + tuple(whole((n,) + packed) for n in (side_n, side_n, face_n, face_n)),
-        scratch_shapes=[table, wide]
+        scratch_shapes=[table, banded_weight, wide]
         + work
         + [pltpu.VMEM((depth, 256), f32), pltpu.VMEM((1024, 128), f32)],
         compiler_params=params(),
@@ -637,13 +644,13 @@
         out_shape=(shape((capacity, channels, 512)), shape((devices, 24, 128))),
         in_specs=[smem, smem, bricks]
         + sides
-        + [per_step, whole((256, depth)), whole((128, 1024)), whole((128, 1024))]
+        + [per_step, whole((channels, 27 * channels)), whole((128, 1024)), whole((128, 1024))]
         + [whole((1024, 256)), whole((256, 256)), whole((devices, 256))],
         out_specs=(per_step, whole((devices, 24, 128))),
-        scratch_shapes=[table] + work + [pltpu.VMEM((capacity,) + packed, bf16)],
+        scratch_shapes=[table, banded_weight] + work + [pltpu.VMEM((steps * channels, 1024), bf16)],
         compiler_params=params(),
         name="backward",
-    )(near, child_src, grad, *near_g, cotangent, back_taps, elow, ehigh, pool, shift, terms)
+    )(near, back_to, grad, *near_g, cotangent, back_taps, elow, ehigh, pool, shift, terms)
     returned = exchange(back)
 
     coarse_grad, weight_grad = pl.pallas_call(

time: 191 us -> 180 us (0.942)
  Pallas kernels: 81.6 us -> 70.5 us
  waiting for transfers between devices: 15.9 us -> 23.3 us
  local copies, waits for them, and re-layouts: 13.2 us -> 7.87 us
  starting transfers between devices: 46.3 us -> 42.8 us
    pallas_call x1, Pallas kernels: 34.7 us -> 24.8 us  [on_device(): pl.pallas_call(backward_kernel, grid=(steps // 2,), out_shape=(shape((cap...]
    unnamed x41 -> x27, local copies, waits for them, and re-layouts: 8.59 us -> 2.75 us
    ppermute x8, starting transfers between devices: 24.7 us -> 20.4 us  [moved(): return lax.ppermute(value, axes, pairs)]
    all_to_all x2, waiting for transfers between devices: 6.33 us -> 10.3 us  [exchange(): return lax.all_to_all(value, axes, split_axis=0, concat_axis=0, tiled=True)]
    ppermute x8, waiting for transfers between devices: 9.53 us -> 13 us  [moved(): return lax.ppermute(value, axes, pairs)]
  transfers between devices with their start and end apart: 10 -> 10, of which waited for: 6 -> 4; matrix products, arithmetic and copies ran while one was open for 9% -> 7% of each run, Pallas kernels for 0% -> 0%
where the time goes in v3:
time: 180 us; the launch traced here: 179 us
  Pallas kernels  70.5 us (39%)
  starting transfers between devices  42.8 us (24%)
  blocking collectives  25.7 us (14%)
  waiting for transfers between devices  23.3 us (13%)
  local copies, waits for them, and re-layouts  7.87 us (4%)
  other arithmetic  7.71 us (4%)
    pallas_call x1, Pallas kernels, on_device(): pl.pallas_call(forward_kernel, grid=(steps // 2,), out_shape=(shape((capa...  34.1 us
    all_to_all x1, blocking collectives, exchange(): return lax.all_to_all(value, axes, split_axis=0, concat_axis=0, tiled=True)  25.7 us
    pallas_call x1, Pallas kernels, on_device(): pl.pallas_call(backward_kernel, grid=(steps // 2,), out_shape=(shape((cap...  24.8 us
    all_to_all x2, starting transfers between devices, exchange(): return lax.all_to_all(value, axes, split_axis=0, concat_axis=0, tiled=True)  22.4 us
    ppermute x8, starting transfers between devices, moved(): return lax.ppermute(value, axes, pairs)  20.4 us
    ppermute x8, waiting for transfers between devices, moved(): return lax.ppermute(value, axes, pairs)  13 us
    all_to_all x2, waiting for transfers between devices, exchange(): return lax.all_to_all(value, axes, split_axis=0, concat_axis=0, tiled=True)  10.3 us
    pallas_call x1, Pallas kernels, on_device(): pl.pallas_call(hidden_kernel, grid=(capacity // 16,), out_shape=(shape((c...  5.2 us
  transfers between devices with their start and end apart: 10, of which 4 were waited for; matrix products, arithmetic and copies ran while one was open for 7% of the time, Pallas kernels for 0%

profile of v3, /device:TPU:1, one launch (start us, length us, event | category | flops | bytes accessed | tf_op | source)
XLA Modules:
  0.0 179.0 jit_solution(3897200488360930446)
XLA Ops:
  0.7 2.6 %octants.1 = bf16[128,16,128]{2,1,0:T(8,128)(2,1)} custom-call(s32[128]{0:T(128)} %bitcast.33, bf16[8,32,512]{2,1,0:T(8,128)(2,1)} %coarse.2, bf16[512,512]{1,0:T(8,128)(2,1)} %constant.74.clone.perm), custom_call_target="tpu_custom_call" | custom-call | tf_op jit(solution)/shard_map/octants/pallas_call | solution.py:567
  3.2 11.5 %all-to-all-start = ((bf16[128,16,128]{2,1,0:T(8,128)(2,1)}), bf16[128,16,128]{2,1,0:T(8,128)(2,1)S(1)}, u32[]{:S(2)}, u32[]{:S(2)}) async-start(bf16[128,16,128]{2,1,0:T(8,128)(2,1)} %octants.1), calls=%async_computation | async-start | bytes 1048576 | tf_op jit(solution)/shard_map/all_to_all | solution.py:545
  15.6 1.0 select_reduce_fusion
  17.1 0.7 concatenate.15.lists
  18.3 10.3 %all-to-all-done.incoming = bf16[128,16,128]{2,1,0:T(8,128)(2,1)S(1)} async-done(((bf16[128,16,128]{2,1,0:T(8,128)(2,1)}), bf16[128,16,128]{2,1,0:T(8,128)(2,1)S(1)}, u32[]{:S(2)}, u32[]{:S(2)}) %all-to-all-start) | async-done | bytes 524320 | tf_op jit(solution)/shard_map/all_to_all | solution.py:545
  28.6 0.8 copy-done
  29.4 5.2 %hidden.1 = (bf16[64,32,512]{2,1,0:T(8,128)(2,1)}, bf16[24,16,128]{2,1,0:T(8,128)(2,1)}, bf16[24,16,128]{2,1,0:T(8,128)(2,1)}, bf16[16,16,128]{2,1,0:T(8,128)(2,1)}, bf16[16,16,128]{2,1,0:T(8,128)(2,1)}) custom-call(s32[64]{0:T(128)} %child.1, s32[64]{0:T(128)} %fusion.17.alive, s32[80]{0:T(128)} %concatenate.15.lists, bf16[128,16,128]{2,1,0:T(8,128)(2,1)} %copy-done, ...), custom_call_target="tpu_custom_call" | custom-call | tf_op jit(solution)/shard_map/hidden/pallas_call | solution.py:587
  34.6 1.3 collective-permute-start
  36.0 0.7 reshape.41.near
  36.9 0.9 reshape.43.taps
  37.7 1.3 collective-permute-start.1
  39.1 4.8 %collective-permute-done.1.rxp = bf16[24,16,128]{2,1,0:T(8,128)(2,1)S(1)} collective-permute-done((bf16[24,16,128]{2,1,0:T(8,128)(2,1)}, bf16[24,16,128]{2,1,0:T(8,128)(2,1)S(1)}, u32[]{:S(2)}, u32[]{:S(2)}) %collective-permute-start.1) | collective-permute-done | bytes 98336 | tf_op jit(solution)/shard_map/ppermute | solution.py:530
  43.9 0.9 pad_maximum_fusion
  44.8 4.4 %collective-permute-start.2 = (bf16[24,16,128]{2,1,0:T(8,128)(2,1)S(1)}, bf16[24,16,128]{2,1,0:T(8,128)(2,1)S(1)}, u32[]{:S(2)}, u32[]{:S(2)}) collective-permute-start(bf16[24,16,128]{2,1,0:T(8,128)(2,1)S(1)} %pad_maximum_fusion), channel_id=1, source_target_pairs={{0,1},{1,2},{2,3},{3,4},{4,5},{5,6},{6,7},{7,8},{8,9},{9,10},{10,1... | collective-permute-start | bytes 294920 | tf_op jit(solution)/shard_map/ppermute | solution.py:530
  49.2 0.9 pad_maximum_fusion.1
  50.0 1.9 %collective-permute-start.3 = (bf16[24,16,128]{2,1,0:T(8,128)(2,1)S(1)}, bf16[24,16,128]{2,1,0:T(8,128)(2,1)S(1)}, u32[]{:S(2)}, u32[]{:S(2)}) collective-permute-start(bf16[24,16,128]{2,1,0:T(8,128)(2,1)S(1)} %pad_maximum_fusion.1), channel_id=1, source_target_pairs={{1,0},{2,1},{3,2},{4,3},{5,4},{6,5},{7,6},{8,7},{9,8},{10,9},{11,1... | collective-permute-start | bytes 294920 | tf_op jit(solution)/shard_map/ppermute | solution.py:530
  52.1 5.4 %collective-permute-done.3.ryp = bf16[24,16,128]{2,1,0:T(8,128)(2,1)S(1)} collective-permute-done((bf16[24,16,128]{2,1,0:T(8,128)(2,1)S(1)}, bf16[24,16,128]{2,1,0:T(8,128)(2,1)S(1)}, u32[]{:S(2)}, u32[]{:S(2)}) %collective-permute-start.3) | collective-permute-done | bytes 98336 | tf_op jit(solution)/shard_map/ppermute | solution.py:530
  58.1 34.1 %forward.1 = (bf16[64,32,512]{2,1,0:T(8,128)(2,1)}, bf16[64,32,512]{2,1,0:T(8,128)(2,1)}, f32[4,32,256]{2,1,0:T(8,128)}, bf16[24,16,128]{2,1,0:T(8,128)(2,1)}, b...) custom-call(s32[1728]{0:T(1024)} %reshape.41.near, s32[80]{0:T(128)} %concatenate.15.lists, ...), custom_call_target="tpu_custom_call" | custom-call | tf_op jit(solution)/shard_map/forward/pallas_call | solution.py:615
  92.2 3.0 %collective-permute-start.4 = (bf16[24,16,128]{2,1,0:T(8,128)(2,1)}, bf16[24,16,128]{2,1,0:T(8,128)(2,1)S(1)}, u32[]{:S(2)}, u32[]{:S(2)}) collective-permute-start(bf16[24,16,128]{2,1,0:T(8,128)(2,1)} %get-tuple-element.27), channel_id=1, source_target_pairs={{0,16},{1,17},{2,18},{3,19},{4,20},{5,21},{6,22},{7,23},{8,24},{9,... | collective-permute-start | bytes 294920 | tf_op jit(solution)/shard_map/ppermute | solution.py:530
  95.9 1.3 collective-permute-start.5
  97.2 1.7 copy.39
  98.9 10.9 %all-to-all-start.1 = ((f32[128,1,256]{2,1,0:T(1,128)}), f32[128,1,256]{2,1,0:T(1,128)S(1)}, u32[]{:S(2)}, u32[]{:S(2)}) async-start(f32[128,1,256]{2,1,0:T(1,128)} %copy.39), calls=%async_computation.1 | async-start | bytes 262144 | tf_op jit(solution)/shard_map/all_to_all | solution.py:545
  109.9 0.9 pad_maximum_fusion.2
  110.8 5.0 %collective-permute-start.6 = (bf16[24,16,128]{2,1,0:T(8,128)(2,1)S(1)}, bf16[24,16,128]{2,1,0:T(8,128)(2,1)S(1)}, u32[]{:S(2)}, u32[]{:S(2)}) collective-permute-start(bf16[24,16,128]{2,1,0:T(8,128)(2,1)S(1)} %pad_maximum_fusion.2), channel_id=1, source_target_pairs={{0,1},{1,2},{2,3},{3,4},{4,5},{5,6},{6,7},{7,8},{8,9},{9,10},{10,1... | collective-permute-start | bytes 294920 | tf_op jit(solution)/shard_map/ppermute | solution.py:530
  115.8 0.9 pad_maximum_fusion.3
  116.7 2.1 %collective-permute-start.7 = (bf16[24,16,128]{2,1,0:T(8,128)(2,1)S(1)}, bf16[24,16,128]{2,1,0:T(8,128)(2,1)S(1)}, u32[]{:S(2)}, u32[]{:S(2)}) collective-permute-start(bf16[24,16,128]{2,1,0:T(8,128)(2,1)S(1)} %pad_maximum_fusion.3), channel_id=1, source_target_pairs={{1,0},{2,1},{3,2},{4,3},{5,4},{6,5},{7,6},{8,7},{9,8},{10,9},{11,1... | collective-permute-start | bytes 294920 | tf_op jit(solution)/shard_map/ppermute | solution.py:530
  118.8 1.1 compare_select_fusion.1.child
  119.9 0.8 copy.40.taps
  121.4 2.8 %collective-permute-done.7.ryp = bf16[24,16,128]{2,1,0:T(8,128)(2,1)S(1)} collective-permute-done((bf16[24,16,128]{2,1,0:T(8,128)(2,1)S(1)}, bf16[24,16,128]{2,1,0:T(8,128)(2,1)S(1)}, u32[]{:S(2)}, u32[]{:S(2)}) %collective-permute-start.7) | collective-permute-done | bytes 98336 | tf_op jit(solution)/shard_map/ppermute | solution.py:530
  124.8 24.8 %backward.1 = (bf16[64,32,512]{2,1,0:T(8,128)(2,1)}, bf16[128,24,128]{2,1,0:T(8,128)(2,1)}) custom-call(s32[1728]{0:T(1024)} %reshape.41.near, s32[64]{0:T(128)} %compare_select_fusion.1.child, bf16[64,32,512]{2,1,0:T(8,128)(2,1)} %get-tuple-element.26.grad, bf16[24,16,128]{2,1,0:T(8,128)(2,1)} %copy-done.2, bf16[24,16,128]{2,1,0:T(8,128)(2,1)} %copy-done.3, ...), custom_call_target="tpu_custom_call" | custom-call | tf_op jit(solution)/shard_map/backward/pallas_call | solution.py:641
  149.6 25.7 %all_to_all.21.returned = bf16[128,24,128]{2,1,0:T(8,128)(2,1)} all-to-all(bf16[128,24,128]{2,1,0:T(8,128)(2,1)} %get-tuple-element.33), channel_id=1, replica_groups=mesh['gx'=8,'gy'=16] {'gx','gy'}, dimensions={0} | all-to-all | bytes 1572864 | tf_op jit(solution)/shard_map/all_to_all | solution.py:545
  175.3 3.7 %coarse.3 = (bf16[8,32,512]{2,1,0:T(8,128)(2,1)}, f32[27,32,32]{2,1,0:T(8,128)}) custom-call(s32[128]{0:T(128)} %bitcast.34, bf16[128,24,128]{2,1,0:T(8,128)(2,1)} %all_to_all.21.returned, bf16[512,512]{1,0:T(8,128)(2,1)} %constant.75.clone.perm), custom_call_target="tpu_custom_call" | custom-call | tf_op jit(solution)/shard_map/coarse/pallas_call | solution.py:656
  (53 shorter events, 4.7 us)
Async XLA Ops:
  0.6 14.8 %copy-start.11 = (s32[9,64]{1,0:T(8,128)S(1)}, s32[9,64]{1,0:T(8,128)}, u32[]{:S(2)}) copy-start(s32[9,64]{1,0:T(8,128)} %constant.89) | copy-start | bytes 6916
  0.6 14.1 %copy-start.6 = (s32[64,27]{0,1:T(8,128)S(1)}, s32[64,27]{0,1:T(8,128)}, u32[]{:S(2)}) copy-start(s32[64,27]{0,1:T(8,128)} %param.21) | copy-start | bytes 20740
  3.2 25.4 %all-to-all-start = ((bf16[128,16,128]{2,1,0:T(8,128)(2,1)}), bf16[128,16,128]{2,1,0:T(8,128)(2,1)S(1)}, u32[]{:S(2)}, u32[]{:S(2)}) async-start(bf16[128,16,128]{2,1,0:T(8,128)(2,1)} %octants.1), calls=%async_computation | async-start | bytes 1048576 | tf_op jit(solution)/shard_map/all_to_all | solution.py:545
  14.8 22.0 %copy-start.1 = (bf16[27,32,32]{2,1,0:T(8,128)(2,1)S(1)}, bf16[27,32,32]{2,1,0:T(8,128)(2,1)}, u32[]{:S(2)}) copy-start(bf16[27,32,32]{2,1,0:T(8,128)(2,1)} %param.19) | copy-start | bytes 165892
  18.3 33.7 %copy-start.12 = (s32[64]{0:T(128)S(1)}, s32[64]{0:T(128)}, u32[]{:S(2)}) copy-start(s32[64]{0:T(128)} %child.1) | copy-start | bytes 772
  28.6 0.8 copy-start
  34.6 4.4 %collective-permute-start = (bf16[24,16,128]{2,1,0:T(8,128)(2,1)}, bf16[24,16,128]{2,1,0:T(8,128)(2,1)S(1)}, u32[]{:S(2)}, u32[]{:S(2)}) collective-permute-start(bf16[24,16,128]{2,1,0:T(8,128)(2,1)} %get-tuple-element.21), channel_id=1, source_target_pairs={{0,16},{1,17},{2,18},{3,19},{4,20},{5,21},{6,22},{7,23},{8,24},{9,... | collective-permute-start | bytes 294920 | tf_op jit(solution)/shard_map/ppermute | solution.py:530
  37.7 6.1 %collective-permute-start.1 = (bf16[24,16,128]{2,1,0:T(8,128)(2,1)}, bf16[24,16,128]{2,1,0:T(8,128)(2,1)S(1)}, u32[]{:S(2)}, u32[]{:S(2)}) collective-permute-start(bf16[24,16,128]{2,1,0:T(8,128)(2,1)} %get-tuple-element.22), channel_id=1, source_target_pairs={{16,0},{17,1},{18,2},{19,3},{20,4},{21,5},{22,6},{23,7},{24,8},{25... | collective-permute-start | bytes 294920 | tf_op jit(solution)/shard_map/ppermute | solution.py:530
  39.0 18.4 %copy-start.4 = (bf16[24,16,128]{2,1,0:T(8,128)(2,1)}, bf16[24,16,128]{2,1,0:T(8,128)(2,1)S(1)}, u32[]{:S(2)}) copy-start(bf16[24,16,128]{2,1,0:T(8,128)(2,1)S(1)} %collective-permute-done.rxm) | copy-start | bytes 294916
  43.9 13.6 %copy-start.5 = (bf16[24,16,128]{2,1,0:T(8,128)(2,1)}, bf16[24,16,128]{2,1,0:T(8,128)(2,1)S(1)}, u32[]{:S(2)}) copy-start(bf16[24,16,128]{2,1,0:T(8,128)(2,1)S(1)} %collective-permute-done.1.rxp) | copy-start | bytes 294916
  44.8 7.3 %collective-permute-start.2 = (bf16[24,16,128]{2,1,0:T(8,128)(2,1)S(1)}, bf16[24,16,128]{2,1,0:T(8,128)(2,1)S(1)}, u32[]{:S(2)}, u32[]{:S(2)}) collective-permute-start(bf16[24,16,128]{2,1,0:T(8,128)(2,1)S(1)} %pad_maximum_fusion), channel_id=1, source_target_pairs={{0,1},{1,2},{2,3},{3,4},{4,5},{5,6},{6,7},{7,8},{8,9},{9,10},{10,1... | collective-permute-start | bytes 294920 | tf_op jit(solution)/shard_map/ppermute | solution.py:530
  50.0 7.4 %collective-permute-start.3 = (bf16[24,16,128]{2,1,0:T(8,128)(2,1)S(1)}, bf16[24,16,128]{2,1,0:T(8,128)(2,1)S(1)}, u32[]{:S(2)}, u32[]{:S(2)}) collective-permute-start(bf16[24,16,128]{2,1,0:T(8,128)(2,1)S(1)} %pad_maximum_fusion.1), channel_id=1, source_target_pairs={{1,0},{2,1},{3,2},{4,3},{5,4},{6,5},{7,6},{8,7},{9,8},{10,9},{11,1... | collective-permute-start | bytes 294920 | tf_op jit(solution)/shard_map/ppermute | solution.py:530
  52.1 5.4 %copy-start.8 = (bf16[24,16,128]{2,1,0:T(8,128)(2,1)}, bf16[24,16,128]{2,1,0:T(8,128)(2,1)S(1)}, u32[]{:S(2)}) copy-start(bf16[24,16,128]{2,1,0:T(8,128)(2,1)S(1)} %collective-permute-done.2.rym) | copy-start | bytes 294916
  57.5 0.6 copy-start.10
  92.2 17.6 %collective-permute-start.4 = (bf16[24,16,128]{2,1,0:T(8,128)(2,1)}, bf16[24,16,128]{2,1,0:T(8,128)(2,1)S(1)}, u32[]{:S(2)}, u32[]{:S(2)}) collective-permute-start(bf16[24,16,128]{2,1,0:T(8,128)(2,1)} %get-tuple-element.27), channel_id=1, source_target_pairs={{0,16},{1,17},{2,18},{3,19},{4,20},{5,21},{6,22},{7,23},{8,24},{9,... | collective-permute-start | bytes 294920 | tf_op jit(solution)/shard_map/ppermute | solution.py:530
  95.9 14.0 %collective-permute-start.5 = (bf16[24,16,128]{2,1,0:T(8,128)(2,1)}, bf16[24,16,128]{2,1,0:T(8,128)(2,1)S(1)}, u32[]{:S(2)}, u32[]{:S(2)}) collective-permute-start(bf16[24,16,128]{2,1,0:T(8,128)(2,1)} %get-tuple-element.28), channel_id=1, source_target_pairs={{16,0},{17,1},{18,2},{19,3},{20,4},{21,5},{22,6},{23,7},{24,8},{25... | collective-permute-start | bytes 294920 | tf_op jit(solution)/shard_map/ppermute | solution.py:530
  98.9 21.8 %all-to-all-start.1 = ((f32[128,1,256]{2,1,0:T(1,128)}), f32[128,1,256]{2,1,0:T(1,128)S(1)}, u32[]{:S(2)}, u32[]{:S(2)}) async-start(f32[128,1,256]{2,1,0:T(1,128)} %copy.39), calls=%async_computation.1 | async-start | bytes 262144 | tf_op jit(solution)/shard_map/all_to_all | solution.py:545
  109.8 14.3 %copy-start.2 = (bf16[24,16,128]{2,1,0:T(8,128)(2,1)}, bf16[24,16,128]{2,1,0:T(8,128)(2,1)S(1)}, u32[]{:S(2)}) copy-start(bf16[24,16,128]{2,1,0:T(8,128)(2,1)S(1)} %collective-permute-done.4.rxm) | copy-start | bytes 294916
  109.9 14.3 %copy-start.3 = (bf16[24,16,128]{2,1,0:T(8,128)(2,1)}, bf16[24,16,128]{2,1,0:T(8,128)(2,1)S(1)}, u32[]{:S(2)}) copy-start(bf16[24,16,128]{2,1,0:T(8,128)(2,1)S(1)} %collective-permute-done.5.rxp) | copy-start | bytes 294916
  110.8 10.6 %collective-permute-start.6 = (bf16[24,16,128]{2,1,0:T(8,128)(2,1)S(1)}, bf16[24,16,128]{2,1,0:T(8,128)(2,1)S(1)}, u32[]{:S(2)}, u32[]{:S(2)}) collective-permute-start(bf16[24,16,128]{2,1,0:T(8,128)(2,1)S(1)} %pad_maximum_fusion.2), channel_id=1, source_target_pairs={{0,1},{1,2},{2,3},{3,4},{4,5},{5,6},{6,7},{7,8},{8,9},{9,10},{10,1... | collective-permute-start | bytes 294920 | tf_op jit(solution)/shard_map/ppermute | solution.py:530
  116.7 7.4 %collective-permute-start.7 = (bf16[24,16,128]{2,1,0:T(8,128)(2,1)S(1)}, bf16[24,16,128]{2,1,0:T(8,128)(2,1)S(1)}, u32[]{:S(2)}, u32[]{:S(2)}) collective-permute-start(bf16[24,16,128]{2,1,0:T(8,128)(2,1)S(1)} %pad_maximum_fusion.3), channel_id=1, source_target_pairs={{1,0},{2,1},{3,2},{4,3},{5,4},{6,5},{7,6},{8,7},{9,8},{10,9},{11,1... | collective-permute-start | bytes 294920 | tf_op jit(solution)/shard_map/ppermute | solution.py:530
  121.4 2.8 %copy-start.7 = (bf16[24,16,128]{2,1,0:T(8,128)(2,1)}, bf16[24,16,128]{2,1,0:T(8,128)(2,1)S(1)}, u32[]{:S(2)}) copy-start(bf16[24,16,128]{2,1,0:T(8,128)(2,1)S(1)} %collective-permute-done.6.rym) | copy-start | bytes 294916
  124.1 0.6 copy-start.9

commit v4 on v3

--- a/solution.py
+++ b/solution.py
@@ -272,6 +272,16 @@
         weight[x * 32 : x * 32 + 32, x * band : x * band + 3 * band] = taps[...]
 
 
+def convolve(weight, stack):
+    halves = []
+    for h in range(2):
+        seen = slice(h * 4 * band, h * 4 * band + 6 * band)
+        halves.append(
+            jnp.dot(weight[h * 128 : h * 128 + 128, seen], stack[seen], preferred_element_type=f32)
+        )
+    return jnp.concatenate(halves, axis=0)
+
+
 def alive_lanes(step, near):
     lane = lax.broadcasted_iota(jnp.int32, (1, 256), 1)
     out = jnp.zeros((1, 256), f32)
@@ -328,7 +338,7 @@
 
     def process(index, slot):
         stack = stacks[slot]
-        pre_all = jnp.dot(weight[...], stack[...], preferred_element_type=f32)
+        pre_all = convolve(weight, stack)
         live = alive_lanes(index, near)
         grad_pair = []
         for t in range(4):
@@ -369,7 +379,9 @@
         term_wide[0 : 3 * band, 0:32] = acc
         across = term_wide[...].T
         for j in range(4):
-            term[j] = across[0:32, j * 256 : j * 256 + 256]
+            for half in range(2):
+                at_lane = j * 256 + half * 128
+                term[j * 32 : j * 32 + 32, half, :] = across[0:32, at_lane : at_lane + 128]
 
 
 def backward_kernel(
@@ -387,12 +399,12 @@
         banded(taps, weight)
         fill_table(table, grad, rxm, rxp, rym, ryp, elow, ehigh)
         build(0, 0)
-        rest = jnp.sum(terms[...], axis=0, keepdims=True)
+        rest = jnp.sum(terms[...], axis=0)
         rows = []
         for i in range(3):
             part = rest.astype(bf16)
             rest = rest - part.astype(f32)
-            rows += [part[:, 0:128].astype(f32), part[:, 128:256].astype(f32)]
+            rows += [part.astype(f32)]
         rows += [jnp.zeros((2, 128), f32)]
         tail = jnp.concatenate(rows, axis=0).astype(bf16)
         clear = jnp.zeros((16, 128), bf16)
@@ -409,7 +421,7 @@
     low16 = lane_id(16) < 64
 
     def process(index, slot):
-        conv = jnp.dot(weight[...], stacks[slot][...], preferred_element_type=f32)
+        conv = convolve(weight, stacks[slot])
         live = alive_lanes(index, near)
         sums = []
         for t in range(4):
@@ -431,8 +443,8 @@
 
     build(2 * step + 1, 1)
     process(2 * step, 0)
+    process(2 * step + 1, 1)
     build(jnp.minimum(2 * step + 2, steps - 1), 0)
-    process(2 * step + 1, 1)
 
     @pl.when(step == steps // 2 - 1)
     def _():
@@ -618,7 +630,7 @@
         out_shape=(
             shape((capacity, channels, 512)),
             shape((capacity, channels, 512)),
-            shape((4, 32, 256), f32),
+            shape((devices, 2, 128), f32),
             side, side, face, face,
         ),
         in_specs=[smem, smem, bricks]
@@ -627,7 +639,7 @@
         + [whole((128, 1024))] * 2
         + [whole((1024, 128))] * 2
         + [whole((256, 256))],
-        out_specs=(per_step, bricks, whole((4, 32, 256)))
+        out_specs=(per_step, bricks, whole((devices, 2, 128)))
         + tuple(whole((n,) + packed) for n in (side_n, side_n, face_n, face_n)),
         scratch_shapes=[table, banded_weight, wide]
         + work
@@ -636,7 +648,7 @@
         name="forward",
     )(near, lists, hidden, *near_h, cotangent, taps, elow, ehigh, ylow, yhigh, shift)
     near_g = halo(gxm, gxp, gym, gyp)
-    terms = exchange(term.reshape(devices, 256))
+    terms = exchange(term)
 
     fine_grad, back = pl.pallas_call(
         backward_kernel,
@@ -645,7 +657,7 @@
         in_specs=[smem, smem, bricks]
         + sides
         + [per_step, whole((channels, 27 * channels)), whole((128, 1024)), whole((128, 1024))]
-        + [whole((1024, 256)), whole((256, 256)), whole((devices, 256))],
+        + [whole((1024, 256)), whole((256, 256)), whole((devices, 2, 128))],
         out_specs=(per_step, whole((devices, 24, 128))),
         scratch_shapes=[table, banded_weight] + work + [pltpu.VMEM((steps * channels, 1024), bf16)],
         compiler_params=params(),

time: 180 us -> 177 us (0.983)
  Pallas kernels: 70.5 us -> 62.8 us
  waiting for transfers between devices: 23.3 us -> 28.9 us
  local copies, waits for them, and re-layouts: 7.87 us -> 5.48 us
    ppermute x8, waiting for transfers between devices: 13 us -> 18.6 us  [moved(): return lax.ppermute(value, axes, pairs)]
    pallas_call x1, Pallas kernels: 34.1 us -> 29.6 us  [on_device(): pl.pallas_call(forward_kernel, grid=(steps // 2,), out_shape=(shape((capa...]
    pallas_call x1, Pallas kernels: 24.8 us -> 21.6 us  [on_device(): pl.pallas_call(backward_kernel, grid=(steps // 2,), out_shape=(shape((cap...]
  transfers between devices with their start and end apart: 10 -> 10, of which waited for: 4 -> 5; matrix products, arithmetic and copies ran while one was open for 7% -> 6% of each run, Pallas kernels for 0% -> 0%
where the time goes in v4:
time: 177 us; the launch traced here: 176 us
  Pallas kernels  62.8 us (35%)
  starting transfers between devices  43.1 us (24%)
  waiting for transfers between devices  28.9 us (16%)
  blocking collectives  26.6 us (15%)
  other arithmetic  7.81 us (4%)
  local copies, waits for them, and re-layouts  5.48 us (3%)
    pallas_call x1, Pallas kernels, on_device(): pl.pallas_call(forward_kernel, grid=(steps // 2,), out_shape=(shape((capa...  29.6 us
    all_to_all x1, blocking collectives, exchange(): return lax.all_to_all(value, axes, split_axis=0, concat_axis=0, tiled=True)  26.6 us
    pallas_call x1, Pallas kernels, on_device(): pl.pallas_call(backward_kernel, grid=(steps // 2,), out_shape=(shape((cap...  21.6 us
    ppermute x8, starting transfers between devices, moved(): return lax.ppermute(value, axes, pairs)  21.6 us
    all_to_all x2, starting transfers between devices, exchange(): return lax.all_to_all(value, axes, split_axis=0, concat_axis=0, tiled=True)  21.5 us
    ppermute x8, waiting for transfers between devices, moved(): return lax.ppermute(value, axes, pairs)  18.6 us
    all_to_all x2, waiting for transfers between devices, exchange(): return lax.all_to_all(value, axes, split_axis=0, concat_axis=0, tiled=True)  10.3 us
    pallas_call x1, Pallas kernels, on_device(): pl.pallas_call(hidden_kernel, grid=(capacity // 16,), out_shape=(shape((c...  5.19 us
  transfers between devices with their start and end apart: 10, of which 5 were waited for; matrix products, arithmetic and copies ran while one was open for 6% of the time, Pallas kernels for 0%

profile of v4, /device:TPU:1, one launch (start us, length us, event | category | flops | bytes accessed | tf_op | source)
XLA Modules:
  0.0 175.8 jit_solution(7061380510392461631)
XLA Ops:
  0.7 2.6 %octants.1 = bf16[128,16,128]{2,1,0:T(8,128)(2,1)} custom-call(s32[128]{0:T(128)} %bitcast.27, bf16[8,32,512]{2,1,0:T(8,128)(2,1)} %coarse.2, bf16[512,512]{1,0:T(8,128)(2,1)} %constant.74.clone.perm), custom_call_target="tpu_custom_call" | custom-call | tf_op jit(solution)/shard_map/octants/pallas_call | solution.py:579
  3.2 11.5 %all-to-all-start = ((bf16[128,16,128]{2,1,0:T(8,128)(2,1)}), bf16[128,16,128]{2,1,0:T(8,128)(2,1)S(1)}, u32[]{:S(2)}, u32[]{:S(2)}) async-start(bf16[128,16,128]{2,1,0:T(8,128)(2,1)} %octants.1), calls=%async_computation | async-start | bytes 1048576 | tf_op jit(solution)/shard_map/all_to_all | solution.py:557
  15.6 1.0 select_reduce_fusion
  17.1 0.7 concatenate.15.lists
  18.3 10.3 %all-to-all-done.incoming = bf16[128,16,128]{2,1,0:T(8,128)(2,1)S(1)} async-done(((bf16[128,16,128]{2,1,0:T(8,128)(2,1)}), bf16[128,16,128]{2,1,0:T(8,128)(2,1)S(1)}, u32[]{:S(2)}, u32[]{:S(2)}) %all-to-all-start) | async-done | bytes 524320 | tf_op jit(solution)/shard_map/all_to_all | solution.py:557
  28.6 0.8 copy-done
  29.4 5.2 %hidden.1 = (bf16[64,32,512]{2,1,0:T(8,128)(2,1)}, bf16[24,16,128]{2,1,0:T(8,128)(2,1)}, bf16[24,16,128]{2,1,0:T(8,128)(2,1)}, bf16[16,16,128]{2,1,0:T(8,128)(2,1)}, bf16[16,16,128]{2,1,0:T(8,128)(2,1)}) custom-call(s32[64]{0:T(128)} %child.1, s32[64]{0:T(128)} %fusion.17.alive, s32[80]{0:T(128)} %concatenate.15.lists, bf16[128,16,128]{2,1,0:T(8,128)(2,1)} %copy-done, ...), custom_call_target="tpu_custom_call" | custom-call | tf_op jit(solution)/shard_map/hidden/pallas_call | solution.py:599
  34.6 1.3 collective-permute-start
  36.0 0.7 reshape.37.near
  36.9 0.9 reshape.39.taps
  37.7 1.3 collective-permute-start.1
  39.0 4.8 %collective-permute-done.1.rxp = bf16[24,16,128]{2,1,0:T(8,128)(2,1)S(1)} collective-permute-done((bf16[24,16,128]{2,1,0:T(8,128)(2,1)}, bf16[24,16,128]{2,1,0:T(8,128)(2,1)S(1)}, u32[]{:S(2)}, u32[]{:S(2)}) %collective-permute-start.1) | collective-permute-done | bytes 98336 | tf_op jit(solution)/shard_map/ppermute | solution.py:542
  43.9 0.9 pad_maximum_fusion
  44.8 4.4 %collective-permute-start.2 = (bf16[24,16,128]{2,1,0:T(8,128)(2,1)S(1)}, bf16[24,16,128]{2,1,0:T(8,128)(2,1)S(1)}, u32[]{:S(2)}, u32[]{:S(2)}) collective-permute-start(bf16[24,16,128]{2,1,0:T(8,128)(2,1)S(1)} %pad_maximum_fusion), channel_id=1, source_target_pairs={{0,1},{1,2},{2,3},{3,4},{4,5},{5,6},{6,7},{7,8},{8,9},{9,10},{10,1... | collective-permute-start | bytes 294920 | tf_op jit(solution)/shard_map/ppermute | solution.py:542
  49.2 0.9 pad_maximum_fusion.1
  50.0 1.9 %collective-permute-start.3 = (bf16[24,16,128]{2,1,0:T(8,128)(2,1)S(1)}, bf16[24,16,128]{2,1,0:T(8,128)(2,1)S(1)}, u32[]{:S(2)}, u32[]{:S(2)}) collective-permute-start(bf16[24,16,128]{2,1,0:T(8,128)(2,1)S(1)} %pad_maximum_fusion.1), channel_id=1, source_target_pairs={{1,0},{2,1},{3,2},{4,3},{5,4},{6,5},{7,6},{8,7},{9,8},{10,9},{11,1... | collective-permute-start | bytes 294920 | tf_op jit(solution)/shard_map/ppermute | solution.py:542
  52.1 5.4 %collective-permute-done.3.ryp = bf16[24,16,128]{2,1,0:T(8,128)(2,1)S(1)} collective-permute-done((bf16[24,16,128]{2,1,0:T(8,128)(2,1)S(1)}, bf16[24,16,128]{2,1,0:T(8,128)(2,1)S(1)}, u32[]{:S(2)}, u32[]{:S(2)}) %collective-permute-start.3) | collective-permute-done | bytes 98336 | tf_op jit(solution)/shard_map/ppermute | solution.py:542
  58.1 29.6 %forward.1 = (bf16[64,32,512]{2,1,0:T(8,128)(2,1)}, bf16[64,32,512]{2,1,0:T(8,128)(2,1)}, f32[128,2,128]{2,1,0:T(2,128)}, bf16[24,16,128]{2,1,0:T(8,128)(2,1)}, ...) custom-call(s32[1728]{0:T(1024)} %reshape.37.near, s32[80]{0:T(128)} %concatenate.15.lists, ...), custom_call_target="tpu_custom_call" | custom-call | tf_op jit(solution)/shard_map/forward/pallas_call | solution.py:627
  87.7 3.0 %collective-permute-start.4 = (bf16[24,16,128]{2,1,0:T(8,128)(2,1)}, bf16[24,16,128]{2,1,0:T(8,128)(2,1)S(1)}, u32[]{:S(2)}, u32[]{:S(2)}) collective-permute-start(bf16[24,16,128]{2,1,0:T(8,128)(2,1)} %get-tuple-element.27), channel_id=1, source_target_pairs={{0,16},{1,17},{2,18},{3,19},{4,20},{5,21},{6,22},{7,23},{8,24},{9,... | collective-permute-start | bytes 294920 | tf_op jit(solution)/shard_map/ppermute | solution.py:542
  91.4 10.0 %all-to-all-start.1 = ((f32[128,2,128]{2,1,0:T(2,128)}), f32[128,2,128]{2,1,0:T(2,128)S(1)}, u32[]{:S(2)}, u32[]{:S(2)}) async-start(f32[128,2,128]{2,1,0:T(2,128)} %get-tuple-element.31), calls=%async_computation.1 | async-start | bytes 262144 | tf_op jit(solution)/shard_map/all_to_all | solution.py:557
  101.4 1.3 collective-permute-start.5
  102.7 5.0 %collective-permute-done.5.rxp = bf16[24,16,128]{2,1,0:T(8,128)(2,1)S(1)} collective-permute-done((bf16[24,16,128]{2,1,0:T(8,128)(2,1)}, bf16[24,16,128]{2,1,0:T(8,128)(2,1)S(1)}, u32[]{:S(2)}, u32[]{:S(2)}) %collective-permute-start.5) | collective-permute-done | bytes 98336 | tf_op jit(solution)/shard_map/ppermute | solution.py:542
  107.8 0.9 pad_maximum_fusion.2
  108.7 6.2 %collective-permute-start.6 = (bf16[24,16,128]{2,1,0:T(8,128)(2,1)S(1)}, bf16[24,16,128]{2,1,0:T(8,128)(2,1)S(1)}, u32[]{:S(2)}, u32[]{:S(2)}) collective-permute-start(bf16[24,16,128]{2,1,0:T(8,128)(2,1)S(1)} %pad_maximum_fusion.2), channel_id=1, source_target_pairs={{0,1},{1,2},{2,3},{3,4},{4,5},{5,6},{6,7},{7,8},{8,9},{9,10},{10,1... | collective-permute-start | bytes 294920 | tf_op jit(solution)/shard_map/ppermute | solution.py:542
  114.9 0.9 pad_maximum_fusion.3
  115.7 2.1 %collective-permute-start.7 = (bf16[24,16,128]{2,1,0:T(8,128)(2,1)S(1)}, bf16[24,16,128]{2,1,0:T(8,128)(2,1)S(1)}, u32[]{:S(2)}, u32[]{:S(2)}) collective-permute-start(bf16[24,16,128]{2,1,0:T(8,128)(2,1)S(1)} %pad_maximum_fusion.3), channel_id=1, source_target_pairs={{1,0},{2,1},{3,2},{4,3},{5,4},{6,5},{7,6},{8,7},{9,8},{10,9},{11,1... | collective-permute-start | bytes 294920 | tf_op jit(solution)/shard_map/ppermute | solution.py:542
  117.9 1.2 compare_select_fusion.1.child
  119.0 0.7 copy.33.taps
  119.8 3.4 %collective-permute-done.7.ryp = bf16[24,16,128]{2,1,0:T(8,128)(2,1)S(1)} collective-permute-done((bf16[24,16,128]{2,1,0:T(8,128)(2,1)S(1)}, bf16[24,16,128]{2,1,0:T(8,128)(2,1)S(1)}, u32[]{:S(2)}, u32[]{:S(2)}) %collective-permute-start.7) | collective-permute-done | bytes 98336 | tf_op jit(solution)/shard_map/ppermute | solution.py:542
  123.8 21.6 %backward.1 = (bf16[64,32,512]{2,1,0:T(8,128)(2,1)}, bf16[128,24,128]{2,1,0:T(8,128)(2,1)}) custom-call(s32[1728]{0:T(1024)} %reshape.37.near, s32[64]{0:T(128)} %compare_select_fusion.1.child, bf16[64,32,512]{2,1,0:T(8,128)(2,1)} %get-tuple-element.26.grad, bf16[24,16,128]{2,1,0:T(8,128)(2,1)} %copy-done.3, bf16[24,16,128]{2,1,0:T(8,128)(2,1)} %copy-done.5, ...), custom_call_target="tpu_custom_call" | custom-call | tf_op jit(solution)/shard_map/backward/pallas_call | solution.py:653
  145.5 26.6 %all_to_all.15.returned = bf16[128,24,128]{2,1,0:T(8,128)(2,1)} all-to-all(bf16[128,24,128]{2,1,0:T(8,128)(2,1)} %get-tuple-element.33), channel_id=1, replica_groups=mesh['gx'=8,'gy'=16] {'gx','gy'}, dimensions={0} | all-to-all | bytes 1572864 | tf_op jit(solution)/shard_map/all_to_all | solution.py:557
  172.1 3.7 %coarse.3 = (bf16[8,32,512]{2,1,0:T(8,128)(2,1)}, f32[27,32,32]{2,1,0:T(8,128)}) custom-call(s32[128]{0:T(128)} %bitcast.28, bf16[128,24,128]{2,1,0:T(8,128)(2,1)} %all_to_all.15.returned, bf16[512,512]{1,0:T(8,128)(2,1)} %constant.75.clone.perm), custom_call_target="tpu_custom_call" | custom-call | tf_op jit(solution)/shard_map/coarse/pallas_call | solution.py:668
  (53 shorter events, 4.1 us)
Async XLA Ops:
  0.6 14.8 %copy-start.12 = (s32[9,64]{1,0:T(8,128)S(1)}, s32[9,64]{1,0:T(8,128)}, u32[]{:S(2)}) copy-start(s32[9,64]{1,0:T(8,128)} %constant.89) | copy-start | bytes 6916
  0.6 14.1 %copy-start.7 = (s32[64,27]{0,1:T(8,128)S(1)}, s32[64,27]{0,1:T(8,128)}, u32[]{:S(2)}) copy-start(s32[64,27]{0,1:T(8,128)} %param.21) | copy-start | bytes 20740
  3.2 25.4 %all-to-all-start = ((bf16[128,16,128]{2,1,0:T(8,128)(2,1)}), bf16[128,16,128]{2,1,0:T(8,128)(2,1)S(1)}, u32[]{:S(2)}, u32[]{:S(2)}) async-start(bf16[128,16,128]{2,1,0:T(8,128)(2,1)} %octants.1), calls=%async_computation | async-start | bytes 1048576 | tf_op jit(solution)/shard_map/all_to_all | solution.py:557
  14.8 22.0 %copy-start.1 = (bf16[27,32,32]{2,1,0:T(8,128)(2,1)S(1)}, bf16[27,32,32]{2,1,0:T(8,128)(2,1)}, u32[]{:S(2)}) copy-start(bf16[27,32,32]{2,1,0:T(8,128)(2,1)} %param.19) | copy-start | bytes 165892
  18.3 33.6 %copy-start.13 = (s32[64]{0:T(128)S(1)}, s32[64]{0:T(128)}, u32[]{:S(2)}) copy-start(s32[64]{0:T(128)} %child.1) | copy-start | bytes 772
  28.6 0.8 copy-start
  34.6 4.4 %collective-permute-start = (bf16[24,16,128]{2,1,0:T(8,128)(2,1)}, bf16[24,16,128]{2,1,0:T(8,128)(2,1)S(1)}, u32[]{:S(2)}, u32[]{:S(2)}) collective-permute-start(bf16[24,16,128]{2,1,0:T(8,128)(2,1)} %get-tuple-element.21), channel_id=1, source_target_pairs={{0,16},{1,17},{2,18},{3,19},{4,20},{5,21},{6,22},{7,23},{8,24},{9,... | collective-permute-start | bytes 294920 | tf_op jit(solution)/shard_map/ppermute | solution.py:542
  37.7 6.1 %collective-permute-start.1 = (bf16[24,16,128]{2,1,0:T(8,128)(2,1)}, bf16[24,16,128]{2,1,0:T(8,128)(2,1)S(1)}, u32[]{:S(2)}, u32[]{:S(2)}) collective-permute-start(bf16[24,16,128]{2,1,0:T(8,128)(2,1)} %get-tuple-element.22), channel_id=1, source_target_pairs={{16,0},{17,1},{18,2},{19,3},{20,4},{21,5},{22,6},{23,7},{24,8},{25... | collective-permute-start | bytes 294920 | tf_op jit(solution)/shard_map/ppermute | solution.py:542
  39.0 18.4 %copy-start.4 = (bf16[24,16,128]{2,1,0:T(8,128)(2,1)}, bf16[24,16,128]{2,1,0:T(8,128)(2,1)S(1)}, u32[]{:S(2)}) copy-start(bf16[24,16,128]{2,1,0:T(8,128)(2,1)S(1)} %collective-permute-done.rxm) | copy-start | bytes 294916
  43.9 13.6 %copy-start.6 = (bf16[24,16,128]{2,1,0:T(8,128)(2,1)}, bf16[24,16,128]{2,1,0:T(8,128)(2,1)S(1)}, u32[]{:S(2)}) copy-start(bf16[24,16,128]{2,1,0:T(8,128)(2,1)S(1)} %collective-permute-done.1.rxp) | copy-start | bytes 294916
  44.8 7.3 %collective-permute-start.2 = (bf16[24,16,128]{2,1,0:T(8,128)(2,1)S(1)}, bf16[24,16,128]{2,1,0:T(8,128)(2,1)S(1)}, u32[]{:S(2)}, u32[]{:S(2)}) collective-permute-start(bf16[24,16,128]{2,1,0:T(8,128)(2,1)S(1)} %pad_maximum_fusion), channel_id=1, source_target_pairs={{0,1},{1,2},{2,3},{3,4},{4,5},{5,6},{6,7},{7,8},{8,9},{9,10},{10,1... | collective-permute-start | bytes 294920 | tf_op jit(solution)/shard_map/ppermute | solution.py:542
  50.0 7.4 %collective-permute-start.3 = (bf16[24,16,128]{2,1,0:T(8,128)(2,1)S(1)}, bf16[24,16,128]{2,1,0:T(8,128)(2,1)S(1)}, u32[]{:S(2)}, u32[]{:S(2)}) collective-permute-start(bf16[24,16,128]{2,1,0:T(8,128)(2,1)S(1)} %pad_maximum_fusion.1), channel_id=1, source_target_pairs={{1,0},{2,1},{3,2},{4,3},{5,4},{6,5},{7,6},{8,7},{9,8},{10,9},{11,1... | collective-permute-start | bytes 294920 | tf_op jit(solution)/shard_map/ppermute | solution.py:542
  52.0 5.4 %copy-start.9 = (bf16[24,16,128]{2,1,0:T(8,128)(2,1)}, bf16[24,16,128]{2,1,0:T(8,128)(2,1)S(1)}, u32[]{:S(2)}) copy-start(bf16[24,16,128]{2,1,0:T(8,128)(2,1)S(1)} %collective-permute-done.2.rym) | copy-start | bytes 294916
  57.5 0.6 copy-start.11
  87.7 15.0 %collective-permute-start.4 = (bf16[24,16,128]{2,1,0:T(8,128)(2,1)}, bf16[24,16,128]{2,1,0:T(8,128)(2,1)S(1)}, u32[]{:S(2)}, u32[]{:S(2)}) collective-permute-start(bf16[24,16,128]{2,1,0:T(8,128)(2,1)} %get-tuple-element.27), channel_id=1, source_target_pairs={{0,16},{1,17},{2,18},{3,19},{4,20},{5,21},{6,22},{7,23},{8,24},{9,... | collective-permute-start | bytes 294920 | tf_op jit(solution)/shard_map/ppermute | solution.py:542
  91.4 28.4 %all-to-all-start.1 = ((f32[128,2,128]{2,1,0:T(2,128)}), f32[128,2,128]{2,1,0:T(2,128)S(1)}, u32[]{:S(2)}, u32[]{:S(2)}) async-start(f32[128,2,128]{2,1,0:T(2,128)} %get-tuple-element.31), calls=%async_computation.1 | async-start | bytes 262144 | tf_op jit(solution)/shard_map/all_to_all | solution.py:557
  101.4 6.4 %collective-permute-start.5 = (bf16[24,16,128]{2,1,0:T(8,128)(2,1)}, bf16[24,16,128]{2,1,0:T(8,128)(2,1)S(1)}, u32[]{:S(2)}, u32[]{:S(2)}) collective-permute-start(bf16[24,16,128]{2,1,0:T(8,128)(2,1)} %get-tuple-element.28), channel_id=1, source_target_pairs={{16,0},{17,1},{18,2},{19,3},{20,4},{21,5},{22,6},{23,7},{24,8},{25... | collective-permute-start | bytes 294920 | tf_op jit(solution)/shard_map/ppermute | solution.py:542
  102.7 20.5 %copy-start.3 = (bf16[24,16,128]{2,1,0:T(8,128)(2,1)}, bf16[24,16,128]{2,1,0:T(8,128)(2,1)S(1)}, u32[]{:S(2)}) copy-start(bf16[24,16,128]{2,1,0:T(8,128)(2,1)S(1)} %collective-permute-done.4.rxm) | copy-start | bytes 294916
  107.8 15.4 %copy-start.5 = (bf16[24,16,128]{2,1,0:T(8,128)(2,1)}, bf16[24,16,128]{2,1,0:T(8,128)(2,1)S(1)}, u32[]{:S(2)}) copy-start(bf16[24,16,128]{2,1,0:T(8,128)(2,1)S(1)} %collective-permute-done.5.rxp) | copy-start | bytes 294916
  108.7 11.1 %collective-permute-start.6 = (bf16[24,16,128]{2,1,0:T(8,128)(2,1)S(1)}, bf16[24,16,128]{2,1,0:T(8,128)(2,1)S(1)}, u32[]{:S(2)}, u32[]{:S(2)}) collective-permute-start(bf16[24,16,128]{2,1,0:T(8,128)(2,1)S(1)} %pad_maximum_fusion.2), channel_id=1, source_target_pairs={{0,1},{1,2},{2,3},{3,4},{4,5},{5,6},{6,7},{7,8},{8,9},{9,10},{10,1... | collective-permute-start | bytes 294920 | tf_op jit(solution)/shard_map/ppermute | solution.py:542
  115.7 7.4 %collective-permute-start.7 = (bf16[24,16,128]{2,1,0:T(8,128)(2,1)S(1)}, bf16[24,16,128]{2,1,0:T(8,128)(2,1)S(1)}, u32[]{:S(2)}, u32[]{:S(2)}) collective-permute-start(bf16[24,16,128]{2,1,0:T(8,128)(2,1)S(1)} %pad_maximum_fusion.3), channel_id=1, source_target_pairs={{1,0},{2,1},{3,2},{4,3},{5,4},{6,5},{7,6},{8,7},{9,8},{10,9},{11,1... | collective-permute-start | bytes 294920 | tf_op jit(solution)/shard_map/ppermute | solution.py:542
  119.8 3.4 %copy-start.2 = (f32[128,2,128]{2,1,0:T(2,128)}, f32[128,2,128]{2,1,0:T(2,128)S(1)}, u32[]{:S(2)}) copy-start(f32[128,2,128]{2,1,0:T(2,128)S(1)} %all-to-all-done.1.terms) | copy-start | bytes 393220
  119.8 3.4 %copy-start.8 = (bf16[24,16,128]{2,1,0:T(8,128)(2,1)}, bf16[24,16,128]{2,1,0:T(8,128)(2,1)S(1)}, u32[]{:S(2)}) copy-start(bf16[24,16,128]{2,1,0:T(8,128)(2,1)S(1)} %collective-permute-done.6.rym) | copy-start | bytes 294916
  123.2 0.6 copy-start.10

commit v5 on v4

--- a/solution.py
+++ b/solution.py
@@ -542,15 +542,34 @@
     return lax.ppermute(value, axes, pairs)
 
 
-def halo(xm, xp, ym, yp):
+def join(ym, yp, from_xm, from_xp, down, up):
+    for out, plane, at in ((down, ym, face_n), (up, yp, face_n + corner_n)):
+        out[0:face_n] = plane[...]
+        out[face_n : face_n + corner_n] = from_xm[at : at + corner_n]
+        out[face_n + corner_n : side_n] = from_xp[at : at + corner_n]
+
+
+def join_term_kernel(ym, yp, from_xm, from_xp, term, down, up, passed):
+    join(ym, yp, from_xm, from_xp, down, up)
+    passed[...] = term[...]
+
+
+def halo(xm, xp, ym, yp, term=None):
     from_xm = moved(xp, 1, 0)
     from_xp = moved(xm, -1, 0)
-    mid = face_n + corner_n
-    up = jnp.concatenate([yp, from_xm[mid:], from_xp[mid:]], axis=0)
-    down = jnp.concatenate([ym, from_xm[face_n:mid], from_xp[face_n:mid]], axis=0)
+    operands = (ym, yp, from_xm, from_xp) + (() if term is None else (term,))
+    side = shape((side_n, 16, 128))
+    down, up, *passed = pl.pallas_call(
+        join if term is None else join_term_kernel,
+        out_shape=(side, side) + (() if term is None else (shape(term.shape, f32),)),
+        in_specs=[vmem] * len(operands),
+        out_specs=(vmem,) * (len(operands) - 2),
+        compiler_params=params(),
+        name="join",
+    )(*operands)
     from_ym = moved(up, 0, 1)
     from_yp = moved(down, 0, -1)
-    return from_xm, from_xp, from_ym, from_yp
+    return [from_xm, from_xp, from_ym, from_yp] + passed
 
 
 def exchange(value):
@@ -647,7 +666,7 @@
         compiler_params=params(),
         name="forward",
     )(near, lists, hidden, *near_h, cotangent, taps, elow, ehigh, ylow, yhigh, shift)
-    near_g = halo(gxm, gxp, gym, gyp)
+    *near_g, term = halo(gxm, gxp, gym, gyp, term)
     terms = exchange(term)
 
     fine_grad, back = pl.pallas_call(

time: 177 us -> 174 us (0.983)
  Pallas kernels: 62.8 us -> 66.3 us
  other arithmetic: 7.81 us -> 4.44 us
  waiting for transfers between devices: 28.9 us -> 26.5 us
    pallas_call x0 -> x2, Pallas kernels: none -> 3.49 us  [halo(): pl.pallas_call(join if term is None else join_term_kernel, out_shape=(sid...]
    concatenate x4 -> x0, other arithmetic: 3.49 us -> none  [the longest x2 1.78 us: halo(): up = jnp.concatenate([yp, from_xm[mid:], from_xp[mid:]], axis=0)]
    ppermute x8, waiting for transfers between devices: 18.6 us -> 16.2 us  [moved(): return lax.ppermute(value, axes, pairs)]
  transfers between devices with their start and end apart: 10 -> 10, of which waited for: 5 -> 5; matrix products, arithmetic and copies ran while one was open for 6% -> 5% of each run, Pallas kernels for 0% -> 0%
where the time goes in v5:
time: 174 us; the launch traced here: 173 us
  Pallas kernels  66.3 us (38%)
  starting transfers between devices  42.5 us (24%)
  waiting for transfers between devices  26.5 us (15%)
  blocking collectives  25.7 us (15%)
  local copies, waits for them, and re-layouts  6.71 us (4%)
  other arithmetic  4.44 us (3%)
    pallas_call x1, Pallas kernels, on_device(): pl.pallas_call(forward_kernel, grid=(steps // 2,), out_shape=(shape((capa...  29.6 us
    all_to_all x1, blocking collectives, exchange(): return lax.all_to_all(value, axes, split_axis=0, concat_axis=0, tiled=True)  25.7 us
    all_to_all x2, starting transfers between devices, exchange(): return lax.all_to_all(value, axes, split_axis=0, concat_axis=0, tiled=True)  22.1 us
    pallas_call x1, Pallas kernels, on_device(): pl.pallas_call(backward_kernel, grid=(steps // 2,), out_shape=(shape((cap...  21.6 us
    ppermute x8, starting transfers between devices, moved(): return lax.ppermute(value, axes, pairs)  20.4 us
    ppermute x8, waiting for transfers between devices, moved(): return lax.ppermute(value, axes, pairs)  16.2 us
    all_to_all x2, waiting for transfers between devices, exchange(): return lax.all_to_all(value, axes, split_axis=0, concat_axis=0, tiled=True)  10.3 us
    pallas_call x1, Pallas kernels, on_device(): pl.pallas_call(hidden_kernel, grid=(capacity // 16,), out_shape=(shape((c...  5.2 us
  transfers between devices with their start and end apart: 10, of which 5 were waited for; matrix products, arithmetic and copies ran while one was open for 5% of the time, Pallas kernels for 0%

profile of v5, /device:TPU:1, one launch (start us, length us, event | category | flops | bytes accessed | tf_op | source)
XLA Modules:
  0.0 173.2 jit_solution(744714876045267990)
XLA Ops:
  0.7 2.6 %octants.1 = bf16[128,16,128]{2,1,0:T(8,128)(2,1)} custom-call(s32[128]{0:T(128)} %bitcast.27, bf16[8,32,512]{2,1,0:T(8,128)(2,1)} %coarse.2, bf16[512,512]{1,0:T(8,128)(2,1)} %constant.74.clone.perm), custom_call_target="tpu_custom_call" | custom-call | tf_op jit(solution)/shard_map/octants/pallas_call | solution.py:598
  3.2 11.5 %all-to-all-start = ((bf16[128,16,128]{2,1,0:T(8,128)(2,1)}), bf16[128,16,128]{2,1,0:T(8,128)(2,1)S(1)}, u32[]{:S(2)}, u32[]{:S(2)}) async-start(bf16[128,16,128]{2,1,0:T(8,128)(2,1)} %octants.1), calls=%async_computation | async-start | bytes 1048576 | tf_op jit(solution)/shard_map/all_to_all | solution.py:576
  15.6 1.0 select_reduce_fusion
  18.3 10.3 %all-to-all-done.incoming = bf16[128,16,128]{2,1,0:T(8,128)(2,1)S(1)} async-done(((bf16[128,16,128]{2,1,0:T(8,128)(2,1)}), bf16[128,16,128]{2,1,0:T(8,128)(2,1)S(1)}, u32[]{:S(2)}, u32[]{:S(2)}) %all-to-all-start) | async-done | bytes 524320 | tf_op jit(solution)/shard_map/all_to_all | solution.py:576
  28.6 0.8 copy-done
  29.4 5.2 %hidden.1 = (bf16[64,32,512]{2,1,0:T(8,128)(2,1)}, bf16[24,16,128]{2,1,0:T(8,128)(2,1)}, bf16[24,16,128]{2,1,0:T(8,128)(2,1)}, bf16[16,16,128]{2,1,0:T(8,128)(2,1)}, bf16[16,16,128]{2,1,0:T(8,128)(2,1)}) custom-call(s32[64]{0:T(128)} %child.1, s32[64]{0:T(128)} %fusion.17.alive, s32[80]{0:T(128)} %concatenate.3.lists, bf16[128,16,128]{2,1,0:T(8,128)(2,1)} %copy-done, ...), custom_call_target="tpu_custom_call" | custom-call | tf_op jit(solution)/shard_map/hidden/pallas_call | solution.py:618
  34.6 1.3 collective-permute-start
  35.9 1.3 collective-permute-start.1
  37.3 0.7 reshape.37.near
  38.2 0.9 reshape.39.taps
  39.0 3.0 %collective-permute-done.1.from_xp.rxp = bf16[24,16,128]{2,1,0:T(8,128)(2,1)S(1)} collective-permute-done((bf16[24,16,128]{2,1,0:T(8,128)(2,1)}, bf16[24,16,128]{2,1,0:T(8,128)(2,1)S(1)}, u32[]{:S(2)}, u32[]{:S(2)}) %collective-permute-start.1) | collective-permute-done | bytes 98336 | tf_op jit(solution)/shard_map/ppermute | solution.py:542
  42.1 0.6 copy-done.6
  42.7 1.7 join.2
  44.4 4.4 %collective-permute-start.2 = (bf16[24,16,128]{2,1,0:T(8,128)(2,1)}, bf16[24,16,128]{2,1,0:T(8,128)(2,1)S(1)}, u32[]{:S(2)}, u32[]{:S(2)}) collective-permute-start(bf16[24,16,128]{2,1,0:T(8,128)(2,1)} %get-tuple-element.30), channel_id=1, source_target_pairs={{0,1},{1,2},{2,3},{3,4},{4,5},{5,6},{6,7},{7,8},{8,9},{9,10},{10,1... | collective-permute-start | bytes 294920 | tf_op jit(solution)/shard_map/ppermute | solution.py:542
  48.8 1.9 %collective-permute-start.3 = (bf16[24,16,128]{2,1,0:T(8,128)(2,1)}, bf16[24,16,128]{2,1,0:T(8,128)(2,1)S(1)}, u32[]{:S(2)}, u32[]{:S(2)}) collective-permute-start(bf16[24,16,128]{2,1,0:T(8,128)(2,1)} %get-tuple-element.31), channel_id=1, source_target_pairs={{1,0},{2,1},{3,2},{4,3},{5,4},{6,5},{7,6},{8,7},{9,8},{10,9},{11,1... | collective-permute-start | bytes 294920 | tf_op jit(solution)/shard_map/ppermute | solution.py:542
  50.8 5.6 %collective-permute-done.3.ryp = bf16[24,16,128]{2,1,0:T(8,128)(2,1)S(1)} collective-permute-done((bf16[24,16,128]{2,1,0:T(8,128)(2,1)}, bf16[24,16,128]{2,1,0:T(8,128)(2,1)S(1)}, u32[]{:S(2)}, u32[]{:S(2)}) %collective-permute-start.3) | collective-permute-done | bytes 98336 | tf_op jit(solution)/shard_map/ppermute | solution.py:542
  56.4 0.6 copy-done.11
  57.1 29.6 %forward.1 = (bf16[64,32,512]{2,1,0:T(8,128)(2,1)}, bf16[64,32,512]{2,1,0:T(8,128)(2,1)}, f32[128,2,128]{2,1,0:T(2,128)}, bf16[24,16,128]{2,1,0:T(8,128)(2,1)}, ...) custom-call(s32[1728]{0:T(1024)} %reshape.37.near, s32[80]{0:T(128)} %concatenate.3.lists, ...), custom_call_target="tpu_custom_call" | custom-call | tf_op jit(solution)/shard_map/forward/pallas_call | solution.py:646
  86.7 3.0 %collective-permute-start.4 = (bf16[24,16,128]{2,1,0:T(8,128)(2,1)}, bf16[24,16,128]{2,1,0:T(8,128)(2,1)S(1)}, u32[]{:S(2)}, u32[]{:S(2)}) collective-permute-start(bf16[24,16,128]{2,1,0:T(8,128)(2,1)} %get-tuple-element.34), channel_id=1, source_target_pairs={{0,16},{1,17},{2,18},{3,19},{4,20},{5,21},{6,22},{7,23},{8,24},{9,... | collective-permute-start | bytes 294920 | tf_op jit(solution)/shard_map/ppermute | solution.py:542
  89.7 1.3 collective-permute-start.5
  91.0 0.7 select_reduce_fusion.2
  91.7 4.0 %collective-permute-done.5.from_xp.rxp = bf16[24,16,128]{2,1,0:T(8,128)(2,1)S(1)} collective-permute-done((bf16[24,16,128]{2,1,0:T(8,128)(2,1)}, bf16[24,16,128]{2,1,0:T(8,128)(2,1)S(1)}, u32[]{:S(2)}, u32[]{:S(2)}) %collective-permute-start.5) | collective-permute-done | bytes 98336 | tf_op jit(solution)/shard_map/ppermute | solution.py:542
  96.3 1.8 %join.3 = (bf16[24,16,128]{2,1,0:T(8,128)(2,1)}, bf16[24,16,128]{2,1,0:T(8,128)(2,1)}, f32[128,2,128]{2,1,0:T(2,128)}) custom-call(bf16[16,16,128]{2,1,0:T(8,128)(2,1)} %get-tuple-element.36.ym, bf16[16,16,128]{2,1,0:T(8,128)(2,1)} %get-tuple-element.37.yp, bf16[24,16,128]{2,1,0:T(8,128)(2,1)} %copy-done.3, bf16[24,16,128]{2,1,0:T(8,128)(2,1)} %copy-done.4, ...), custom_call_target="tpu_custom_call" | custom-call | tf_op jit(solution)/shard_map/join/pallas_call | solution.py:562
  98.1 10.6 %all-to-all-start.1 = ((f32[128,2,128]{2,1,0:T(2,128)}), f32[128,2,128]{2,1,0:T(2,128)S(1)}, u32[]{:S(2)}, u32[]{:S(2)}) async-start(f32[128,2,128]{2,1,0:T(2,128)} %get-tuple-element.41), calls=%async_computation.1 | async-start | bytes 262144 | tf_op jit(solution)/shard_map/all_to_all | solution.py:576
  108.7 5.0 %collective-permute-start.6 = (bf16[24,16,128]{2,1,0:T(8,128)(2,1)}, bf16[24,16,128]{2,1,0:T(8,128)(2,1)S(1)}, u32[]{:S(2)}, u32[]{:S(2)}) collective-permute-start(bf16[24,16,128]{2,1,0:T(8,128)(2,1)} %get-tuple-element.39), channel_id=1, source_target_pairs={{0,1},{1,2},{2,3},{3,4},{4,5},{5,6},{6,7},{7,8},{8,9},{9,10},{10,1... | collective-permute-start | bytes 294920 | tf_op jit(solution)/shard_map/ppermute | solution.py:542
  113.8 2.1 %collective-permute-start.7 = (bf16[24,16,128]{2,1,0:T(8,128)(2,1)}, bf16[24,16,128]{2,1,0:T(8,128)(2,1)S(1)}, u32[]{:S(2)}, u32[]{:S(2)}) collective-permute-start(bf16[24,16,128]{2,1,0:T(8,128)(2,1)} %get-tuple-element.40), channel_id=1, source_target_pairs={{1,0},{2,1},{3,2},{4,3},{5,4},{6,5},{7,6},{8,7},{9,8},{10,9},{11,1... | collective-permute-start | bytes 294920 | tf_op jit(solution)/shard_map/ppermute | solution.py:542
  115.9 1.2 compare_select_fusion.1.child
  117.1 0.7 copy.33.taps
  117.8 3.6 %collective-permute-done.7.ryp = bf16[24,16,128]{2,1,0:T(8,128)(2,1)S(1)} collective-permute-done((bf16[24,16,128]{2,1,0:T(8,128)(2,1)}, bf16[24,16,128]{2,1,0:T(8,128)(2,1)S(1)}, u32[]{:S(2)}, u32[]{:S(2)}) %collective-permute-start.7) | collective-permute-done | bytes 98336 | tf_op jit(solution)/shard_map/ppermute | solution.py:542
  122.1 21.6 %backward.1 = (bf16[64,32,512]{2,1,0:T(8,128)(2,1)}, bf16[128,24,128]{2,1,0:T(8,128)(2,1)}) custom-call(s32[1728]{0:T(1024)} %reshape.37.near, s32[64]{0:T(128)} %compare_select_fusion.1.child, bf16[64,32,512]{2,1,0:T(8,128)(2,1)} %get-tuple-element.33.grad, bf16[24,16,128]{2,1,0:T(8,128)(2,1)} %copy-done.3, bf16[24,16,128]{2,1,0:T(8,128)(2,1)} %copy-done.4, ...), custom_call_target="tpu_custom_call" | custom-call | tf_op jit(solution)/shard_map/backward/pallas_call | solution.py:672
  143.7 25.7 %all_to_all.15.returned = bf16[128,24,128]{2,1,0:T(8,128)(2,1)} all-to-all(bf16[128,24,128]{2,1,0:T(8,128)(2,1)} %get-tuple-element.43), channel_id=1, replica_groups=mesh['gx'=8,'gy'=16] {'gx','gy'}, dimensions={0} | all-to-all | bytes 1572864 | tf_op jit(solution)/shard_map/all_to_all | solution.py:576
  169.5 3.7 %coarse.3 = (bf16[8,32,512]{2,1,0:T(8,128)(2,1)}, f32[27,32,32]{2,1,0:T(8,128)}) custom-call(s32[128]{0:T(128)} %bitcast.28, bf16[128,24,128]{2,1,0:T(8,128)(2,1)} %all_to_all.15.returned, bf16[512,512]{1,0:T(8,128)(2,1)} %constant.75.clone.perm), custom_call_target="tpu_custom_call" | custom-call | tf_op jit(solution)/shard_map/coarse/pallas_call | solution.py:687
  (47 shorter events, 4.1 us)
Async XLA Ops:
  0.6 14.8 %copy-start.12 = (s32[9,64]{1,0:T(8,128)S(1)}, s32[9,64]{1,0:T(8,128)}, u32[]{:S(2)}) copy-start(s32[9,64]{1,0:T(8,128)} %constant.89) | copy-start | bytes 6916
  0.6 14.1 %copy-start.7 = (s32[64,27]{0,1:T(8,128)S(1)}, s32[64,27]{0,1:T(8,128)}, u32[]{:S(2)}) copy-start(s32[64,27]{0,1:T(8,128)} %param.21) | copy-start | bytes 20740
  3.2 25.4 %all-to-all-start = ((bf16[128,16,128]{2,1,0:T(8,128)(2,1)}), bf16[128,16,128]{2,1,0:T(8,128)(2,1)S(1)}, u32[]{:S(2)}, u32[]{:S(2)}) async-start(bf16[128,16,128]{2,1,0:T(8,128)(2,1)} %octants.1), calls=%async_computation | async-start | bytes 1048576 | tf_op jit(solution)/shard_map/all_to_all | solution.py:576
  14.8 23.3 %copy-start.1 = (bf16[27,32,32]{2,1,0:T(8,128)(2,1)S(1)}, bf16[27,32,32]{2,1,0:T(8,128)(2,1)}, u32[]{:S(2)}) copy-start(bf16[27,32,32]{2,1,0:T(8,128)(2,1)} %param.19) | copy-start | bytes 165892
  18.3 32.4 %copy-start.13 = (s32[64]{0:T(128)S(1)}, s32[64]{0:T(128)}, u32[]{:S(2)}) copy-start(s32[64]{0:T(128)} %child.1) | copy-start | bytes 772
  28.6 0.8 copy-start
  34.6 4.4 %collective-permute-start = (bf16[24,16,128]{2,1,0:T(8,128)(2,1)}, bf16[24,16,128]{2,1,0:T(8,128)(2,1)S(1)}, u32[]{:S(2)}, u32[]{:S(2)}) collective-permute-start(bf16[24,16,128]{2,1,0:T(8,128)(2,1)} %get-tuple-element.26), channel_id=1, source_target_pairs={{0,16},{1,17},{2,18},{3,19},{4,20},{5,21},{6,22},{7,23},{8,24},{9,... | collective-permute-start | bytes 294920 | tf_op jit(solution)/shard_map/ppermute | solution.py:542
  35.9 6.1 %collective-permute-start.1 = (bf16[24,16,128]{2,1,0:T(8,128)(2,1)}, bf16[24,16,128]{2,1,0:T(8,128)(2,1)S(1)}, u32[]{:S(2)}, u32[]{:S(2)}) collective-permute-start(bf16[24,16,128]{2,1,0:T(8,128)(2,1)} %get-tuple-element.27), channel_id=1, source_target_pairs={{16,0},{17,1},{18,2},{19,3},{20,4},{21,5},{22,6},{23,7},{24,8},{25... | collective-permute-start | bytes 294920 | tf_op jit(solution)/shard_map/ppermute | solution.py:542
  39.0 3.1 %copy-start.5 = (bf16[24,16,128]{2,1,0:T(8,128)(2,1)}, bf16[24,16,128]{2,1,0:T(8,128)(2,1)S(1)}, u32[]{:S(2)}) copy-start(bf16[24,16,128]{2,1,0:T(8,128)(2,1)S(1)} %collective-permute-done.from_xm.rxm) | copy-start | bytes 294916
  42.1 0.6 copy-start.6
  44.4 6.4 %collective-permute-start.2 = (bf16[24,16,128]{2,1,0:T(8,128)(2,1)}, bf16[24,16,128]{2,1,0:T(8,128)(2,1)S(1)}, u32[]{:S(2)}, u32[]{:S(2)}) collective-permute-start(bf16[24,16,128]{2,1,0:T(8,128)(2,1)} %get-tuple-element.30), channel_id=1, source_target_pairs={{0,1},{1,2},{2,3},{3,4},{4,5},{5,6},{6,7},{7,8},{8,9},{9,10},{10,1... | collective-permute-start | bytes 294920 | tf_op jit(solution)/shard_map/ppermute | solution.py:542
  48.8 7.7 %collective-permute-start.3 = (bf16[24,16,128]{2,1,0:T(8,128)(2,1)}, bf16[24,16,128]{2,1,0:T(8,128)(2,1)S(1)}, u32[]{:S(2)}, u32[]{:S(2)}) collective-permute-start(bf16[24,16,128]{2,1,0:T(8,128)(2,1)} %get-tuple-element.31), channel_id=1, source_target_pairs={{1,0},{2,1},{3,2},{4,3},{5,4},{6,5},{7,6},{8,7},{9,8},{10,9},{11,1... | collective-permute-start | bytes 294920 | tf_op jit(solution)/shard_map/ppermute | solution.py:542
  50.8 5.6 %copy-start.10 = (bf16[24,16,128]{2,1,0:T(8,128)(2,1)}, bf16[24,16,128]{2,1,0:T(8,128)(2,1)S(1)}, u32[]{:S(2)}) copy-start(bf16[24,16,128]{2,1,0:T(8,128)(2,1)S(1)} %collective-permute-done.2.rym) | copy-start | bytes 294916
  56.4 0.6 copy-start.11
  86.7 5.0 %collective-permute-start.4 = (bf16[24,16,128]{2,1,0:T(8,128)(2,1)}, bf16[24,16,128]{2,1,0:T(8,128)(2,1)S(1)}, u32[]{:S(2)}, u32[]{:S(2)}) collective-permute-start(bf16[24,16,128]{2,1,0:T(8,128)(2,1)} %get-tuple-element.34), channel_id=1, source_target_pairs={{0,16},{1,17},{2,18},{3,19},{4,20},{5,21},{6,22},{7,23},{8,24},{9,... | collective-permute-start | bytes 294920 | tf_op jit(solution)/shard_map/ppermute | solution.py:542
  89.7 6.0 %collective-permute-start.5 = (bf16[24,16,128]{2,1,0:T(8,128)(2,1)}, bf16[24,16,128]{2,1,0:T(8,128)(2,1)S(1)}, u32[]{:S(2)}, u32[]{:S(2)}) collective-permute-start(bf16[24,16,128]{2,1,0:T(8,128)(2,1)} %get-tuple-element.35), channel_id=1, source_target_pairs={{16,0},{17,1},{18,2},{19,3},{20,4},{21,5},{22,6},{23,7},{24,8},{25... | collective-permute-start | bytes 294920 | tf_op jit(solution)/shard_map/ppermute | solution.py:542
  91.7 4.0 %copy-start.3 = (bf16[24,16,128]{2,1,0:T(8,128)(2,1)}, bf16[24,16,128]{2,1,0:T(8,128)(2,1)S(1)}, u32[]{:S(2)}) copy-start(bf16[24,16,128]{2,1,0:T(8,128)(2,1)S(1)} %collective-permute-done.4.from_xm.rxm) | copy-start | bytes 294916
  95.7 0.6 copy-start.4
  98.1 23.3 %all-to-all-start.1 = ((f32[128,2,128]{2,1,0:T(2,128)}), f32[128,2,128]{2,1,0:T(2,128)S(1)}, u32[]{:S(2)}, u32[]{:S(2)}) async-start(f32[128,2,128]{2,1,0:T(2,128)} %get-tuple-element.41), calls=%async_computation.1 | async-start | bytes 262144 | tf_op jit(solution)/shard_map/all_to_all | solution.py:576
  108.7 9.1 %collective-permute-start.6 = (bf16[24,16,128]{2,1,0:T(8,128)(2,1)}, bf16[24,16,128]{2,1,0:T(8,128)(2,1)S(1)}, u32[]{:S(2)}, u32[]{:S(2)}) collective-permute-start(bf16[24,16,128]{2,1,0:T(8,128)(2,1)} %get-tuple-element.39), channel_id=1, source_target_pairs={{0,1},{1,2},{2,3},{3,4},{4,5},{5,6},{6,7},{7,8},{8,9},{9,10},{10,1... | collective-permute-start | bytes 294920 | tf_op jit(solution)/shard_map/ppermute | solution.py:542
  113.8 7.7 %collective-permute-start.7 = (bf16[24,16,128]{2,1,0:T(8,128)(2,1)}, bf16[24,16,128]{2,1,0:T(8,128)(2,1)S(1)}, u32[]{:S(2)}, u32[]{:S(2)}) collective-permute-start(bf16[24,16,128]{2,1,0:T(8,128)(2,1)} %get-tuple-element.40), channel_id=1, source_target_pairs={{1,0},{2,1},{3,2},{4,3},{5,4},{6,5},{7,6},{8,7},{9,8},{10,9},{11,1... | collective-permute-start | bytes 294920 | tf_op jit(solution)/shard_map/ppermute | solution.py:542
  117.8 3.6 %copy-start.8 = (bf16[24,16,128]{2,1,0:T(8,128)(2,1)}, bf16[24,16,128]{2,1,0:T(8,128)(2,1)S(1)}, u32[]{:S(2)}) copy-start(bf16[24,16,128]{2,1,0:T(8,128)(2,1)S(1)} %collective-permute-done.6.rym) | copy-start | bytes 294916
  121.4 0.6 copy-start.9
  121.4 0.7 copy-start.2

commit v6 on v5

--- a/solution.py
+++ b/solution.py
@@ -549,26 +549,36 @@
         out[face_n + corner_n : side_n] = from_xp[at : at + corner_n]
 
 
-def join_term_kernel(ym, yp, from_xm, from_xp, term, down, up, passed):
-    join(ym, yp, from_xm, from_xp, down, up)
+def hold_kernel(term, after, passed):
     passed[...] = term[...]
 
 
 def halo(xm, xp, ym, yp, term=None):
     from_xm = moved(xp, 1, 0)
     from_xp = moved(xm, -1, 0)
-    operands = (ym, yp, from_xm, from_xp) + (() if term is None else (term,))
     side = shape((side_n, 16, 128))
-    down, up, *passed = pl.pallas_call(
-        join if term is None else join_term_kernel,
-        out_shape=(side, side) + (() if term is None else (shape(term.shape, f32),)),
-        in_specs=[vmem] * len(operands),
-        out_specs=(vmem,) * (len(operands) - 2),
+    down, up = pl.pallas_call(
+        join,
+        out_shape=(side, side),
+        in_specs=[vmem] * 4,
+        out_specs=(vmem, vmem),
         compiler_params=params(),
         name="join",
-    )(*operands)
+    )(ym, yp, from_xm, from_xp)
     from_ym = moved(up, 0, 1)
     from_yp = moved(down, 0, -1)
+    passed = []
+    if term is not None:
+        passed = [
+            pl.pallas_call(
+                hold_kernel,
+                out_shape=shape(term.shape, f32),
+                in_specs=[vmem, pl.BlockSpec(memory_space=pl.ANY)],
+                out_specs=vmem,
+                compiler_params=params(),
+                name="hold",
+            )(term, down)
+        ]
     return [from_xm, from_xp, from_ym, from_yp] + passed
 
 

time: 174 us -> 174 us (level)
    ppermute x8, waiting for transfers between devices: 16.2 us -> 12.6 us  [moved(): return lax.ppermute(value, axes, pairs)]
    all_to_all x2, waiting for transfers between devices: 10.3 us -> 13.1 us  [exchange(): return lax.all_to_all(value, axes, split_axis=0, concat_axis=0, tiled=True)]
    pallas_call x2 -> x3, Pallas kernels: 3.49 us -> 4.94 us  [the longest x2 3.37 us: halo(): pl.pallas_call(join, out_shape=(side, side), in_specs=[vmem] * 4, out_spe...]
  transfers between devices with their start and end apart: 10 -> 10, of which waited for: 5 -> 5; matrix products, arithmetic and copies ran while one was open for 5% -> 5% of each run, Pallas kernels for 0% -> 1%
where the time goes in v6:
time: 174 us
  Pallas kernels  67.7 us (39%)
  starting transfers between devices  43.8 us (25%)
  waiting for transfers between devices  25.7 us (15%)
  blocking collectives  24.2 us (14%)
  local copies, waits for them, and re-layouts  6.69 us (4%)
  other arithmetic  4.44 us (3%)
    pallas_call x1, Pallas kernels, on_device(): pl.pallas_call(forward_kernel, grid=(steps // 2,), out_shape=(shape((capa...  29.6 us
    all_to_all x1, blocking collectives, exchange(): return lax.all_to_all(value, axes, split_axis=0, concat_axis=0, tiled=True)  24.2 us
    all_to_all x2, starting transfers between devices, exchange(): return lax.all_to_all(value, axes, split_axis=0, concat_axis=0, tiled=True)  23.5 us
    pallas_call x1, Pallas kernels, on_device(): pl.pallas_call(backward_kernel, grid=(steps // 2,), out_shape=(shape((cap...  21.6 us
    ppermute x8, starting transfers between devices, moved(): return lax.ppermute(value, axes, pairs)  20.4 us
    all_to_all x2, waiting for transfers between devices, exchange(): return lax.all_to_all(value, axes, split_axis=0, concat_axis=0, tiled=True)  13.1 us
    ppermute x8, waiting for transfers between devices, moved(): return lax.ppermute(value, axes, pairs)  12.6 us
    pallas_call x1, Pallas kernels, on_device(): pl.pallas_call(hidden_kernel, grid=(capacity // 16,), out_shape=(shape((c...  5.2 us
  transfers between devices with their start and end apart: 10, of which 5 were waited for; matrix products, arithmetic and copies ran while one was open for 5% of the time, Pallas kernels for 1%

profile of v6, /device:TPU:1, one launch (start us, length us, event | category | flops | bytes accessed | tf_op | source)
XLA Modules:
  0.0 173.6 jit_solution(5044012658796881908)
XLA Ops:
  0.7 2.6 %octants.1 = bf16[128,16,128]{2,1,0:T(8,128)(2,1)} custom-call(s32[128]{0:T(128)} %bitcast.27, bf16[8,32,512]{2,1,0:T(8,128)(2,1)} %coarse.2, bf16[512,512]{1,0:T(8,128)(2,1)} %constant.74.clone.perm), custom_call_target="tpu_custom_call" | custom-call | tf_op jit(solution)/shard_map/octants/pallas_call | solution.py:608
  3.2 11.5 %all-to-all-start = ((bf16[128,16,128]{2,1,0:T(8,128)(2,1)}), bf16[128,16,128]{2,1,0:T(8,128)(2,1)S(1)}, u32[]{:S(2)}, u32[]{:S(2)}) async-start(bf16[128,16,128]{2,1,0:T(8,128)(2,1)} %octants.1), calls=%async_computation | async-start | bytes 1048576 | tf_op jit(solution)/shard_map/all_to_all | solution.py:586
  15.6 1.0 select_reduce_fusion
  18.3 10.3 %all-to-all-done.incoming = bf16[128,16,128]{2,1,0:T(8,128)(2,1)S(1)} async-done(((bf16[128,16,128]{2,1,0:T(8,128)(2,1)}), bf16[128,16,128]{2,1,0:T(8,128)(2,1)S(1)}, u32[]{:S(2)}, u32[]{:S(2)}) %all-to-all-start) | async-done | bytes 524320 | tf_op jit(solution)/shard_map/all_to_all | solution.py:586
  28.6 0.8 copy-done
  29.4 5.2 %hidden.1 = (bf16[64,32,512]{2,1,0:T(8,128)(2,1)}, bf16[24,16,128]{2,1,0:T(8,128)(2,1)}, bf16[24,16,128]{2,1,0:T(8,128)(2,1)}, bf16[16,16,128]{2,1,0:T(8,128)(2,1)}, bf16[16,16,128]{2,1,0:T(8,128)(2,1)}) custom-call(s32[64]{0:T(128)} %child.1, s32[64]{0:T(128)} %fusion.17.alive, s32[80]{0:T(128)} %concatenate.3.lists, bf16[128,16,128]{2,1,0:T(8,128)(2,1)} %copy-done, ...), custom_call_target="tpu_custom_call" | custom-call | tf_op jit(solution)/shard_map/hidden/pallas_call | solution.py:628
  34.6 1.3 collective-permute-start
  35.9 1.3 collective-permute-start.1
  37.3 0.7 reshape.37.near
  38.2 0.9 reshape.39.taps
  39.0 3.0 %collective-permute-done.1.from_xp.rxp = bf16[24,16,128]{2,1,0:T(8,128)(2,1)S(1)} collective-permute-done((bf16[24,16,128]{2,1,0:T(8,128)(2,1)}, bf16[24,16,128]{2,1,0:T(8,128)(2,1)S(1)}, u32[]{:S(2)}, u32[]{:S(2)}) %collective-permute-start.1) | collective-permute-done | bytes 98336 | tf_op jit(solution)/shard_map/ppermute | solution.py:542
  42.7 1.7 join.2
  44.4 4.4 %collective-permute-start.2 = (bf16[24,16,128]{2,1,0:T(8,128)(2,1)}, bf16[24,16,128]{2,1,0:T(8,128)(2,1)S(1)}, u32[]{:S(2)}, u32[]{:S(2)}) collective-permute-start(bf16[24,16,128]{2,1,0:T(8,128)(2,1)} %get-tuple-element.29), channel_id=1, source_target_pairs={{0,1},{1,2},{2,3},{3,4},{4,5},{5,6},{6,7},{7,8},{8,9},{9,10},{10,1... | collective-permute-start | bytes 294920 | tf_op jit(solution)/shard_map/ppermute | solution.py:542
  48.8 1.9 %collective-permute-start.3 = (bf16[24,16,128]{2,1,0:T(8,128)(2,1)}, bf16[24,16,128]{2,1,0:T(8,128)(2,1)S(1)}, u32[]{:S(2)}, u32[]{:S(2)}) collective-permute-start(bf16[24,16,128]{2,1,0:T(8,128)(2,1)} %get-tuple-element.30), channel_id=1, source_target_pairs={{1,0},{2,1},{3,2},{4,3},{5,4},{6,5},{7,6},{8,7},{9,8},{10,9},{11,1... | collective-permute-start | bytes 294920 | tf_op jit(solution)/shard_map/ppermute | solution.py:542
  50.8 5.6 %collective-permute-done.3.ryp = bf16[24,16,128]{2,1,0:T(8,128)(2,1)S(1)} collective-permute-done((bf16[24,16,128]{2,1,0:T(8,128)(2,1)}, bf16[24,16,128]{2,1,0:T(8,128)(2,1)S(1)}, u32[]{:S(2)}, u32[]{:S(2)}) %collective-permute-start.3) | collective-permute-done | bytes 98336 | tf_op jit(solution)/shard_map/ppermute | solution.py:542
  57.1 29.6 %forward.1 = (bf16[64,32,512]{2,1,0:T(8,128)(2,1)}, bf16[64,32,512]{2,1,0:T(8,128)(2,1)}, f32[128,2,128]{2,1,0:T(2,128)}, bf16[24,16,128]{2,1,0:T(8,128)(2,1)}, ...) custom-call(s32[1728]{0:T(1024)} %reshape.37.near, s32[80]{0:T(128)} %concatenate.3.lists, ...), custom_call_target="tpu_custom_call" | custom-call | tf_op jit(solution)/shard_map/forward/pallas_call | solution.py:656
  86.7 3.0 %collective-permute-start.4 = (bf16[24,16,128]{2,1,0:T(8,128)(2,1)}, bf16[24,16,128]{2,1,0:T(8,128)(2,1)S(1)}, u32[]{:S(2)}, u32[]{:S(2)}) collective-permute-start(bf16[24,16,128]{2,1,0:T(8,128)(2,1)} %get-tuple-element.33), channel_id=1, source_target_pairs={{0,16},{1,17},{2,18},{3,19},{4,20},{5,21},{6,22},{7,23},{8,24},{9,... | collective-permute-start | bytes 294920 | tf_op jit(solution)/shard_map/ppermute | solution.py:542
  89.7 1.3 collective-permute-start.5
  91.0 0.7 select_reduce_fusion.2
  91.7 4.0 %collective-permute-done.5.from_xp.rxp = bf16[24,16,128]{2,1,0:T(8,128)(2,1)S(1)} collective-permute-done((bf16[24,16,128]{2,1,0:T(8,128)(2,1)}, bf16[24,16,128]{2,1,0:T(8,128)(2,1)S(1)}, u32[]{:S(2)}, u32[]{:S(2)}) %collective-permute-start.5) | collective-permute-done | bytes 98336 | tf_op jit(solution)/shard_map/ppermute | solution.py:542
  96.3 1.7 join.3
  98.0 1.9 %collective-permute-start.7 = (bf16[24,16,128]{2,1,0:T(8,128)(2,1)}, bf16[24,16,128]{2,1,0:T(8,128)(2,1)S(1)}, u32[]{:S(2)}, u32[]{:S(2)}) collective-permute-start(bf16[24,16,128]{2,1,0:T(8,128)(2,1)} %get-tuple-element.38.after), channel_id=1, source_target_pairs={{1,0},{2,1},{3,2},{4,3},{5,4},{6,5},{7,6},{8,7},{9,8},{10,9},{11,1... | collective-permute-start | bytes 294920 | tf_op jit(solution)/shard_map/ppermute | solution.py:542
  99.9 1.6 hold.1
  101.5 12.0 %all-to-all-start.1 = ((f32[128,2,128]{2,1,0:T(2,128)}), f32[128,2,128]{2,1,0:T(2,128)S(1)}, u32[]{:S(2)}, u32[]{:S(2)}) async-start(f32[128,2,128]{2,1,0:T(2,128)} %hold.1), calls=%async_computation.1 | async-start | bytes 262144 | tf_op jit(solution)/shard_map/all_to_all | solution.py:586
  113.5 5.2 %collective-permute-start.6 = (bf16[24,16,128]{2,1,0:T(8,128)(2,1)}, bf16[24,16,128]{2,1,0:T(8,128)(2,1)S(1)}, u32[]{:S(2)}, u32[]{:S(2)}) collective-permute-start(bf16[24,16,128]{2,1,0:T(8,128)(2,1)} %get-tuple-element.37), channel_id=1, source_target_pairs={{0,1},{1,2},{2,3},{3,4},{4,5},{5,6},{6,7},{7,8},{8,9},{9,10},{10,1... | collective-permute-start | bytes 294920 | tf_op jit(solution)/shard_map/ppermute | solution.py:542
  118.7 1.2 compare_select_fusion.1.child
  119.9 0.7 copy.33.taps
  120.7 2.7 %all-to-all-done.1.terms = f32[128,2,128]{2,1,0:T(2,128)S(1)} async-done(((f32[128,2,128]{2,1,0:T(2,128)}), f32[128,2,128]{2,1,0:T(2,128)S(1)}, u32[]{:S(2)}, u32[]{:S(2)}) %all-to-all-start.1) | async-done | bytes 131104 | tf_op jit(solution)/shard_map/all_to_all | solution.py:586
  123.4 0.6 copy-done.2
  124.1 21.6 %backward.1 = (bf16[64,32,512]{2,1,0:T(8,128)(2,1)}, bf16[128,24,128]{2,1,0:T(8,128)(2,1)}) custom-call(s32[1728]{0:T(1024)} %reshape.37.near, s32[64]{0:T(128)} %compare_select_fusion.1.child, bf16[64,32,512]{2,1,0:T(8,128)(2,1)} %get-tuple-element.32.grad, bf16[24,16,128]{2,1,0:T(8,128)(2,1)} %copy-done.3, bf16[24,16,128]{2,1,0:T(8,128)(2,1)} %copy-done.4, ...), custom_call_target="tpu_custom_call" | custom-call | tf_op jit(solution)/shard_map/backward/pallas_call | solution.py:682
  145.7 24.2 %all_to_all.15.returned = bf16[128,24,128]{2,1,0:T(8,128)(2,1)} all-to-all(bf16[128,24,128]{2,1,0:T(8,128)(2,1)} %get-tuple-element.41), channel_id=1, replica_groups=mesh['gx'=8,'gy'=16] {'gx','gy'}, dimensions={0} | all-to-all | bytes 1572864 | tf_op jit(solution)/shard_map/all_to_all | solution.py:586
  169.9 3.7 %coarse.3 = (bf16[8,32,512]{2,1,0:T(8,128)(2,1)}, f32[27,32,32]{2,1,0:T(8,128)}) custom-call(s32[128]{0:T(128)} %bitcast.28, bf16[128,24,128]{2,1,0:T(8,128)(2,1)} %all_to_all.15.returned, bf16[512,512]{1,0:T(8,128)(2,1)} %constant.75.clone.perm), custom_call_target="tpu_custom_call" | custom-call | tf_op jit(solution)/shard_map/coarse/pallas_call | solution.py:697
  (48 shorter events, 4.7 us)
Async XLA Ops:
  0.6 14.8 %copy-start.12 = (s32[9,64]{1,0:T(8,128)S(1)}, s32[9,64]{1,0:T(8,128)}, u32[]{:S(2)}) copy-start(s32[9,64]{1,0:T(8,128)} %constant.89) | copy-start | bytes 6916
  0.6 14.1 %copy-start.7 = (s32[64,27]{0,1:T(8,128)S(1)}, s32[64,27]{0,1:T(8,128)}, u32[]{:S(2)}) copy-start(s32[64,27]{0,1:T(8,128)} %param.21) | copy-start | bytes 20740
  3.2 25.4 %all-to-all-start = ((bf16[128,16,128]{2,1,0:T(8,128)(2,1)}), bf16[128,16,128]{2,1,0:T(8,128)(2,1)S(1)}, u32[]{:S(2)}, u32[]{:S(2)}) async-start(bf16[128,16,128]{2,1,0:T(8,128)(2,1)} %octants.1), calls=%async_computation | async-start | bytes 1048576 | tf_op jit(solution)/shard_map/all_to_all | solution.py:586
  14.8 23.3 %copy-start.1 = (bf16[27,32,32]{2,1,0:T(8,128)(2,1)S(1)}, bf16[27,32,32]{2,1,0:T(8,128)(2,1)}, u32[]{:S(2)}) copy-start(bf16[27,32,32]{2,1,0:T(8,128)(2,1)} %param.19) | copy-start | bytes 165892
  18.3 32.4 %copy-start.13 = (s32[64]{0:T(128)S(1)}, s32[64]{0:T(128)}, u32[]{:S(2)}) copy-start(s32[64]{0:T(128)} %child.1) | copy-start | bytes 772
  28.6 0.8 copy-start
  34.6 4.4 %collective-permute-start = (bf16[24,16,128]{2,1,0:T(8,128)(2,1)}, bf16[24,16,128]{2,1,0:T(8,128)(2,1)S(1)}, u32[]{:S(2)}, u32[]{:S(2)}) collective-permute-start(bf16[24,16,128]{2,1,0:T(8,128)(2,1)} %get-tuple-element.25), channel_id=1, source_target_pairs={{0,16},{1,17},{2,18},{3,19},{4,20},{5,21},{6,22},{7,23},{8,24},{9,... | collective-permute-start | bytes 294920 | tf_op jit(solution)/shard_map/ppermute | solution.py:542
  35.9 6.1 %collective-permute-start.1 = (bf16[24,16,128]{2,1,0:T(8,128)(2,1)}, bf16[24,16,128]{2,1,0:T(8,128)(2,1)S(1)}, u32[]{:S(2)}, u32[]{:S(2)}) collective-permute-start(bf16[24,16,128]{2,1,0:T(8,128)(2,1)} %get-tuple-element.26), channel_id=1, source_target_pairs={{16,0},{17,1},{18,2},{19,3},{20,4},{21,5},{22,6},{23,7},{24,8},{25... | collective-permute-start | bytes 294920 | tf_op jit(solution)/shard_map/ppermute | solution.py:542
  39.0 3.1 %copy-start.5 = (bf16[24,16,128]{2,1,0:T(8,128)(2,1)}, bf16[24,16,128]{2,1,0:T(8,128)(2,1)S(1)}, u32[]{:S(2)}) copy-start(bf16[24,16,128]{2,1,0:T(8,128)(2,1)S(1)} %collective-permute-done.from_xm.rxm) | copy-start | bytes 294916
  42.1 0.6 copy-start.6
  44.4 6.4 %collective-permute-start.2 = (bf16[24,16,128]{2,1,0:T(8,128)(2,1)}, bf16[24,16,128]{2,1,0:T(8,128)(2,1)S(1)}, u32[]{:S(2)}, u32[]{:S(2)}) collective-permute-start(bf16[24,16,128]{2,1,0:T(8,128)(2,1)} %get-tuple-element.29), channel_id=1, source_target_pairs={{0,1},{1,2},{2,3},{3,4},{4,5},{5,6},{6,7},{7,8},{8,9},{9,10},{10,1... | collective-permute-start | bytes 294920 | tf_op jit(solution)/shard_map/ppermute | solution.py:542
  48.8 7.7 %collective-permute-start.3 = (bf16[24,16,128]{2,1,0:T(8,128)(2,1)}, bf16[24,16,128]{2,1,0:T(8,128)(2,1)S(1)}, u32[]{:S(2)}, u32[]{:S(2)}) collective-permute-start(bf16[24,16,128]{2,1,0:T(8,128)(2,1)} %get-tuple-element.30), channel_id=1, source_target_pairs={{1,0},{2,1},{3,2},{4,3},{5,4},{6,5},{7,6},{8,7},{9,8},{10,9},{11,1... | collective-permute-start | bytes 294920 | tf_op jit(solution)/shard_map/ppermute | solution.py:542
  50.8 5.6 %copy-start.10 = (bf16[24,16,128]{2,1,0:T(8,128)(2,1)}, bf16[24,16,128]{2,1,0:T(8,128)(2,1)S(1)}, u32[]{:S(2)}) copy-start(bf16[24,16,128]{2,1,0:T(8,128)(2,1)S(1)} %collective-permute-done.2.rym) | copy-start | bytes 294916
  56.4 0.6 copy-start.11
  86.7 5.0 %collective-permute-start.4 = (bf16[24,16,128]{2,1,0:T(8,128)(2,1)}, bf16[24,16,128]{2,1,0:T(8,128)(2,1)S(1)}, u32[]{:S(2)}, u32[]{:S(2)}) collective-permute-start(bf16[24,16,128]{2,1,0:T(8,128)(2,1)} %get-tuple-element.33), channel_id=1, source_target_pairs={{0,16},{1,17},{2,18},{3,19},{4,20},{5,21},{6,22},{7,23},{8,24},{9,... | collective-permute-start | bytes 294920 | tf_op jit(solution)/shard_map/ppermute | solution.py:542
  89.7 6.0 %collective-permute-start.5 = (bf16[24,16,128]{2,1,0:T(8,128)(2,1)}, bf16[24,16,128]{2,1,0:T(8,128)(2,1)S(1)}, u32[]{:S(2)}, u32[]{:S(2)}) collective-permute-start(bf16[24,16,128]{2,1,0:T(8,128)(2,1)} %get-tuple-element.34), channel_id=1, source_target_pairs={{16,0},{17,1},{18,2},{19,3},{20,4},{21,5},{22,6},{23,7},{24,8},{25... | collective-permute-start | bytes 294920 | tf_op jit(solution)/shard_map/ppermute | solution.py:542
  91.7 4.0 %copy-start.3 = (bf16[24,16,128]{2,1,0:T(8,128)(2,1)}, bf16[24,16,128]{2,1,0:T(8,128)(2,1)S(1)}, u32[]{:S(2)}) copy-start(bf16[24,16,128]{2,1,0:T(8,128)(2,1)S(1)} %collective-permute-done.4.from_xm.rxm) | copy-start | bytes 294916
  95.7 0.6 copy-start.4
  98.0 22.7 %collective-permute-start.7 = (bf16[24,16,128]{2,1,0:T(8,128)(2,1)}, bf16[24,16,128]{2,1,0:T(8,128)(2,1)S(1)}, u32[]{:S(2)}, u32[]{:S(2)}) collective-permute-start(bf16[24,16,128]{2,1,0:T(8,128)(2,1)} %get-tuple-element.38.after), channel_id=1, source_target_pairs={{1,0},{2,1},{3,2},{4,3},{5,4},{6,5},{7,6},{8,7},{9,8},{10,9},{11,1... | collective-permute-start | bytes 294920 | tf_op jit(solution)/shard_map/ppermute | solution.py:542
  101.5 21.9 %all-to-all-start.1 = ((f32[128,2,128]{2,1,0:T(2,128)}), f32[128,2,128]{2,1,0:T(2,128)S(1)}, u32[]{:S(2)}, u32[]{:S(2)}) async-start(f32[128,2,128]{2,1,0:T(2,128)} %hold.1), calls=%async_computation.1 | async-start | bytes 262144 | tf_op jit(solution)/shard_map/all_to_all | solution.py:586
  113.5 7.2 %collective-permute-start.6 = (bf16[24,16,128]{2,1,0:T(8,128)(2,1)}, bf16[24,16,128]{2,1,0:T(8,128)(2,1)S(1)}, u32[]{:S(2)}, u32[]{:S(2)}) collective-permute-start(bf16[24,16,128]{2,1,0:T(8,128)(2,1)} %get-tuple-element.37), channel_id=1, source_target_pairs={{0,1},{1,2},{2,3},{3,4},{4,5},{5,6},{6,7},{7,8},{8,9},{9,10},{10,1... | collective-permute-start | bytes 294920 | tf_op jit(solution)/shard_map/ppermute | solution.py:542
  120.7 2.8 %copy-start.9 = (bf16[24,16,128]{2,1,0:T(8,128)(2,1)}, bf16[24,16,128]{2,1,0:T(8,128)(2,1)S(1)}, u32[]{:S(2)}) copy-start(bf16[24,16,128]{2,1,0:T(8,128)(2,1)S(1)} %collective-permute-done.6.rym) | copy-start | bytes 294916
  120.7 2.8 %copy-start.8 = (bf16[24,16,128]{2,1,0:T(8,128)(2,1)}, bf16[24,16,128]{2,1,0:T(8,128)(2,1)S(1)}, u32[]{:S(2)}) copy-start(bf16[24,16,128]{2,1,0:T(8,128)(2,1)S(1)} %collective-permute-done.7.ryp) | copy-start | bytes 294916
  123.4 0.7 copy-start.2
